TPU v7x, 32 devices: a whole 2x2x4 slice. The times are simulated.
32 devices in a mesh: dp: 16 (over z, y, x), tensor: 2 (over core).
Axes of the slice: x: 2, y: 2, z: 4, core: 2. Of those that a mesh axis runs over, the one named last changes fastest.
Arguments:
- tokens_in: bfloat16 [16, 1024, 1024], P('dp', 'tensor'), may hold values from -6 to 6
- segments: int32 [16, 1024], P('dp'), may hold values from 0 to 4, as said below
- gains: bfloat16 [4, 1024], P(None, 'dp'), may hold values from 0.5 to 1.5
- taps: bfloat16 [3, 1024], P(None, 'dp'), may hold values from -3 to 3
- in_proj: bfloat16 [1024, 3, 1024], P('dp', None, 'tensor'), may hold values from -0.1875 to 0.1875
- out_proj: bfloat16 [1024, 1024], P('tensor', 'dp'), may hold values from -0.1875 to 0.1875
- gate_up_a: bfloat16 [1024, 2, 4608], P('dp', None, 'tensor'), may hold values from -0.1875 to 0.1875
- down_a: bfloat16 [4608, 1024], P('tensor', 'dp'), may hold values from -0.09375 to 0.09375
- query_w: bfloat16 [1024, 1024], P('dp', 'tensor'), may hold values from -0.1875 to 0.1875
- key_value_w: bfloat16 [1024, 2, 512], P('dp', None, 'tensor'), may hold values from -0.1875 to 0.1875
- attn_out_w: bfloat16 [1024, 1024], P('tensor', 'dp'), may hold values from -0.75 to 0.75
- gate_up_b: bfloat16 [1024, 2, 4608], P('dp', None, 'tensor'), may hold values from -0.1875 to 0.1875
- down_b: bfloat16 [4608, 1024], P('tensor', 'dp'), may hold values from -0.09375 to 0.09375
- cotangent: bfloat16 [16, 1024, 1024], P('dp', 'tensor'), may hold values from -6 to 6
Outputs:
- output: bfloat16 [16, 1024, 1024], P('dp', 'tensor')
- grad_input: float32 [16, 1024, 1024], P('dp', 'tensor')
- grad_gains: float32 [4, 1024], P(None, 'dp')
- grad_taps: float32 [3, 1024], P(None, 'dp')
- grad_in_proj: float32 [1024, 3, 1024], P('dp', None, 'tensor')
- grad_out_proj: float32 [1024, 1024], P('tensor', 'dp')
- grad_gate_up_a: float32 [1024, 2, 4608], P('dp', None, 'tensor')
- grad_down_a: float32 [4608, 1024], P('tensor', 'dp')
- grad_query: float32 [1024, 1024], P('dp', 'tensor')
- grad_key_value: float32 [1024, 2, 512], P('dp', None, 'tensor')
- grad_attn_out: float32 [1024, 1024], P('tensor', 'dp')
- grad_gate_up_b: float32 [1024, 2, 4608], P('dp', None, 'tensor')
- grad_down_b: float32 [4608, 1024], P('tensor', 'dp')
Inputs may be any that keep to these rules, and one draw needn't show every extreme that they name: `segments`: along each sequence the numbers start at 0, never fall, and rise by at most 1 from one token to the next; the last token's number is 4 (each sequence holds exactly 5 documents); the document that holds token 512 holds all tokens from 384 to 639.
All inputs are finite; a program needn't handle non-finite values.
Results may differ from a plain program's by a relative error of at most 0.03.
Values may be sent and summed in bfloat16 or wider, within the bound.
No kernel may reach another device: no remote copies, remote signals or barrier semaphores. Data moves between devices by JAX's collectives and lax.ppermute only.
A program may use at most 320 MiB of HBM per device.

v0:
```python
import math

import jax
import jax.numpy as jnp
from jax import lax
from jax.sharding import PartitionSpec as P

HD = 64


EPS = 1e-05
THETA = 1000000.0
SCALE = 0.125


def norm_rows(values_in, gain):
    return (
        values_in * lax.rsqrt(jnp.mean(values_in * values_in, axis=-1, keepdims=True) + EPS) * gain
    )


def doc_positions(segment_ids):
    length = segment_ids.shape[0]
    index = jnp.arange(length, dtype=jnp.int32)
    starts = jnp.concatenate([jnp.ones((1,), jnp.bool_), segment_ids[1:] != segment_ids[:-1]])
    first = lax.cummax(jnp.where(starts, index, 0), axis=0)
    return (index - first).astype(jnp.float32)


def rope(values_in, positions):
    half = values_in.shape[-1] // 2
    freq = jnp.exp(jnp.arange(half, dtype=jnp.float32) * (-2.0 * math.log(THETA) / (2 * half)))
    angle = positions[:, None] * freq[None, :]
    cosine = jnp.cos(angle)[:, None, :]
    sine = jnp.sin(angle)[:, None, :]
    first_half = values_in[..., :half]
    second_half = values_in[..., half:]
    return jnp.concatenate(
        [first_half * cosine - second_half * sine, second_half * cosine + first_half * sine],
        axis=-1,
    )


def conv_mix(mixed, kernel, segment_ids):
    driven = mixed[:, 0] * mixed[:, 2]
    channels = driven.shape[1]
    same_one = jnp.concatenate(
        [jnp.zeros((1,), jnp.bool_), segment_ids[1:] == segment_ids[:-1]]
    ).astype(driven.dtype)
    same_two = jnp.concatenate(
        [jnp.zeros((2,), jnp.bool_), segment_ids[2:] == segment_ids[:-2]]
    ).astype(driven.dtype)
    back_one = (
        jnp.concatenate([jnp.zeros((1, channels), driven.dtype), driven[:-1]], axis=0)
        * same_one[:, None]
    )
    back_two = (
        jnp.concatenate([jnp.zeros((2, channels), driven.dtype), driven[:-2]], axis=0)
        * same_two[:, None]
    )
    return mixed[:, 1] * (kernel[0] * driven + kernel[1] * back_one + kernel[2] * back_two)


def glu(gate_up):
    return jax.nn.silu(gate_up[:, 0]) * gate_up[:, 1]


def spread(values_in):
    return lax.all_gather(values_in, "tensor", axis=0, tiled=True)


def spread_grad(values_in):
    return lax.all_gather(values_in, "tensor", axis=0, tiled=True)


def row_product(operand, weight):

    def make_term(start, count):
        return jnp.dot(operand, weight, preferred_element_type=jnp.float32)

    return make_term


def allowed_mask(segment_ids, start, block):
    length = segment_ids.shape[0]
    row_index = start + jnp.arange(block)
    col_index = jnp.arange(length)
    row_segs = segment_ids[start : start + block]
    return (col_index[None, :] <= row_index[:, None]) & (segment_ids[None, :] == row_segs[:, None])


def attend_forward(q_block, keys, values, allowed):
    scores = SCALE * jnp.einsum("qhgd,khd->hgqk", q_block, keys, preferred_element_type=jnp.float32)
    scores = jnp.where(allowed, scores, -1e30)
    row_max = jnp.max(scores, axis=-1, keepdims=True)
    lifted = jnp.exp(scores - row_max)
    row_total = jnp.sum(lifted, axis=-1, keepdims=True)
    probs = (lifted / row_total).astype(jnp.bfloat16)
    attended = jnp.einsum("hgqk,khd->qhgd", probs, values, preferred_element_type=jnp.float32)
    return (attended, row_max + jnp.log(row_total))


def attend_backward(q_block, keys, values, allowed, log_total, grad_block):
    scores = SCALE * jnp.einsum("qhgd,khd->hgqk", q_block, keys, preferred_element_type=jnp.float32)
    probs = jnp.exp(jnp.where(allowed, scores, -1e30) - log_total)
    grad_values = jnp.einsum(
        "hgqk,qhgd->khd", probs.astype(jnp.bfloat16), grad_block, preferred_element_type=jnp.float32
    )
    grad_probs = jnp.einsum(
        "qhgd,khd->hgqk", grad_block, values, preferred_element_type=jnp.float32
    )
    grad_scores = (
        probs * (grad_probs - jnp.sum(probs * grad_probs, axis=-1, keepdims=True))
    ).astype(jnp.bfloat16)
    grad_query = SCALE * jnp.einsum(
        "hgqk,khd->qhgd", grad_scores, keys, preferred_element_type=jnp.float32
    )
    grad_keys = SCALE * jnp.einsum(
        "hgqk,qhgd->khd", grad_scores, q_block, preferred_element_type=jnp.float32
    )
    return (grad_query, grad_keys, grad_values)


def per_device(
    tokens_in,
    segments,
    gains,
    taps,
    in_proj,
    out_proj,
    gate_up_a,
    down_a,
    query_w,
    key_value_w,
    attn_out_w,
    gate_up_b,
    down_b,
    cotangent,
):
    row_count = tokens_in.shape[1]
    segment_ids = segments[0]
    length = segment_ids.shape[0]
    tensor_rank = lax.axis_index("tensor")
    positions = doc_positions(segment_ids)

    def collect(make_term):
        return lax.psum_scatter(
            make_term(jnp.int32(0), lax.axis_size("tensor") * row_count).astype(jnp.bfloat16),
            "tensor",
            scatter_dimension=0,
            tiled=True,
        ).astype(jnp.float32)

    def collect_grad(make_term):
        return lax.psum_scatter(
            make_term(jnp.int32(0), lax.axis_size("tensor") * row_count).astype(jnp.bfloat16),
            "tensor",
            scatter_dimension=0,
            tiled=True,
        ).astype(jnp.float32)

    def feed_forward(hidden, gain, w_gate_up, w_down):
        normed_full = spread(norm_rows(hidden, gain).astype(jnp.bfloat16))
        gate_up = jnp.einsum(
            "sd,dkf->skf", normed_full, w_gate_up, preferred_element_type=jnp.float32
        )
        product = glu(gate_up).astype(jnp.bfloat16)
        return (hidden + collect(row_product(product, w_down)), (normed_full, gate_up, product))

    def feed_back(grad_out, hidden, gain, w_gate_up, w_down, kept):
        normed_full, gate_up, product = kept
        grad_full = spread_grad(grad_out.astype(jnp.bfloat16))
        grad_down = jnp.einsum("sf,sd->fd", product, grad_full, preferred_element_type=jnp.float32)
        grad_product = jnp.einsum(
            "sd,fd->sf", grad_full, w_down, preferred_element_type=jnp.float32
        )
        glu_pull = jax.vjp(glu, gate_up)[1]
        grad_gate_up = glu_pull(grad_product)[0].astype(jnp.bfloat16)
        grad_w_gate_up = jnp.einsum(
            "sd,skf->dkf", normed_full, grad_gate_up, preferred_element_type=jnp.float32
        )

        def make_term(start, count):
            return jnp.einsum(
                "skf,dkf->sd", grad_gate_up, w_gate_up, preferred_element_type=jnp.float32
            )

        grad_normed = collect_grad(make_term)
        norm_pull = jax.vjp(norm_rows, hidden, gain)[1]
        grad_hidden, grad_gain = norm_pull(grad_normed)
        return (grad_out + grad_hidden, grad_gain, grad_w_gate_up, grad_down)

    gain_all, conv_all, w_in, w_out, w_gu_a, w_down_a = (
        lax.all_gather(gains, "dp", axis=1, tiled=True),
        lax.all_gather(taps, "dp", axis=1, tiled=True),
        lax.all_gather(in_proj, "dp", axis=0, tiled=True),
        lax.all_gather(out_proj, "dp", axis=1, tiled=True),
        lax.all_gather(gate_up_a, "dp", axis=0, tiled=True),
        lax.all_gather(down_a, "dp", axis=1, tiled=True),
    )
    gain_rows = gain_all.astype(jnp.float32)
    width_half = w_in.shape[2]
    conv_half = lax.dynamic_slice_in_dim(conv_all, tensor_rank * width_half, width_half, 1).astype(
        jnp.float32
    )
    hidden_zero = tokens_in[0].astype(jnp.float32)
    first_full = spread(norm_rows(hidden_zero, gain_rows[0]).astype(jnp.bfloat16))
    mixed = jnp.einsum("sd,dkc->skc", first_full, w_in, preferred_element_type=jnp.float32)
    conv_out, conv_pull = jax.vjp(
        lambda mixed_in, kernel_in: conv_mix(mixed_in, kernel_in, segment_ids), mixed, conv_half
    )
    conv_low = conv_out.astype(jnp.bfloat16)
    hidden_one = hidden_zero + collect(row_product(conv_low, w_out))
    hidden_two, kept_a = feed_forward(hidden_one, gain_rows[1], w_gu_a, w_down_a)
    w_query, w_kv, w_attn, w_gu_b, w_down_b = (
        lax.all_gather(query_w, "dp", axis=0, tiled=True),
        lax.all_gather(key_value_w, "dp", axis=0, tiled=True),
        lax.all_gather(attn_out_w, "dp", axis=1, tiled=True),
        lax.all_gather(gate_up_b, "dp", axis=0, tiled=True),
        lax.all_gather(down_b, "dp", axis=1, tiled=True),
    )
    query_cols = w_query.shape[1]
    heads_local = query_cols // HD
    kv_local = w_kv.shape[2] // HD
    group = heads_local // kv_local
    third_full = spread(norm_rows(hidden_two, gain_rows[2]).astype(jnp.bfloat16))
    query_pre = jnp.dot(third_full, w_query, preferred_element_type=jnp.float32)
    key_value = jnp.einsum("sd,dkc->skc", third_full, w_kv, preferred_element_type=jnp.float32)
    query_rot, query_pull = jax.vjp(
        lambda inner: rope(inner, positions), query_pre.reshape(length, heads_local, HD)
    )
    keys_rot, keys_pull = jax.vjp(
        lambda inner: rope(inner, positions), key_value[:, 0].reshape(length, kv_local, HD)
    )
    query_low = query_rot.astype(jnp.bfloat16).reshape(length, kv_local, group, HD)
    keys_low = keys_rot.astype(jnp.bfloat16)
    values_low = key_value[:, 1].reshape(length, kv_local, HD).astype(jnp.bfloat16)
    block = min(512, length)
    attended_parts = []
    log_totals = []
    for block_index in range(length // block):
        start = block_index * block
        allowed = allowed_mask(segment_ids, start, block)
        attended, log_total = attend_forward(
            query_low[start : start + block], keys_low, values_low, allowed
        )
        attended_parts.append(attended)
        log_totals.append(log_total)
    attended_low = (
        jnp.concatenate(attended_parts, axis=0).reshape(length, query_cols).astype(jnp.bfloat16)
    )
    hidden_three = hidden_two + collect(row_product(attended_low, w_attn))
    hidden_four, kept_b = feed_forward(hidden_three, gain_rows[3], w_gu_b, w_down_b)
    output = hidden_four.astype(jnp.bfloat16)[None]
    w_query, w_kv, w_attn, w_gu_b, w_down_b = (
        lax.all_gather(query_w, "dp", axis=0, tiled=True),
        lax.all_gather(key_value_w, "dp", axis=0, tiled=True),
        lax.all_gather(attn_out_w, "dp", axis=1, tiled=True),
        lax.all_gather(gate_up_b, "dp", axis=0, tiled=True),
        lax.all_gather(down_b, "dp", axis=1, tiled=True),
    )
    grad_four = cotangent[0].astype(jnp.float32)
    grad_three, gain_grad_three, grad_gu_b, grad_dn_b = feed_back(
        grad_four, hidden_three, gain_rows[3], w_gu_b, w_down_b, kept_b
    )
    attn_full = spread_grad(grad_three.astype(jnp.bfloat16))
    grad_attn = jnp.einsum("sc,sd->cd", attended_low, attn_full, preferred_element_type=jnp.float32)
    grad_attended = jnp.einsum("sd,cd->sc", attn_full, w_attn, preferred_element_type=jnp.float32)
    grad_attended = grad_attended.astype(jnp.bfloat16).reshape(length, kv_local, group, HD)
    grad_keys = jnp.zeros((length, kv_local, HD), jnp.float32)
    grad_values = jnp.zeros((length, kv_local, HD), jnp.float32)
    query_grads = []
    for block_index in range(length // block):
        start = block_index * block
        allowed = allowed_mask(segment_ids, start, block)
        grad_query, keys_part, values_part = attend_backward(
            query_low[start : start + block],
            keys_low,
            values_low,
            allowed,
            log_totals[block_index],
            grad_attended[start : start + block],
        )
        query_grads.append(grad_query)
        grad_keys = grad_keys + keys_part
        grad_values = grad_values + values_part
    grad_query_rot = jnp.concatenate(query_grads, axis=0).reshape(length, heads_local, HD)
    grad_query_low = query_pull(grad_query_rot)[0].reshape(length, query_cols).astype(jnp.bfloat16)
    grad_keys_low = keys_pull(grad_keys)[0].reshape(length, kv_local * HD).astype(jnp.bfloat16)
    grad_kv_low = jnp.stack(
        [grad_keys_low, grad_values.reshape(length, kv_local * HD).astype(jnp.bfloat16)], axis=1
    )
    grad_wq = jnp.einsum(
        "sd,sc->dc", third_full, grad_query_low, preferred_element_type=jnp.float32
    )
    grad_wkv = jnp.einsum(
        "sd,skc->dkc", third_full, grad_kv_low, preferred_element_type=jnp.float32
    )

    def attn_term(start, count):
        from_query = jnp.einsum(
            "sc,dc->sd", grad_query_low, w_query, preferred_element_type=jnp.float32
        )
        return from_query + jnp.einsum(
            "skc,dkc->sd", grad_kv_low, w_kv, preferred_element_type=jnp.float32
        )

    grad_third = collect_grad(attn_term)
    norm_pull_three = jax.vjp(norm_rows, hidden_two, gain_rows[2])[1]
    grad_hidden_two, gain_grad_two = norm_pull_three(grad_third)
    grad_two = grad_three + grad_hidden_two
    summed_wq, summed_wkv, summed_attn, summed_gu_b, summed_dn_b = (
        lax.psum_scatter(grad_wq, "dp", scatter_dimension=0, tiled=True),
        lax.psum_scatter(grad_wkv, "dp", scatter_dimension=0, tiled=True),
        lax.psum_scatter(grad_attn, "dp", scatter_dimension=1, tiled=True),
        lax.psum_scatter(grad_gu_b, "dp", scatter_dimension=0, tiled=True),
        lax.psum_scatter(grad_dn_b, "dp", scatter_dimension=1, tiled=True),
    )
    conv_all, w_in, w_out, w_gu_a, w_down_a = (
        lax.all_gather(taps, "dp", axis=1, tiled=True),
        lax.all_gather(in_proj, "dp", axis=0, tiled=True),
        lax.all_gather(out_proj, "dp", axis=1, tiled=True),
        lax.all_gather(gate_up_a, "dp", axis=0, tiled=True),
        lax.all_gather(down_a, "dp", axis=1, tiled=True),
    )
    grad_one, gain_grad_one, grad_gu_a, grad_dn_a = feed_back(
        grad_two, hidden_one, gain_rows[1], w_gu_a, w_down_a, kept_a
    )
    conv_full = spread_grad(grad_one.astype(jnp.bfloat16))
    grad_wout = jnp.einsum("sc,sd->cd", conv_low, conv_full, preferred_element_type=jnp.float32)
    grad_conv = jnp.einsum("sd,cd->sc", conv_full, w_out, preferred_element_type=jnp.float32)
    grad_mixed, grad_kernel = conv_pull(grad_conv)
    grad_mixed_low = grad_mixed.astype(jnp.bfloat16)
    grad_win = jnp.einsum(
        "sd,skc->dkc", first_full, grad_mixed_low, preferred_element_type=jnp.float32
    )

    def conv_term(start, count):
        return jnp.einsum("skc,dkc->sd", grad_mixed_low, w_in, preferred_element_type=jnp.float32)

    grad_first = collect_grad(conv_term)
    norm_pull_one = jax.vjp(norm_rows, hidden_zero, gain_rows[0])[1]
    grad_hidden_zero, gain_grad_zero = norm_pull_one(grad_first)
    grad_zero = grad_one + grad_hidden_zero
    model_width = gain_rows.shape[1]
    kernel_full = lax.dynamic_update_slice(
        jnp.zeros((3, model_width), jnp.float32), grad_kernel, (0, tensor_rank * width_half)
    )
    gains_full = jnp.stack([gain_grad_zero, gain_grad_one, gain_grad_two, gain_grad_three], axis=0)
    gain_part, kernel_part, summed_win, summed_wout, summed_gu_a, summed_dn_a = (
        lax.psum_scatter(gains_full, "dp", scatter_dimension=1, tiled=True),
        lax.psum_scatter(kernel_full, "dp", scatter_dimension=1, tiled=True),
        lax.psum_scatter(grad_win, "dp", scatter_dimension=0, tiled=True),
        lax.psum_scatter(grad_wout, "dp", scatter_dimension=1, tiled=True),
        lax.psum_scatter(grad_gu_a, "dp", scatter_dimension=0, tiled=True),
        lax.psum_scatter(grad_dn_a, "dp", scatter_dimension=1, tiled=True),
    )
    gain_sums, kernel_sums = lax.psum((gain_part, kernel_part), "tensor")
    return (
        output,
        grad_zero[None],
        gain_sums,
        kernel_sums,
        summed_win,
        summed_wout,
        summed_gu_a,
        summed_dn_a,
        summed_wq,
        summed_wkv,
        summed_attn,
        summed_gu_b,
        summed_dn_b,
    )


def solution(mesh):
    return jax.shard_map(
        per_device,
        mesh=mesh,
        in_specs=(
            P("dp", "tensor", None),
            P("dp", None),
            P(None, "dp"),
            P(None, "dp"),
            P("dp", None, "tensor"),
            P("tensor", "dp"),
            P("dp", None, "tensor"),
            P("tensor", "dp"),
            P("dp", "tensor"),
            P("dp", None, "tensor"),
            P("tensor", "dp"),
            P("dp", None, "tensor"),
            P("tensor", "dp"),
            P("dp", "tensor", None),
        ),
        out_specs=(
            P("dp", "tensor", None),
            P("dp", "tensor", None),
            P(None, "dp"),
            P(None, "dp"),
            P("dp", None, "tensor"),
            P("tensor", "dp"),
            P("dp", None, "tensor"),
            P("tensor", "dp"),
            P("dp", "tensor"),
            P("dp", None, "tensor"),
            P("tensor", "dp"),
            P("dp", None, "tensor"),
            P("tensor", "dp"),
        ),
        check_vma=False,
    )
```

profile of v0, /device:TPU:0, one launch (start us, length us, event | category | flops | bytes accessed | tf_op | source)
XLA Modules:
  0.0 2718.4 jit_solution(13431535442109676375)
XLA Ops:
  8.8 42.7 %all-gather.1 = bf16[16,64,4]{1,2,0:T(4,128)(2,1)S(1)} all-gather(bf16[1,64,4]{1,2,0:T(4,128)(2,1)} %bitcast.398), channel_id=1, replica_groups=mesh['dp'=16,'tensor'=2] {'dp'}, dimensions={0}, use_global_device_ids=true | all-gather | bytes 8704 | tf_op jit(solution)/shard_map/all_gather | solution.py:194
  55.8 35.5 %all-gather.2 = bf16[16,64,3]{1,2,0:T(4,128)(2,1)S(1)} all-gather(bf16[1,64,3]{1,2,0:T(4,128)(2,1)S(1)} %bitcast.399), channel_id=1, replica_groups=mesh['dp'=16,'tensor'=2] {'dp'}, dimensions={0}, use_global_device_ids=true | all-gather | bytes 6528 | tf_op jit(solution)/shard_map/all_gather | solution.py:195
  91.7 40.6 %all-gather.23.cloned.1.call-done = bf16[1024,3,512]{2,0,1:T(8,128)(2,1)} async-done(((bf16[64,3,512]{2,0,1:T(8,128)(2,1)}), bf16[1024,3,512]{2,0,1:T(8,128)(2,1)}) %all-gather.23.cloned.1.call-update) | async-done | bytes 3145744 | tf_op jit(solution)/shard_map/all_gather | solution.py:196
  143.9 45.5 %all-gather.25.cloned.1.call-done = bf16[512,1024]{0,1:T(8,128)(2,1)} async-done(((bf16[512,64]{0,1:T(8,128)(2,1)}), bf16[512,1024]{0,1:T(8,128)(2,1)}) %all-gather.25.cloned.1.call-update) | async-done | bytes 1048592 | tf_op jit(solution)/shard_map/all_gather | solution.py:197
  217.1 127.1 %all-gather.29.cloned.1.call-done = bf16[1024,2,2304]{2,0,1:T(8,128)(2,1)} async-done(((bf16[64,2,2304]{2,0,1:T(8,128)(2,1)}), bf16[1024,2,2304]{2,0,1:T(8,128)(2,1)}) %all-gather.29.cloned.1.call-update) | async-done | bytes 9437200 | tf_op jit(solution)/shard_map/all_gather | solution.py:198
  344.2 13.1 fusion.66
  368.1 57.9 %all-gather.31.cloned.1.call-done = bf16[2304,1024]{0,1:T(8,128)(2,1)} async-done(((bf16[2304,64]{0,1:T(8,128)(2,1)}), bf16[2304,1024]{0,1:T(8,128)(2,1)}) %all-gather.31.cloned.1.call-update) | async-done | bytes 4718608 | tf_op jit(solution)/shard_map/all_gather | solution.py:199
  451.8 52.0 %all-gather.35.cloned.1.call-done = bf16[1024,2,256]{2,0,1:T(8,128)(2,1)} async-done(((bf16[64,2,256]{2,0,1:T(8,128)(2,1)}), bf16[1024,2,256]{2,0,1:T(8,128)(2,1)}) %all-gather.35.cloned.1.call-update) | async-done | bytes 1048592 | tf_op jit(solution)/shard_map/all_gather | solution.py:217
  518.8 55.8 %all-gather.37.cloned.1.call-done = bf16[1024,512]{1,0:T(8,128)(2,1)} async-done(((bf16[64,512]{1,0:T(8,128)(2,1)}), bf16[1024,512]{1,0:T(8,128)(2,1)}) %all-gather.37.cloned.1.call-update) | async-done | bytes 1048592 | tf_op jit(solution)/shard_map/all_gather | solution.py:216
  648.3 122.8 %all-gather.43.cloned.1.call-done = bf16[1024,2,2304]{2,0,1:T(8,128)(2,1)} async-done(((bf16[64,2,2304]{2,0,1:T(8,128)(2,1)}), bf16[1024,2,2304]{2,0,1:T(8,128)(2,1)}) %all-gather.43.cloned.1.call-update) | async-done | bytes 9437200 | tf_op jit(solution)/shard_map/all_gather | solution.py:219
  782.0 16.9 fusion.58
  798.9 81.1 %all-gather.45.cloned.1.call-done = bf16[2304,1024]{0,1:T(8,128)(2,1)} async-done(((bf16[2304,64]{0,1:T(8,128)(2,1)}), bf16[2304,1024]{0,1:T(8,128)(2,1)}) %all-gather.45.cloned.1.call-update) | async-done | bytes 4718608 | tf_op jit(solution)/shard_map/all_gather | solution.py:220
  880.0 19.2 multiply_bitcast_fusion.1
  899.1 17.6 bitcast_convert_fusion.2
  931.8 11.8 all-gather.47.cloned.1.call-done
  967.8 12.9 fusion.5
  1000.6 12.8 fusion.2
  1058.5 11.9 all-gather.49.cloned.1.call-done
  1070.3 17.9 multiply_bitcast_fusion
  1088.2 17.6 bitcast_convert_fusion.1
  1166.9 17.7 fusion.56
  1186.2 17.8 fusion.64
  1256.0 66.9 %reduce-scatter.60.cloned.1.call-done = f32[64,3]{1,0:T(8,128)} async-done(((f32[1024,3]{1,0:T(8,128)}), f32[64,3]{1,0:T(8,128)}) %reduce-scatter.60.cloned.1.call-update) | async-done | bytes 784
  1328.2 70.6 %reduce-scatter.58.cloned.1.call-done = f32[64,4]{1,0:T(8,128)} async-done(((f32[1024,4]{1,0:T(8,128)}), f32[64,4]{1,0:T(8,128)}) %reduce-scatter.58.cloned.1.call-update) | async-done | bytes 1040
  1402.7 283.0 %reduce-scatter.54.cloned.1.call-done = f32[64,2,2304]{2,0,1:T(8,128)} async-done(((f32[1024,2,2304]{2,0,1:T(8,128)}), f32[64,2,2304]{2,0,1:T(8,128)}) %reduce-scatter.54.cloned.1.call-update) | async-done | bytes 1179664 | tf_op jit(solution)/shard_map/reduce_scatter | solution.py:316
  1688.9 286.4 %reduce-scatter.44.cloned.1.call-done = f32[64,2,2304]{2,0,1:T(8,128)} async-done(((f32[1024,2,2304]{2,0,1:T(8,128)}), f32[64,2,2304]{2,0,1:T(8,128)}) %reduce-scatter.44.cloned.1.call-update) | async-done | bytes 1179664 | tf_op jit(solution)/shard_map/reduce_scatter | solution.py:355
  1978.4 79.3 %reduce-scatter.52.cloned.1.call-done = f32[512,64]{0,1:T(8,128)} async-done(((f32[512,1024]{0,1:T(8,128)}), f32[512,64]{0,1:T(8,128)}) %reduce-scatter.52.cloned.1.call-update) | async-done | bytes 131088 | tf_op jit(solution)/shard_map/reduce_scatter | solution.py:315
  2057.7 81.1 %reduce-scatter.48.cloned.1.call-done = f32[64,512]{1,0:T(8,128)} async-done(((f32[1024,512]{1,0:T(8,128)}), f32[64,512]{1,0:T(8,128)}) %reduce-scatter.48.cloned.1.call-update) | async-done | bytes 131088 | tf_op jit(solution)/shard_map/reduce_scatter | solution.py:313
  2138.8 174.5 %reduce-scatter.56.cloned.1.call-done = f32[2304,64]{0,1:T(8,128)} async-done(((f32[2304,1024]{0,1:T(8,128)}), f32[2304,64]{0,1:T(8,128)}) %reduce-scatter.56.cloned.1.call-update) | async-done | bytes 589840 | tf_op jit(solution)/shard_map/reduce_scatter | solution.py:317
  2313.4 82.4 %reduce-scatter.42.cloned.1.call-done = f32[512,64]{0,1:T(8,128)} async-done(((f32[512,1024]{0,1:T(8,128)}), f32[512,64]{0,1:T(8,128)}) %reduce-scatter.42.cloned.1.call-update) | async-done | bytes 131088 | tf_op jit(solution)/shard_map/reduce_scatter | solution.py:354
  2395.7 136.5 %reduce-scatter.40.cloned.1.call-done = f32[64,3,512]{2,0,1:T(8,128)} async-done(((f32[1024,3,512]{2,0,1:T(8,128)}), f32[64,3,512]{2,0,1:T(8,128)}) %reduce-scatter.40.cloned.1.call-update) | async-done | bytes 393232 | tf_op jit(solution)/shard_map/reduce_scatter | solution.py:353
  2532.2 179.5 %reduce-scatter.46.cloned.1.call-done = f32[2304,64]{0,1:T(8,128)} async-done(((f32[2304,1024]{0,1:T(8,128)}), f32[2304,64]{0,1:T(8,128)}) %reduce-scatter.46.cloned.1.call-update) | async-done | bytes 589840 | tf_op jit(solution)/shard_map/reduce_scatter | solution.py:356
  (390 shorter events, 414.5 us)
Async XLA Ops:
  7.2 84.5 %all-gather.21.cloned.1.call-start = ((), (), s32[]{:S(2)}) async-start(), calls=%async_computation.19 | async-start | bytes 3145728 | tf_op jit(solution)/shard_map/all_gather | solution.py:69
  54.1 78.2 %all-gather.23.cloned.1.call-start = ((), (), s32[]{:S(2)}) async-start(), calls=%async_computation.20 | async-start | bytes 3342336 | tf_op jit(solution)/shard_map/all_gather | solution.py:196
  54.9 134.6 %all-gather.25.cloned.1.call-start = ((), (), s32[]{:S(2)}) async-start(), calls=%async_computation.21 | async-start | bytes 1114112 | tf_op jit(solution)/shard_map/all_gather | solution.py:197
  55.6 146.3 %reduce-scatter.24.cloned.1.call-start = ((), (), s32[]{:S(2)}) async-start(), calls=%async_computation.22 | async-start | bytes 3145728 | tf_op jit(solution)/shard_map/reduce_scatter | solution.py:147
  205.2 139.0 %all-gather.29.cloned.1.call-start = ((), (), s32[]{:S(2)}) async-start(), calls=%async_computation.24 | async-start | bytes 10027008 | tf_op jit(solution)/shard_map/all_gather | solution.py:198
  206.1 219.9 %all-gather.31.cloned.1.call-start = ((), (), s32[]{:S(2)}) async-start(), calls=%async_computation.25 | async-start | bytes 5013504 | tf_op jit(solution)/shard_map/all_gather | solution.py:199
  206.9 236.9 %reduce-scatter.26.cloned.1.call-start = ((), (), s32[]{:S(2)}) async-start(), calls=%async_computation.26 | async-start | bytes 3145728 | tf_op jit(solution)/shard_map/reduce_scatter | solution.py:147
  435.4 68.4 %all-gather.35.cloned.1.call-start = ((), (), s32[]{:S(2)}) async-start(), calls=%async_computation.28 | async-start | bytes 1114112 | tf_op jit(solution)/shard_map/all_gather | solution.py:217
  436.9 78.4 %all-gather.33.cloned.1.call-start = ((), (), s32[]{:S(2)}) async-start(), calls=%async_computation.27 | async-start | bytes 3145728 | tf_op jit(solution)/shard_map/all_gather | solution.py:69
  447.5 127.1 %all-gather.37.cloned.1.call-start = ((), (), s32[]{:S(2)}) async-start(), calls=%async_computation.29 | async-start | bytes 1114112 | tf_op jit(solution)/shard_map/all_gather | solution.py:216
  448.2 183.0 %all-gather.39.cloned.1.call-start = ((), (), s32[]{:S(2)}) async-start(), calls=%async_computation.30 | async-start | bytes 1114112 | tf_op jit(solution)/shard_map/all_gather | solution.py:218
  448.8 195.2 %reduce-scatter.28.cloned.1.call-start = ((), (), s32[]{:S(2)}) async-start(), calls=%async_computation.31 | async-start | bytes 3145728 | tf_op jit(solution)/shard_map/reduce_scatter | solution.py:147
  635.5 135.7 %all-gather.43.cloned.1.call-start = ((), (), s32[]{:S(2)}) async-start(), calls=%async_computation.33 | async-start | bytes 10027008 | tf_op jit(solution)/shard_map/all_gather | solution.py:219
  637.4 144.6 %all-gather.41.cloned.1.call-start = ((), (), s32[]{:S(2)}) async-start(), calls=%async_computation.32 | async-start | bytes 3145728 | tf_op jit(solution)/shard_map/all_gather | solution.py:69
  647.1 151.8 %all-gather.53.cloned.1.call-start = ((), (), s32[]{:S(2)}) async-start(), calls=%async_computation.52 | async-start | bytes 3145728 | tf_op jit(solution)/shard_map/all_gather | solution.py:73
  647.7 232.3 %all-gather.45.cloned.1.call-start = ((), (), s32[]{:S(2)}) async-start(), calls=%async_computation.34 | async-start | bytes 5013504 | tf_op jit(solution)/shard_map/all_gather | solution.py:220
  648.3 276.9 %reduce-scatter.32.cloned.1.call-start = ((), (), s32[]{:S(2)}) async-start(), calls=%async_computation.36 | async-start | bytes 3145728 | tf_op jit(solution)/shard_map/reduce_scatter | solution.py:155
  931.7 108.7 %reduce-scatter.34.cloned.1.call-start = ((), (), s32[]{:S(2)}) async-start(), calls=%async_computation.38 | async-start | bytes 3145728 | tf_op jit(solution)/shard_map/reduce_scatter | solution.py:155
  1038.9 31.4 %all-gather.49.cloned.1.call-start = ((), (), s32[]{:S(2)}) async-start(), calls=%async_computation.39 | async-start | bytes 3145728 | tf_op jit(solution)/shard_map/all_gather | solution.py:73
  1058.4 58.4 %reduce-scatter.36.cloned.1.call-start = ((), (), s32[]{:S(2)}) async-start(), calls=%async_computation.40 | async-start | bytes 3145728 | tf_op jit(solution)/shard_map/reduce_scatter | solution.py:155
  1122.3 40.9 %reduce-scatter.38.cloned.1.call-start = ((), (), s32[]{:S(2)}) async-start(), calls=%async_computation.42 | async-start | bytes 3145728 | tf_op jit(solution)/shard_map/reduce_scatter | solution.py:155
  1152.3 101.9 %reduce-scatter.50.cloned.1.call-start = ((), (), s32[]{:S(2)}) async-start(), calls=%async_computation.48 | async-start | bytes 2228224 | tf_op jit(solution)/shard_map/reduce_scatter | solution.py:314
  1157.7 165.1 %reduce-scatter.60.cloned.1.call-start = ((), (), s32[]{:S(2)}) async-start(), calls=%async_computation.54 | async-start | bytes 557056
  1158.9 240.0 %reduce-scatter.58.cloned.1.call-start = ((), (), s32[]{:S(2)}) async-start(), calls=%async_computation.53 | async-start | bytes 557056
  1166.5 519.2 %reduce-scatter.54.cloned.1.call-start = ((), (), s32[]{:S(2)}) async-start(), calls=%async_computation.50 | async-start | bytes 20054016 | tf_op jit(solution)/shard_map/reduce_scatter | solution.py:316
  1184.6 790.6 %reduce-scatter.44.cloned.1.call-start = ((), (), s32[]{:S(2)}) async-start(), calls=%async_computation.45 | async-start | bytes 20054016 | tf_op jit(solution)/shard_map/reduce_scatter | solution.py:355
  1204.0 853.7 %reduce-scatter.52.cloned.1.call-start = ((), (), s32[]{:S(2)}) async-start(), calls=%async_computation.49 | async-start | bytes 2228224 | tf_op jit(solution)/shard_map/reduce_scatter | solution.py:315
  1209.5 929.3 %reduce-scatter.48.cloned.1.call-start = ((), (), s32[]{:S(2)}) async-start(), calls=%async_computation.47 | async-start | bytes 2228224 | tf_op jit(solution)/shard_map/reduce_scatter | solution.py:313
  1215.0 1098.3 %reduce-scatter.56.cloned.1.call-start = ((), (), s32[]{:S(2)}) async-start(), calls=%async_computation.51 | async-start | bytes 10027008 | tf_op jit(solution)/shard_map/reduce_scatter | solution.py:317
  1226.6 1169.2 %reduce-scatter.42.cloned.1.call-start = ((), (), s32[]{:S(2)}) async-start(), calls=%async_computation.44 | async-start | bytes 2228224 | tf_op jit(solution)/shard_map/reduce_scatter | solution.py:354
  1232.1 1300.1 %reduce-scatter.40.cloned.1.call-start = ((), (), s32[]{:S(2)}) async-start(), calls=%async_computation.43 | async-start | bytes 6684672 | tf_op jit(solution)/shard_map/reduce_scatter | solution.py:353
  1242.7 1469.0 %reduce-scatter.46.cloned.1.call-start = ((), (), s32[]{:S(2)}) async-start(), calls=%async_computation.46 | async-start | bytes 10027008 | tf_op jit(solution)/shard_map/reduce_scatter | solution.py:356
  (96 other events, 2252.5 us)
Sparse Core Ops, SparseCore 0:
  63.5 68.7 all-gather.22
  135.1 54.3 all-gather.24
  193.5 8.3 reduce-scatter.23
  205.3 11.7 all-gather.26
  220.5 123.5 all-gather.28
  347.3 78.6 all-gather.30
  447.1 56.5 all-gather.34
  505.7 9.5 all-gather.32
  518.1 56.4 all-gather.36
  577.2 54.0 all-gather.38
  647.5 123.5 all-gather.42
  773.2 8.7 all-gather.40
  783.5 11.7 all-gather.52
  798.3 81.6 all-gather.44
  931.8 11.7 all-gather.46
  1029.6 10.7 reduce-scatter.33
  1042.7 10.7 reduce-scatter.29
  1058.5 11.7 all-gather.48
  1105.9 10.7 reduce-scatter.35
  1122.4 11.7 all-gather.50
  1152.4 10.7 reduce-scatter.37
  1165.4 82.0 reduce-scatter.49
  1249.5 73.2 reduce-scatter.59
  1325.8 73.0 reduce-scatter.57
  1404.6 281.0 reduce-scatter.53
  1691.3 283.8 reduce-scatter.43
  1978.1 79.5 reduce-scatter.51
  2060.6 78.2 reduce-scatter.47
  2144.9 168.3 reduce-scatter.55
  2316.3 79.3 reduce-scatter.41
  2398.7 133.4 reduce-scatter.39
  2539.2 172.3 reduce-scatter.45
  (4 shorter events, 31.1 us)
where the time goes:
time: 2730 us; the launch traced here: 2720 us
  waiting for transfers between devices  2160 us (79%)
  matrix products  313 us (11%)
  other arithmetic  104 us (4%)
  blocking collectives  81.2 us (3%)
  local copies, waits for them, and re-layouts  43.3 us (2%)
    reduce_scatter x1, waiting for transfers between devices, per_device(): lax.psum_scatter(grad_gu_a, 'dp', scatter_dimension=0, tiled=True)  286 us
    reduce_scatter x1, waiting for transfers between devices, per_device(): lax.psum_scatter(grad_gu_b, 'dp', scatter_dimension=0, tiled=True)  283 us
    reduce_scatter x1, waiting for transfers between devices, per_device(): lax.psum_scatter(grad_dn_a, 'dp', scatter_dimension=1, tiled=True)  179 us
    reduce_scatter x1, waiting for transfers between devices, per_device(): lax.psum_scatter(grad_dn_b, 'dp', scatter_dimension=1, tiled=True)  175 us
    unnamed x38, waiting for transfers between devices  142 us
    reduce_scatter x1, waiting for transfers between devices, per_device(): lax.psum_scatter(grad_win, 'dp', scatter_dimension=0, tiled=True)  136 us
    all_gather x1, waiting for transfers between devices, per_device(): lax.all_gather(gate_up_a, 'dp', axis=0, tiled=True)  127 us
    all_gather x1, waiting for transfers between devices, per_device(): lax.all_gather(gate_up_b, 'dp', axis=0, tiled=True)  123 us
  transfers between devices with their start and end apart: 36, of which 33 were waited for; matrix products, arithmetic and copies ran while one was open for 8% of the time, Pallas kernels for 0%

commit v1 on v0

v1 whole, which is shorter than its diff:
```python
import math

import jax
import jax.numpy as jnp
from jax import lax
from jax.sharding import PartitionSpec as P

HD = 64
EPS = 1e-05
THETA = 1000000.0
SCALE = 0.125
BF = jnp.bfloat16
F32 = jnp.float32


def flip(values, bit):
    n = lax.axis_size("dp")
    return lax.ppermute(values, "dp", [(i, i ^ bit) for i in range(n)])


def turn(values, step):
    n = lax.axis_size("dp")
    return lax.ppermute(values, "dp", [(i, (i + 4 * step) % n) for i in range(n)])


def swap(values):
    return lax.ppermute(values, "tensor", [(0, 1), (1, 0)])


def z_gather(own):
    nz = lax.axis_size("dp") // 4
    blocks = [own] + [None] * (nz - 1)
    from_above = from_below = own
    for r in range(1, nz // 2 + 1):
        from_above = turn(from_above, -1)
        blocks[r] = from_above
        if nz - r > r:
            from_below = turn(from_below, 1)
            blocks[nz - r] = from_below
    return blocks


def z_scatter(blocks):
    nz = len(blocks)
    half = nz // 2
    up = blocks[half]
    for r in range(half - 1, 0, -1):
        up = add_low(blocks[r], turn(up, 1))
    down = blocks[half + 1]
    for r in range(half + 2, nz):
        down = add_low(blocks[r], turn(down, -1))
    return blocks[0].astype(F32) + turn(up, 1).astype(F32) + turn(down, -1).astype(F32)


def add_low(a, b):
    return (a.astype(F32) + b.astype(F32)).astype(BF)


def gather_z_first(own, far):
    base = jnp.concatenate(z_gather(own), axis=0)
    by_x = flip(base, 1)
    by_y = flip(base, 2)
    by_xy = flip(by_x, 2) if far == "y" else flip(by_y, 1)
    return jnp.concatenate([base, by_x, by_y, by_xy], axis=0)


def gather_z_last(own, far):
    by_x = flip(own, 1)
    by_y = flip(own, 2)
    by_xy = flip(by_x, 2) if far == "y" else flip(by_y, 1)
    blocks = z_gather(jnp.stack([own, by_x, by_y, by_xy]))
    full = jnp.stack(blocks, axis=1)
    return full.reshape(-1, own.shape[-1])


def flip_scatter(parts, far):
    if far == "y":
        one = add_low(parts[1], flip(parts[3], 2))
        return parts[0].astype(F32) + flip(one, 1).astype(F32) + flip(parts[2], 2).astype(F32)
    two = add_low(parts[2], flip(parts[3], 1))
    return parts[0].astype(F32) + flip(two, 2).astype(F32) + flip(parts[1], 1).astype(F32)


def scatter_z_last(grad, far):
    nz = lax.axis_size("dp") // 4
    quarter = grad.shape[0] // 4
    rows = quarter // nz
    mine = flip_scatter([grad[j * quarter : (j + 1) * quarter] for j in range(4)], far).astype(BF)
    return z_scatter([mine[r * rows : (r + 1) * rows] for r in range(nz)])


def scatter_z_first(grad, far):
    nz = lax.axis_size("dp") // 4
    rows = grad.shape[0] // (4 * nz)
    blocks = grad.reshape(4, nz, rows, grad.shape[1])
    mine = z_scatter([blocks[:, r] for r in range(nz)]).astype(BF)
    return flip_scatter([mine[j] for j in range(4)], far)


def dot_nn(a, w):
    return jnp.dot(a, w, preferred_element_type=F32)


def dot_nt(a, w):
    return lax.dot_general(a, w, (((1,), (1,)), ((), ())), preferred_element_type=F32)


def dot_tn(a, b):
    return lax.dot_general(a, b, (((0,), (0,)), ((), ())), preferred_element_type=F32)


def inv_rms(values):
    return lax.rsqrt(jnp.mean(values * values, axis=-1, keepdims=True) + EPS)


def norm_low(values, gain):
    return (values * inv_rms(values) * gain).astype(BF)


def norm_back(grad_normed, values, gain, grad_out):
    q = inv_rms(values)
    grad_gain = jnp.sum(grad_normed * values * q, axis=0)
    a2 = grad_normed * gain
    inner = jnp.mean(a2 * values, axis=-1, keepdims=True)
    return grad_out + q * a2 - values * (q * q * q * inner), grad_gain


def rope_tables(positions):
    half = HD // 2
    freq = jnp.exp(jnp.arange(half, dtype=F32) * (-2.0 * math.log(THETA) / (2 * half)))
    angle = positions[:, None] * freq[None, :]
    return jnp.cos(angle)[:, None, :], jnp.sin(angle)[:, None, :]


def rope(values, cosine, sine):
    half = HD // 2
    first, second = values[..., :half], values[..., half:]
    return jnp.concatenate([first * cosine - second * sine, second * cosine + first * sine], axis=-1)


def conv_mix(mixed, kernel, same_one, same_two):
    driven = mixed[0] * mixed[2]
    zero = jnp.zeros((2, driven.shape[1]), driven.dtype)
    back_one = jnp.concatenate([zero[:1], driven[:-1]], axis=0) * same_one
    back_two = jnp.concatenate([zero, driven[:-2]], axis=0) * same_two
    return mixed[1] * (kernel[0] * driven + kernel[1] * back_one + kernel[2] * back_two)


def allowed_mask(segment_ids, start, block):
    length = segment_ids.shape[0]
    row_index = start + jnp.arange(block)
    col_index = jnp.arange(length)
    row_segs = segment_ids[start : start + block]
    return (col_index[None, :] <= row_index[:, None]) & (segment_ids[None, :] == row_segs[:, None])


def attend_forward(q_block, keys, values, allowed):
    scores = SCALE * jnp.einsum("qhgd,khd->hgqk", q_block, keys, preferred_element_type=F32)
    scores = jnp.where(allowed, scores, -1e30)
    row_max = jnp.max(scores, axis=-1, keepdims=True)
    lifted = jnp.exp(scores - row_max)
    row_total = jnp.sum(lifted, axis=-1, keepdims=True)
    probs = (lifted / row_total).astype(BF)
    attended = jnp.einsum("hgqk,khd->qhgd", probs, values, preferred_element_type=F32)
    return (attended, row_max + jnp.log(row_total))


def attend_backward(q_block, keys, values, allowed, log_total, grad_block):
    scores = SCALE * jnp.einsum("qhgd,khd->hgqk", q_block, keys, preferred_element_type=F32)
    probs = jnp.exp(jnp.where(allowed, scores, -1e30) - log_total)
    grad_values = jnp.einsum("hgqk,qhgd->khd", probs.astype(BF), grad_block, preferred_element_type=F32)
    grad_probs = jnp.einsum("qhgd,khd->hgqk", grad_block, values, preferred_element_type=F32)
    grad_scores = (
        probs * (grad_probs - jnp.sum(probs * grad_probs, axis=-1, keepdims=True))
    ).astype(BF)
    grad_query = SCALE * jnp.einsum("hgqk,khd->qhgd", grad_scores, keys, preferred_element_type=F32)
    grad_keys = SCALE * jnp.einsum("hgqk,qhgd->khd", grad_scores, q_block, preferred_element_type=F32)
    return (grad_query, grad_keys, grad_values)


def per_device(
    tokens_in,
    segments,
    gains,
    taps,
    in_proj,
    out_proj,
    gate_up_a,
    down_a,
    query_w,
    key_value_w,
    attn_out_w,
    gate_up_b,
    down_b,
    cotangent,
):
    half = tokens_in.shape[1]
    segment_ids = segments[0]
    length = segment_ids.shape[0]
    dp_size = lax.axis_size("dp")
    nz = dp_size // 4
    rows = in_proj.shape[0]
    width = rows * dp_size
    rank = lax.axis_index("tensor")
    me = lax.axis_index("dp")

    flips = jnp.arange(dp_size) // nz
    steps = jnp.arange(dp_size) % nz
    owner = ((me // 4 + steps) % nz) * 4 + ((me % 4) ^ flips)
    place = (owner[:, None] * rows + jnp.arange(rows)[None, :]).reshape(width)
    to_rel = (jnp.arange(width)[:, None] == place[None, :]).astype(BF)

    def both(own):
        return jnp.concatenate([own, swap(own)], axis=0)

    def in_order(own):
        other = swap(own)
        first = jnp.where(rank == 0, own, other)
        second = jnp.where(rank == 0, other, own)
        return jnp.concatenate([first, second], axis=0)

    def own_half(full):
        return lax.dynamic_slice_in_dim(full, rank * half, half, 0)

    def other_half(full):
        return lax.dynamic_slice_in_dim(full, (1 - rank) * half, half, 0)

    misc = jnp.concatenate(
        [gains.T, taps.T, jnp.zeros((rows, 128 - gains.shape[0] - taps.shape[0]), BF)], axis=1
    )
    conv_cols = in_proj.shape[2]
    first_item = gather_z_first(
        jnp.concatenate([misc] + [in_proj[:, k] for k in range(3)], axis=1), "y"
    )
    w_out = gather_z_last(out_proj.T, "x")
    misc_all = first_item[:, :128]
    w_in = [first_item[:, 128 + k * conv_cols : 128 + (k + 1) * conv_cols] for k in range(3)]

    def gather_ff(gate_up, down):
        gate = gather_z_first(gate_up[:, 0], "y")
        up = gather_z_first(gate_up[:, 1], "x")
        down_t = down.T
        cut = down_t.shape[1] // 2
        one = gather_z_last(down_t[:, :cut], "y")
        two = gather_z_first(down_t[:, cut:], "x")
        return gate, up, jnp.concatenate([one, two], axis=1)

    ff_a = gather_ff(gate_up_a, down_a)
    query_cols = query_w.shape[1]
    kv_cols = key_value_w.shape[2]
    w_qkv = gather_z_first(
        jnp.concatenate([query_w, key_value_w[:, 0], key_value_w[:, 1]], axis=1), "y"
    )
    w_attn = gather_z_last(attn_out_w.T, "x")
    ff_b = gather_ff(gate_up_b, down_b)

    gain_rows = misc_all[:, : gains.shape[0]].T.astype(F32)
    taps_all = lax.dot_general(
        misc_all[:, 4:7], to_rel, (((0,), (1,)), ((), ())), preferred_element_type=F32
    )
    kernel = lax.dynamic_slice_in_dim(taps_all, rank * conv_cols, conv_cols, 1)

    index = jnp.arange(length)
    first_of_doc = jnp.sum((segment_ids[None, :] < segment_ids[:, None]).astype(jnp.int32), axis=1)
    positions = (index - first_of_doc).astype(F32)
    same_one = (positions >= 1).astype(F32)[:, None]
    same_two = (positions >= 2).astype(F32)[:, None]
    cosine, sine = rope_tables(positions)

    hidden_zero = dot_nn(tokens_in[0], to_rel)
    first_full = in_order(norm_low(hidden_zero, gain_rows[0]))
    mixed = [dot_nn(first_full, w) for w in w_in]
    conv_out, conv_pull = jax.vjp(
        lambda mixed_in, kernel_in: conv_mix(mixed_in, kernel_in, same_one, same_two), mixed, kernel
    )
    conv_low = conv_out.astype(BF)

    def collect(own, other, w):
        sent = swap(dot_nt(other, w).astype(BF))
        return dot_nt(own, w) + sent.astype(F32)

    hidden_one = hidden_zero + collect(own_half(conv_low), other_half(conv_low), w_out)

    def feed_forward(hidden, gain, weights):
        w_gate, w_up, w_down = weights
        normed = both(norm_low(hidden, gain))
        gate = dot_nn(normed, w_gate)
        up = dot_nn(normed, w_up)
        product = (jax.nn.silu(gate) * up).astype(BF)
        gate, up = gate.astype(BF), up.astype(BF)
        return hidden + collect(product[:half], product[half:], w_down), (normed, gate, up, product)

    def feed_back(grad_out, hidden, gain, weights, kept):
        w_gate, w_up, w_down = weights
        normed, gate, up, product = kept
        grad_full = both(grad_out.astype(BF))
        grad_product = dot_nn(grad_full, w_down)
        gate, up = gate.astype(F32), up.astype(F32)
        sig = jax.nn.sigmoid(gate)
        grad_up = (grad_product * (gate * sig)).astype(BF)
        grad_gate = (grad_product * up * (sig * (1.0 + gate * (1.0 - sig)))).astype(BF)
        g_down = dot_tn(grad_full, product).astype(BF)
        g_gate = dot_tn(normed, grad_gate).astype(BF)
        g_up = dot_tn(normed, grad_up).astype(BF)
        sent = swap((dot_nt(grad_gate[half:], w_gate) + dot_nt(grad_up[half:], w_up)).astype(BF))
        grad_normed = (
            dot_nt(grad_gate[:half], w_gate) + dot_nt(grad_up[:half], w_up) + sent.astype(F32)
        )
        grad_hidden, grad_gain = norm_back(grad_normed, hidden, gain, grad_out)
        return grad_hidden, grad_gain, (g_gate, g_up, g_down)

    def scatter_ff(grads):
        g_gate, g_up, g_down = grads
        cut = g_down.shape[1] // 2
        one = scatter_z_first(g_down[:, :cut], "y")
        two = scatter_z_last(g_down[:, cut:], "x")
        gate = scatter_z_last(g_gate, "y")
        up = scatter_z_last(g_up, "x")
        return jnp.stack([gate, up], axis=1), jnp.concatenate([one, two], axis=1).T

    hidden_two, kept_a = feed_forward(hidden_one, gain_rows[1], ff_a)

    heads_local = query_cols // HD
    kv_local = kv_cols // HD
    group = heads_local // kv_local
    third_full = in_order(norm_low(hidden_two, gain_rows[2]))
    qkv = dot_nn(third_full, w_qkv)
    query_low = rope(qkv[:, :query_cols].reshape(length, heads_local, HD), cosine, sine)
    query_low = query_low.astype(BF).reshape(length, kv_local, group, HD)
    keys_low = rope(
        qkv[:, query_cols : query_cols + kv_cols].reshape(length, kv_local, HD), cosine, sine
    ).astype(BF)
    values_low = qkv[:, query_cols + kv_cols :].reshape(length, kv_local, HD).astype(BF)
    block = min(512, length)
    attended_parts = []
    log_totals = []
    for start in range(0, length, block):
        stop = start + block
        allowed = allowed_mask(segment_ids, start, block)[:, :stop]
        attended, log_total = attend_forward(
            query_low[start:stop], keys_low[:stop], values_low[:stop], allowed
        )
        attended_parts.append(attended)
        log_totals.append(log_total)
    attended_low = jnp.concatenate(attended_parts, axis=0).reshape(length, query_cols).astype(BF)
    hidden_three = hidden_two + collect(own_half(attended_low), other_half(attended_low), w_attn)
    hidden_four, kept_b = feed_forward(hidden_three, gain_rows[3], ff_b)
    output = dot_nt(hidden_four.astype(BF), to_rel).astype(BF)[None]

    grad_four = dot_nn(cotangent[0], to_rel)
    grad_three, gain_grad_three, grads_b = feed_back(
        grad_four, hidden_three, gain_rows[3], ff_b, kept_b
    )
    summed_gu_b, summed_dn_b = scatter_ff(grads_b)
    attn_full = in_order(grad_three.astype(BF))
    grad_attn = dot_tn(attn_full, attended_low).astype(BF)
    grad_attended = dot_nn(attn_full, w_attn).astype(BF).reshape(length, kv_local, group, HD)
    grad_keys = jnp.zeros((length, kv_local, HD), F32)
    grad_values = jnp.zeros((length, kv_local, HD), F32)
    query_grads = []
    for block_index, start in enumerate(range(0, length, block)):
        stop = start + block
        allowed = allowed_mask(segment_ids, start, block)[:, :stop]
        grad_query, keys_part, values_part = attend_backward(
            query_low[start:stop],
            keys_low[:stop],
            values_low[:stop],
            allowed,
            log_totals[block_index],
            grad_attended[start:stop],
        )
        query_grads.append(grad_query)
        pad = ((0, length - stop), (0, 0), (0, 0))
        grad_keys = grad_keys + jnp.pad(keys_part, pad)
        grad_values = grad_values + jnp.pad(values_part, pad)
    grad_query_rot = jnp.concatenate(query_grads, axis=0).reshape(length, heads_local, HD)
    grad_qkv = jnp.concatenate(
        [
            rope(grad_query_rot, cosine, -sine).reshape(length, query_cols).astype(BF),
            rope(grad_keys, cosine, -sine).reshape(length, kv_cols).astype(BF),
            grad_values.reshape(length, kv_cols).astype(BF),
        ],
        axis=1,
    )
    grad_wqkv = dot_tn(third_full, grad_qkv).astype(BF)
    grad_third = collect(own_half(grad_qkv), other_half(grad_qkv), w_qkv)
    grad_two, gain_grad_two = norm_back(grad_third, hidden_two, gain_rows[2], grad_three)
    summed_qkv = scatter_z_last(grad_wqkv, "y")
    summed_attn = scatter_z_first(grad_attn, "x").T

    grad_one, gain_grad_one, grads_a = feed_back(
        grad_two, hidden_one, gain_rows[1], ff_a, kept_a
    )
    summed_gu_a, summed_dn_a = scatter_ff(grads_a)
    conv_full = in_order(grad_one.astype(BF))
    grad_wout = dot_tn(conv_full, conv_low).astype(BF)
    grad_conv = dot_nn(conv_full, w_out)
    grad_mixed, grad_kernel = conv_pull(grad_conv)
    grad_mixed = [g.astype(BF) for g in grad_mixed]
    own_first = sum(dot_nt(own_half(g), w) for g, w in zip(grad_mixed, w_in))
    other_first = sum(dot_nt(other_half(g), w) for g, w in zip(grad_mixed, w_in))
    grad_first = own_first + swap(other_first.astype(BF)).astype(F32)
    grad_zero, gain_grad_zero = norm_back(grad_first, hidden_zero, gain_rows[0], grad_one)

    high = grad_zero.astype(BF)
    lower = (grad_zero - high.astype(F32)).astype(BF)
    grad_input = (dot_nt(high, to_rel) + dot_nt(lower, to_rel))[None]

    kernel_full = lax.dynamic_update_slice(
        jnp.zeros((3, width), F32), grad_kernel, (0, rank * conv_cols)
    )
    kernel_rel = dot_nn(kernel_full.astype(BF), to_rel)
    small = jnp.concatenate(
        [
            jnp.stack([gain_grad_zero, gain_grad_one, gain_grad_two, gain_grad_three]),
            kernel_rel,
            jnp.zeros((128 - 7, width), F32),
        ],
        axis=0,
    ).T.astype(BF)
    grad_win = [dot_tn(first_full, g).astype(BF) for g in grad_mixed]
    summed_first = scatter_z_last(jnp.concatenate([small] + grad_win, axis=1), "y")
    summed_wout = scatter_z_first(grad_wout, "x").T
    summed_win = summed_first[:, 128:].reshape(rows, 3, conv_cols)
    small_sum = summed_first[:, :128]
    small_sum = (small_sum + swap(small_sum)).T
    return (
        output,
        grad_input,
        small_sum[:4],
        small_sum[4:7],
        summed_win,
        summed_wout,
        summed_gu_a,
        summed_dn_a,
        summed_qkv[:, :query_cols],
        summed_qkv[:, query_cols:].reshape(rows, 2, kv_cols),
        summed_attn,
        summed_gu_b,
        summed_dn_b,
    )


def solution(mesh):
    return jax.shard_map(
        per_device,
        mesh=mesh,
        in_specs=(
            P("dp", "tensor", None),
            P("dp", None),
            P(None, "dp"),
            P(None, "dp"),
            P("dp", None, "tensor"),
            P("tensor", "dp"),
            P("dp", None, "tensor"),
            P("tensor", "dp"),
            P("dp", "tensor"),
            P("dp", None, "tensor"),
            P("tensor", "dp"),
            P("dp", None, "tensor"),
            P("tensor", "dp"),
            P("dp", "tensor", None),
        ),
        out_specs=(
            P("dp", "tensor", None),
            P("dp", "tensor", None),
            P(None, "dp"),
            P(None, "dp"),
            P("dp", None, "tensor"),
            P("tensor", "dp"),
            P("dp", None, "tensor"),
            P("tensor", "dp"),
            P("dp", "tensor"),
            P("dp", None, "tensor"),
            P("tensor", "dp"),
            P("dp", None, "tensor"),
            P("tensor", "dp"),
        ),
        check_vma=False,
    )
```

time: 2730 us -> 1080 us (0.40)
  waiting for transfers between devices: 2160 us -> 434 us
  starting transfers between devices: 3.07 us -> 176 us
  blocking collectives: 81.2 us -> 0 us
  local copies, waits for them, and re-layouts: 43.3 us -> 93.5 us
  matrix products: 313 us -> 267 us
    reduce_scatter x17 -> x0, waiting for transfers between devices: 1360 us -> none  [the longest x1 286 us: per_device(): lax.psum_scatter(grad_gu_a, 'dp', scatter_dimension=0, tiled=True)]
    all_gather x17 -> x0, waiting for transfers between devices: 656 us -> none  [the longest x1 127 us: per_device(): lax.all_gather(gate_up_a, 'dp', axis=0, tiled=True)]
    ppermute x0 -> x161, waiting for transfers between devices: none -> 434 us  [the longest x72 229 us: turn(): lax.ppermute(values, 'dp', [(i, (i + 4 * step) % n) for i in range(n)])]
    ppermute x0 -> x161, starting transfers between devices: none -> 176 us  [the longest x72 99.6 us: turn(): lax.ppermute(values, 'dp', [(i, (i + 4 * step) % n) for i in range(n)])]
    unnamed x38 -> x0, waiting for transfers between devices: 142 us -> none
    all_gather x2 -> x0, blocking collectives: 78.2 us -> none  [the longest x1 42.7 us: per_device(): lax.all_gather(gains, 'dp', axis=1, tiled=True)]
    dot_general x37 -> x64, matrix products: 307 us -> 263 us  [the longest x15 93.8 us: dot_nn(): return jnp.dot(a, w, preferred_element_type=F32)]
    unnamed x195 -> x396, local copies, waits for them, and re-layouts: 40.4 us -> 57.2 us
  transfers between devices with their start and end apart: 36 -> 161, of which waited for: 33 -> 65; matrix products, arithmetic and copies ran while one was open for 8% -> 36% of each run, Pallas kernels for 0% -> 0%
where the time goes in v1:
time: 1080 us; the launch traced here: 1070 us
  waiting for transfers between devices  434 us (40%)
  matrix products  267 us (25%)
  starting transfers between devices  176 us (16%)
  other arithmetic  99 us (9%)
  local copies, waits for them, and re-layouts  93.5 us (9%)
    ppermute x72, waiting for transfers between devices, turn(): lax.ppermute(values, 'dp', [(i, (i + 4 * step) % n) for i in range(n)])  229 us
    ppermute x72, waiting for transfers between devices, flip(): return lax.ppermute(values, 'dp', [(i, i ^ bit) for i in range(n)])  204 us
    ppermute x72, starting transfers between devices, turn(): lax.ppermute(values, 'dp', [(i, (i + 4 * step) % n) for i in range(n)])  99.6 us
    dot_general x15, matrix products, dot_nn(): return jnp.dot(a, w, preferred_element_type=F32)  93.8 us
    ppermute x72, starting transfers between devices, flip(): return lax.ppermute(values, 'dp', [(i, i ^ bit) for i in range(n)])  74 us
    dot_general x26, matrix products, dot_nt(): lax.dot_general(a, w, (((1,), (1,)), ((), ())), preferred_element_type=F32)  70.5 us
    dot_general x12, matrix products, dot_tn(): lax.dot_general(a, b, (((0,), (0,)), ((), ())), preferred_element_type=F32)  60.5 us
    unnamed x396, local copies, waits for them, and re-layouts  57.2 us
  transfers between devices with their start and end apart: 161, of which 65 were waited for; matrix products, arithmetic and copies ran while one was open for 36% of the time, Pallas kernels for 0%

profile of v1, /device:TPU:0, one launch (start us, length us, event | category | flops | bytes accessed | tf_op | source)
XLA Modules:
  0.0 1073.0 jit_solution(7089397113585141580)
XLA Ops:
  54.5 10.6 collective-permute-done.73
  129.7 12.4 %collective-permute-done.61 = bf16[64,2304]{1,0:T(8,128)(2,1)S(1)} collective-permute-done((bf16[64,2304]{1,0:T(8,128)(2,1)S(1)}, bf16[64,2304]{1,0:T(8,128)(2,1)S(1)}, u32[]{:S(2)}, u32[]{:S(2)}) %collective-permute-start.61) | collective-permute-done | bytes 294944 | tf_op jit(solution)/shard_map/ppermute | solution.py:23
  225.4 12.7 %collective-permute-done.31 = bf16[4,64,1152]{2,1,0:T(8,128)(2,1)S(1)} collective-permute-done((bf16[4,64,1152]{2,1,0:T(8,128)(2,1)S(1)}, bf16[4,64,1152]{2,1,0:T(8,128)(2,1)S(1)}, u32[]{:S(2)}, u32[]{:S(2)}) %collective-permute-start.31) | collective-permute-done | bytes 589856 | tf_op jit(solution)/shard_map/ppermute | solution.py:23
  253.0 25.7 %collective-permute-done.18 = bf16[256,2304]{1,0:T(8,128)(2,1)S(1)} collective-permute-done((bf16[256,2304]{1,0:T(8,128)(2,1)S(1)}, bf16[256,2304]{1,0:T(8,128)(2,1)S(1)}, u32[]{:S(2)}, u32[]{:S(2)}) %collective-permute-start.18) | collective-permute-done | bytes 1179680 | tf_op jit(solution)/shard_map/ppermute | solution.py:18
  284.4 24.1 %collective-permute-done.19 = bf16[256,2304]{1,0:T(8,128)(2,1)S(1)} collective-permute-done((bf16[256,2304]{1,0:T(8,128)(2,1)S(1)}, bf16[256,2304]{1,0:T(8,128)(2,1)S(1)}, u32[]{:S(2)}, u32[]{:S(2)}) %collective-permute-start.19) | collective-permute-done | bytes 1179680 | tf_op jit(solution)/shard_map/ppermute | solution.py:18
  308.7 24.8 %collective-permute-done.20 = bf16[256,2304]{1,0:T(8,128)(2,1)S(1)} collective-permute-done((bf16[256,2304]{1,0:T(8,128)(2,1)S(1)}, bf16[256,2304]{1,0:T(8,128)(2,1)S(1)}, u32[]{:S(2)}, u32[]{:S(2)}) %collective-permute-start.20) | collective-permute-done | bytes 1179680 | tf_op jit(solution)/shard_map/ppermute | solution.py:18
  340.8 8.3 fusion.245
  349.1 11.1 %multiply_convert_fusion.1 = (bf16[1024,2304]{1,0:T(8,128)(2,1)}, bf16[1024,2304]{1,0:T(8,128)(2,1)}) fusion(f32[1024,2304]{1,0:T(8,128)} %fusion.245, bf16[1024,2304]{1,0:T(8,128)(2,1)S(1)} %constant_dynamic-update-slice_fusion.14, bf16[512,1024]{1,0:T(8,128)(2,1)S(1)} %collective-permute-done.14, bf16[512,1024]{1,0:T(8,128)(2,1)S(1)} %multiply_convert_fusion.7), kind=kOutput, calls=%fused_computation.36 | convolution fusion | flops 4852547584 | bytes 25690112 | tf_op jit(solution)/shard_map/dot_general | solution.py:101
  370.0 11.3 %collective-permute-done.77 = bf16[256,1152]{1,0:T(8,128)(2,1)S(1)} collective-permute-done((bf16[256,1152]{1,0:T(8,128)(2,1)S(1)}, bf16[256,1152]{1,0:T(8,128)(2,1)S(1)}, u32[]{:S(2)}, u32[]{:S(2)}) %collective-permute-start.77) | collective-permute-done | bytes 589856 | tf_op jit(solution)/shard_map/ppermute | solution.py:18
  382.3 12.5 %collective-permute-done.70 = bf16[4,64,1152]{2,1,0:T(8,128)(2,1)S(1)} collective-permute-done((bf16[4,64,1152]{2,1,0:T(8,128)(2,1)S(1)}, bf16[4,64,1152]{2,1,0:T(8,128)(2,1)S(1)}, u32[]{:S(2)}, u32[]{:S(2)}) %collective-permute-start.70) | collective-permute-done | bytes 589856 | tf_op jit(solution)/shard_map/ppermute | solution.py:23
  401.8 18.6 %collective-permute-done.46 = bf16[256,1024]{1,0:T(8,128)(2,1)S(1)} collective-permute-done((bf16[256,1024]{1,0:T(8,128)(2,1)S(1)}, bf16[256,1024]{1,0:T(8,128)(2,1)S(1)}, u32[]{:S(2)}, u32[]{:S(2)}) %collective-permute-start.46) | collective-permute-done | bytes 524320 | tf_op jit(solution)/shard_map/ppermute | solution.py:18
  447.5 8.2 fusion.3
  480.9 8.2 fusion.243
  489.2 8.6 fusion.242
  497.8 23.0 %fusion.11 = (bf16[1024,2304]{1,0:T(8,128)(2,1)}, bf16[1024,2304]{1,0:T(8,128)(2,1)}, bf16[1024,2304]{1,0:T(8,128)(2,1)}) fusion(f32[1024,2304]{1,0:T(8,128)} %fusion.242, f32[1024,2304]{1,0:T(8,128)} %fusion.243, bf16[1024,1152]{1,0:T(8,128)(2,1)} %copy-done.130, bf16[1024,1152]{1,0:T(8,128)(2,1)} %bitcast.508, ...), kind=kOutput, calls=%fused_computation.23 | convolution fusion | flops 4899733504 | bytes 39845888 | tf_op jit(solution)/shard_map/dot_general | solution.py:101
  520.8 8.1 convolution_convert_fusion
  563.9 8.0 convolution_convert_fusion.1
  592.8 8.1 fusion.100
  609.0 12.1 %collective-permute-done.143 = bf16[256,2304]{1,0:T(8,128)(2,1)} collective-permute-done((bf16[256,2304]{1,0:T(8,128)(2,1)}, bf16[256,2304]{1,0:T(8,128)(2,1)}, u32[]{:S(2)}, u32[]{:S(2)}) %collective-permute-start.143) | collective-permute-done | bytes 1179680 | tf_op jit(solution)/shard_map/ppermute | solution.py:18
  624.9 11.1 %collective-permute-done.150 = bf16[4,64,1152]{2,1,0:T(8,128)(2,1)S(1)} collective-permute-done((bf16[4,64,1152]{2,1,0:T(8,128)(2,1)S(1)}, bf16[4,64,1152]{2,1,0:T(8,128)(2,1)S(1)}, u32[]{:S(2)}, u32[]{:S(2)}) %collective-permute-start.150) | collective-permute-done | bytes 589856 | tf_op jit(solution)/shard_map/ppermute | solution.py:23
  689.1 8.3 fusion.2
  732.7 10.9 %collective-permute-done.132 = bf16[4,64,512]{2,1,0:T(8,128)(2,1)S(1)} collective-permute-done((bf16[4,64,512]{2,1,0:T(8,128)(2,1)S(1)}, bf16[4,64,512]{2,1,0:T(8,128)(2,1)S(1)}, u32[]{:S(2)}, u32[]{:S(2)}) %collective-permute-start.132) | collective-permute-done | bytes 262176 | tf_op jit(solution)/shard_map/ppermute | solution.py:23
  760.9 9.2 collective-permute-done.148
  787.7 8.0 convolution_convert_fusion.3
  805.0 15.7 %fusion.20 = (bf16[1024,2304]{1,0:T(8,128)(2,1)}, bf16[1024,2304]{1,0:T(8,128)(2,1)}) fusion(bf16[1024,2304]{1,0:T(8,128)(2,1)} %get-tuple-element.210, f32[1024,2304]{1,0:T(8,128)} %fusion.245, bf16[1024,1152]{1,0:T(8,128)(2,1)} %copy-done.128, bf16[1024,1152]{1,0:T(8,128)(2,1)} %bitcast.507, bf16[512,1024]{1,0:T(8,128)(2,1)} %collective-permute-done.84, ...), kind=kOutput, calls=%fused_computation.32 | convolution fusion | flops 4883218432 | bytes 30408704 | tf_op jit(solution)/shard_map/dot_general | solution.py:101
  839.3 7.9 convolution_convert_fusion.4
  865.5 13.6 %collective-permute-done.114 = bf16[4,64,1152]{2,1,0:T(8,128)(2,1)S(1)} collective-permute-done((bf16[4,64,1152]{2,1,0:T(8,128)(2,1)S(1)}, bf16[4,64,1152]{2,1,0:T(8,128)(2,1)S(1)}, u32[]{:S(2)}, u32[]{:S(2)}) %collective-permute-start.114) | collective-permute-done | bytes 589856 | tf_op jit(solution)/shard_map/ppermute | solution.py:23
  882.3 18.4 %collective-permute-done.120 = bf16[256,1152]{1,0:T(8,128)(2,1)S(1)} collective-permute-done((bf16[256,1152]{1,0:T(8,128)(2,1)S(1)}, bf16[256,1152]{1,0:T(8,128)(2,1)S(1)}, u32[]{:S(2)}, u32[]{:S(2)}) %collective-permute-start.120) | collective-permute-done | bytes 589856 | tf_op jit(solution)/shard_map/ppermute | solution.py:18
  968.6 16.8 %collective-permute-done.96 = bf16[4,64,512]{2,1,0:T(8,128)(2,1)S(1)} collective-permute-done((bf16[4,64,512]{2,1,0:T(8,128)(2,1)S(1)}, bf16[4,64,512]{2,1,0:T(8,128)(2,1)S(1)}, u32[]{:S(2)}, u32[]{:S(2)}) %collective-permute-start.96) | collective-permute-done | bytes 262176 | tf_op jit(solution)/shard_map/ppermute | solution.py:23
  1007.3 13.7 %collective-permute-done.88 = bf16[256,1664]{0,1:T(8,128)(2,1)S(1)} collective-permute-done((bf16[256,1664]{0,1:T(8,128)(2,1)S(1)}, bf16[256,1664]{0,1:T(8,128)(2,1)S(1)}, u32[]{:S(2)}, u32[]{:S(2)}) %collective-permute-start.88) | collective-permute-done | bytes 852000 | tf_op jit(solution)/shard_map/ppermute | solution.py:18
  1026.3 10.7 %collective-permute-done.90 = bf16[256,1664]{0,1:T(8,128)(2,1)S(1)} collective-permute-done((bf16[256,1664]{0,1:T(8,128)(2,1)S(1)}, bf16[256,1664]{0,1:T(8,128)(2,1)S(1)}, u32[]{:S(2)}, u32[]{:S(2)}) %collective-permute-start.90) | collective-permute-done | bytes 852000 | tf_op jit(solution)/shard_map/ppermute | solution.py:18
  1042.9 10.2 collective-permute-done.91
  (959 shorter events, 657.4 us)
Async XLA Ops:
  4.1 61.8 %collective-permute-start = (bf16[64,1664]{1,0:T(8,128)(2,1)}, bf16[64,1664]{1,0:T(8,128)(2,1)}, u32[]{:S(2)}, u32[]{:S(2)}) collective-permute-start(bf16[64,1664]{1,0:T(8,128)(2,1)} %concatenate.137), channel_id=1, source_target_pairs={{0,24},{2,26},{4,28},{6,30},{8,0},{10,2},{12,4},{14,6},{16,8},{18,... | collective-permute-start | bytes 638984 | tf_op jit(solution)/shard_map/ppermute | solution.py:23
  9.1 141.4 %collective-permute-start.2 = (bf16[64,1664]{1,0:T(8,128)(2,1)}, bf16[64,1664]{1,0:T(8,128)(2,1)}, u32[]{:S(2)}, u32[]{:S(2)}) collective-permute-start(bf16[64,1664]{1,0:T(8,128)(2,1)} %concatenate.137), channel_id=1, source_target_pairs={{0,8},{2,10},{4,12},{6,14},{8,16},{10,18},{12,20},{14,22},{16,24},... | collective-permute-start | bytes 638984 | tf_op jit(solution)/shard_map/ppermute | solution.py:23
  49.0 107.6 %collective-permute-start.17 = (bf16[64,2304]{1,0:T(8,128)(2,1)}, bf16[64,2304]{1,0:T(8,128)(2,1)S(1)}, u32[]{:S(2)}, u32[]{:S(2)}) collective-permute-start(bf16[64,2304]{1,0:T(8,128)(2,1)} %get-tuple-element.84), channel_id=1, source_target_pairs={{0,8},{2,10},{4,12},{6,14},{8,16},{10,18},{12,20},{14,22},{16,24},... | collective-permute-start | bytes 884744 | tf_op jit(solution)/shard_map/ppermute | solution.py:23
  90.2 80.4 %collective-permute-start.23 = (bf16[64,2304]{1,0:T(8,128)(2,1)S(1)}, bf16[64,2304]{1,0:T(8,128)(2,1)S(1)}, u32[]{:S(2)}, u32[]{:S(2)}) collective-permute-start(bf16[64,2304]{1,0:T(8,128)(2,1)S(1)} %copy-done.66), channel_id=1, source_target_pairs={{0,8},{2,10},{4,12},{6,14},{8,16},{10,18},{12,20},{14,22},{16,24},... | collective-permute-start | bytes 884744 | tf_op jit(solution)/shard_map/ppermute | solution.py:23
  129.7 48.4 %collective-permute-start.57 = (bf16[64,2304]{1,0:T(8,128)(2,1)S(1)}, bf16[64,2304]{1,0:T(8,128)(2,1)S(1)}, u32[]{:S(2)}, u32[]{:S(2)}) collective-permute-start(bf16[64,2304]{1,0:T(8,128)(2,1)S(1)} %copy-done.64), channel_id=1, source_target_pairs={{0,8},{2,10},{4,12},{6,14},{8,16},{10,18},{12,20},{14,22},{16,24},... | collective-permute-start | bytes 884744 | tf_op jit(solution)/shard_map/ppermute | solution.py:23
  211.2 124.5 %collective-permute-start.50 = (bf16[4,64,512]{2,1,0:T(8,128)(2,1)S(1)}, bf16[4,64,512]{2,1,0:T(8,128)(2,1)S(1)}, u32[]{:S(2)}, u32[]{:S(2)}) collective-permute-start(bf16[4,64,512]{2,1,0:T(8,128)(2,1)S(1)} %get-tuple-element.182), channel_id=1, source_target_pairs={{0,24},{2,26},{4,28},{6,30},{8,0},{10,2},{12,4},{14,6},{16,8},{18,... | collective-permute-start | bytes 786440 | tf_op jit(solution)/shard_map/ppermute | solution.py:23
  225.3 139.4 %collective-permute-start.52 = (bf16[4,64,512]{2,1,0:T(8,128)(2,1)S(1)}, bf16[4,64,512]{2,1,0:T(8,128)(2,1)S(1)}, u32[]{:S(2)}, u32[]{:S(2)}) collective-permute-start(bf16[4,64,512]{2,1,0:T(8,128)(2,1)S(1)} %get-tuple-element.182), channel_id=1, source_target_pairs={{0,8},{2,10},{4,12},{6,14},{8,16},{10,18},{12,20},{14,22},{16,24},... | collective-permute-start | bytes 786440 | tf_op jit(solution)/shard_map/ppermute | solution.py:23
  281.0 52.4 %collective-permute-start.20 = (bf16[256,2304]{1,0:T(8,128)(2,1)S(1)}, bf16[256,2304]{1,0:T(8,128)(2,1)S(1)}, u32[]{:S(2)}, u32[]{:S(2)}) collective-permute-start(bf16[256,2304]{1,0:T(8,128)(2,1)S(1)} %collective-permute-done.18), channel_id=1, source_target_pairs={{0,4},{2,6},{4,0},{6,2},{8,12},{10,14},{12,8},{14,10},{16,20},{18,... | collective-permute-start | bytes 3538952 | tf_op jit(solution)/shard_map/ppermute | solution.py:18
  282.1 52.5 %collective-permute-start.26 = (bf16[256,2304]{1,0:T(8,128)(2,1)S(1)}, bf16[256,2304]{1,0:T(8,128)(2,1)S(1)}, u32[]{:S(2)}, u32[]{:S(2)}) collective-permute-start(bf16[256,2304]{1,0:T(8,128)(2,1)S(1)} %collective-permute-done.25), channel_id=1, source_target_pairs={{0,2},{2,0},{4,6},{6,4},{8,10},{10,8},{12,14},{14,12},{16,18},{18,... | collective-permute-start | bytes 3538952 | tf_op jit(solution)/shard_map/ppermute | solution.py:18
  368.9 55.2 %collective-permute-start.58 = (bf16[256,2304]{1,0:T(8,128)(2,1)}, bf16[256,2304]{1,0:T(8,128)(2,1)}, u32[]{:S(2)}, u32[]{:S(2)}) collective-permute-start(bf16[256,2304]{1,0:T(8,128)(2,1)} %pad_maximum_fusion.33), channel_id=1, source_target_pairs={{0,2},{2,0},{4,6},{6,4},{8,10},{10,8},{12,14},{14,12},{16,18},{18,... | collective-permute-start | bytes 3538952 | tf_op jit(solution)/shard_map/ppermute | solution.py:18
  381.3 46.2 %collective-permute-start.65 = (bf16[256,2304]{1,0:T(8,128)(2,1)}, bf16[256,2304]{1,0:T(8,128)(2,1)}, u32[]{:S(2)}, u32[]{:S(2)}) collective-permute-start(bf16[256,2304]{1,0:T(8,128)(2,1)} %pad_maximum_fusion.34), channel_id=1, source_target_pairs={{0,4},{2,6},{4,0},{6,2},{8,12},{10,14},{12,8},{14,10},{16,20},{18,... | collective-permute-start | bytes 3538952 | tf_op jit(solution)/shard_map/ppermute | solution.py:18
  420.5 77.3 %collective-permute-start.80 = (bf16[512,1024]{1,0:T(8,128)(2,1)}, bf16[512,1024]{1,0:T(8,128)(2,1)}, u32[]{:S(2)}, u32[]{:S(2)}) collective-permute-start(bf16[512,1024]{1,0:T(8,128)(2,1)} %get-tuple-element.219), channel_id=1, source_target_pairs={{0,1},{1,0},{2,3},{3,2},{4,5},{5,4},{6,7},{7,6},{8,9},{9,8},{10,11... | collective-permute-start | bytes 3145736 | tf_op jit(solution)/shard_map/ppermute | solution.py:27
  423.1 45.9 %collective-permute-start.59 = (bf16[256,2304]{1,0:T(8,128)(2,1)}, bf16[256,2304]{1,0:T(8,128)(2,1)}, u32[]{:S(2)}, u32[]{:S(2)}) collective-permute-start(bf16[256,2304]{1,0:T(8,128)(2,1)} %pad_maximum_fusion.33), channel_id=1, source_target_pairs={{0,4},{2,6},{4,0},{6,2},{8,12},{10,14},{12,8},{14,10},{16,20},{18,... | collective-permute-start | bytes 3538952 | tf_op jit(solution)/shard_map/ppermute | solution.py:18
  427.5 49.0 %collective-permute-start.60 = (bf16[256,2304]{1,0:T(8,128)(2,1)}, bf16[256,2304]{1,0:T(8,128)(2,1)}, u32[]{:S(2)}, u32[]{:S(2)}) collective-permute-start(bf16[256,2304]{1,0:T(8,128)(2,1)} %collective-permute-done.58), channel_id=1, source_target_pairs={{0,4},{2,6},{4,0},{6,2},{8,12},{10,14},{12,8},{14,10},{16,20},{18,... | collective-permute-start | bytes 3538952 | tf_op jit(solution)/shard_map/ppermute | solution.py:18
  428.5 49.4 %collective-permute-start.66 = (bf16[256,2304]{1,0:T(8,128)(2,1)}, bf16[256,2304]{1,0:T(8,128)(2,1)}, u32[]{:S(2)}, u32[]{:S(2)}) collective-permute-start(bf16[256,2304]{1,0:T(8,128)(2,1)} %collective-permute-done.65), channel_id=1, source_target_pairs={{0,2},{2,0},{4,6},{6,4},{8,10},{10,8},{12,14},{14,12},{16,18},{18,... | collective-permute-start | bytes 3538952 | tf_op jit(solution)/shard_map/ppermute | solution.py:18
  537.6 46.6 %collective-permute-start.149 = (bf16[4,64,1152]{2,1,0:T(8,128)(2,1)S(1)}, bf16[4,64,1152]{2,1,0:T(8,128)(2,1)S(1)}, u32[]{:S(2)}, u32[]{:S(2)}) collective-permute-start(bf16[4,64,1152]{2,1,0:T(8,128)(2,1)S(1)} %get-tuple-element.108), channel_id=1, source_target_pairs={{0,8},{2,10},{4,12},{6,14},{8,16},{10,18},{12,20},{14,22},{16,24},... | collective-permute-start | bytes 1769480 | tf_op jit(solution)/shard_map/ppermute | solution.py:23
  537.6 86.4 %collective-permute-start.151 = (bf16[4,64,1152]{2,1,0:T(8,128)(2,1)}, bf16[4,64,1152]{2,1,0:T(8,128)(2,1)}, u32[]{:S(2)}, u32[]{:S(2)}) collective-permute-start(bf16[4,64,1152]{2,1,0:T(8,128)(2,1)} %get-tuple-element.109), channel_id=1, source_target_pairs={{0,24},{2,26},{4,28},{6,30},{8,0},{10,2},{12,4},{14,6},{16,8},{18,... | collective-permute-start | bytes 1769480 | tf_op jit(solution)/shard_map/ppermute | solution.py:23
  541.6 43.7 %collective-permute-start.155 = (bf16[256,1152]{1,0:T(8,128)(2,1)S(1)}, bf16[256,1152]{1,0:T(8,128)(2,1)S(1)}, u32[]{:S(2)}, u32[]{:S(2)}) collective-permute-start(bf16[256,1152]{1,0:T(8,128)(2,1)S(1)} %get-tuple-element.94), channel_id=1, source_target_pairs={{0,2},{2,0},{4,6},{6,4},{8,10},{10,8},{12,14},{14,12},{16,18},{18,... | collective-permute-start | bytes 1769480 | tf_op jit(solution)/shard_map/ppermute | solution.py:18
  542.4 95.1 %collective-permute-start.157 = (bf16[256,1152]{1,0:T(8,128)(2,1)}, bf16[256,1152]{1,0:T(8,128)(2,1)}, u32[]{:S(2)}, u32[]{:S(2)}) collective-permute-start(bf16[256,1152]{1,0:T(8,128)(2,1)} %get-tuple-element.95), channel_id=1, source_target_pairs={{0,2},{2,0},{4,6},{6,4},{8,10},{10,8},{12,14},{14,12},{16,18},{18,... | collective-permute-start | bytes 1769480 | tf_op jit(solution)/shard_map/ppermute | solution.py:18
  558.7 46.2 %collective-permute-start.137 = (bf16[256,2304]{1,0:T(8,128)(2,1)}, bf16[256,2304]{1,0:T(8,128)(2,1)}, u32[]{:S(2)}, u32[]{:S(2)}) collective-permute-start(bf16[256,2304]{1,0:T(8,128)(2,1)} %get-tuple-element.96), channel_id=1, source_target_pairs={{0,4},{2,6},{4,0},{6,2},{8,12},{10,14},{12,8},{14,10},{16,20},{18,... | collective-permute-start | bytes 3538952 | tf_op jit(solution)/shard_map/ppermute | solution.py:18
  586.9 129.7 %collective-permute-start.139 = (bf16[256,2304]{1,0:T(8,128)(2,1)}, bf16[256,2304]{1,0:T(8,128)(2,1)}, u32[]{:S(2)}, u32[]{:S(2)}) collective-permute-start(bf16[256,2304]{1,0:T(8,128)(2,1)} %get-tuple-element.97), channel_id=1, source_target_pairs={{0,4},{2,6},{4,0},{6,2},{8,12},{10,14},{12,8},{14,10},{16,20},{18,... | collective-permute-start | bytes 3538952 | tf_op jit(solution)/shard_map/ppermute | solution.py:18
  604.9 121.1 %collective-permute-start.145 = (bf16[256,2304]{1,0:T(8,128)(2,1)}, bf16[256,2304]{1,0:T(8,128)(2,1)}, u32[]{:S(2)}, u32[]{:S(2)}) collective-permute-start(bf16[256,2304]{1,0:T(8,128)(2,1)} %get-tuple-element.99), channel_id=1, source_target_pairs={{0,2},{2,0},{4,6},{6,4},{8,10},{10,8},{12,14},{14,12},{16,18},{18,... | collective-permute-start | bytes 3538952 | tf_op jit(solution)/shard_map/ppermute | solution.py:18
  657.3 63.1 %collective-permute-start.138 = (bf16[256,2304]{1,0:T(8,128)(2,1)}, bf16[256,2304]{1,0:T(8,128)(2,1)}, u32[]{:S(2)}, u32[]{:S(2)}) collective-permute-start(bf16[256,2304]{1,0:T(8,128)(2,1)} %add_convert_fusion.3), channel_id=1, source_target_pairs={{0,2},{2,0},{4,6},{6,4},{8,10},{10,8},{12,14},{14,12},{16,18},{18,... | collective-permute-start | bytes 3538952 | tf_op jit(solution)/shard_map/ppermute | solution.py:18
  664.0 62.1 %collective-permute-start.144 = (bf16[256,2304]{1,0:T(8,128)(2,1)}, bf16[256,2304]{1,0:T(8,128)(2,1)}, u32[]{:S(2)}, u32[]{:S(2)}) collective-permute-start(bf16[256,2304]{1,0:T(8,128)(2,1)} %add_convert_fusion.1), channel_id=1, source_target_pairs={{0,4},{2,6},{4,0},{6,2},{8,12},{10,14},{12,8},{14,10},{16,20},{18,... | collective-permute-start | bytes 3538952 | tf_op jit(solution)/shard_map/ppermute | solution.py:18
  724.2 47.9 %collective-permute-start.127 = (bf16[256,1024]{1,0:T(8,128)(2,1)S(1)}, bf16[256,1024]{1,0:T(8,128)(2,1)S(1)}, u32[]{:S(2)}, u32[]{:S(2)}) collective-permute-start(bf16[256,1024]{1,0:T(8,128)(2,1)S(1)} %get-tuple-element.117), channel_id=1, source_target_pairs={{0,4},{2,6},{4,0},{6,2},{8,12},{10,14},{12,8},{14,10},{16,20},{18,... | collective-permute-start | bytes 1572872 | tf_op jit(solution)/shard_map/ppermute | solution.py:18
  799.2 60.0 %collective-permute-start.113 = (bf16[4,64,1152]{2,1,0:T(8,128)(2,1)S(1)}, bf16[4,64,1152]{2,1,0:T(8,128)(2,1)S(1)}, u32[]{:S(2)}, u32[]{:S(2)}) collective-permute-start(bf16[4,64,1152]{2,1,0:T(8,128)(2,1)S(1)} %get-tuple-element.110), channel_id=1, source_target_pairs={{0,8},{2,10},{4,12},{6,14},{8,16},{10,18},{12,20},{14,22},{16,24},... | collective-permute-start | bytes 1769480 | tf_op jit(solution)/shard_map/ppermute | solution.py:23
  799.6 65.1 %collective-permute-start.115 = (bf16[4,64,1152]{2,1,0:T(8,128)(2,1)}, bf16[4,64,1152]{2,1,0:T(8,128)(2,1)}, u32[]{:S(2)}, u32[]{:S(2)}) collective-permute-start(bf16[4,64,1152]{2,1,0:T(8,128)(2,1)} %get-tuple-element.111), channel_id=1, source_target_pairs={{0,24},{2,26},{4,28},{6,30},{8,0},{10,2},{12,4},{14,6},{16,8},{18,... | collective-permute-start | bytes 1769480 | tf_op jit(solution)/shard_map/ppermute | solution.py:23
  803.0 56.5 %collective-permute-start.119 = (bf16[256,1152]{1,0:T(8,128)(2,1)}, bf16[256,1152]{1,0:T(8,128)(2,1)S(1)}, u32[]{:S(2)}, u32[]{:S(2)}) collective-permute-start(bf16[256,1152]{1,0:T(8,128)(2,1)} %get-tuple-element.100), channel_id=1, source_target_pairs={{0,2},{2,0},{4,6},{6,4},{8,10},{10,8},{12,14},{14,12},{16,18},{18,... | collective-permute-start | bytes 1769480 | tf_op jit(solution)/shard_map/ppermute | solution.py:18
  804.0 77.4 %collective-permute-start.121 = (bf16[256,1152]{1,0:T(8,128)(2,1)}, bf16[256,1152]{1,0:T(8,128)(2,1)}, u32[]{:S(2)}, u32[]{:S(2)}) collective-permute-start(bf16[256,1152]{1,0:T(8,128)(2,1)} %get-tuple-element.101), channel_id=1, source_target_pairs={{0,2},{2,0},{4,6},{6,4},{8,10},{10,8},{12,14},{14,12},{16,18},{18,... | collective-permute-start | bytes 1769480 | tf_op jit(solution)/shard_map/ppermute | solution.py:18
  835.4 66.9 %collective-permute-start.101 = (bf16[256,2304]{1,0:T(8,128)(2,1)S(1)}, bf16[256,2304]{1,0:T(8,128)(2,1)S(1)}, u32[]{:S(2)}, u32[]{:S(2)}) collective-permute-start(bf16[256,2304]{1,0:T(8,128)(2,1)S(1)} %get-tuple-element.102), channel_id=1, source_target_pairs={{0,4},{2,6},{4,0},{6,2},{8,12},{10,14},{12,8},{14,10},{16,20},{18,... | collective-permute-start | bytes 3538952 | tf_op jit(solution)/shard_map/ppermute | solution.py:18
  859.5 95.5 %collective-permute-start.103 = (bf16[256,2304]{1,0:T(8,128)(2,1)}, bf16[256,2304]{1,0:T(8,128)(2,1)}, u32[]{:S(2)}, u32[]{:S(2)}) collective-permute-start(bf16[256,2304]{1,0:T(8,128)(2,1)} %get-tuple-element.103), channel_id=1, source_target_pairs={{0,4},{2,6},{4,0},{6,2},{8,12},{10,14},{12,8},{14,10},{16,20},{18,... | collective-permute-start | bytes 3538952 | tf_op jit(solution)/shard_map/ppermute | solution.py:18
  881.4 80.5 %collective-permute-start.109 = (bf16[256,2304]{1,0:T(8,128)(2,1)}, bf16[256,2304]{1,0:T(8,128)(2,1)S(1)}, u32[]{:S(2)}, u32[]{:S(2)}) collective-permute-start(bf16[256,2304]{1,0:T(8,128)(2,1)} %get-tuple-element.105), channel_id=1, source_target_pairs={{0,2},{2,0},{4,6},{6,4},{8,10},{10,8},{12,14},{14,12},{16,18},{18,... | collective-permute-start | bytes 3538952 | tf_op jit(solution)/shard_map/ppermute | solution.py:18
  (302 other events, 6418.8 us)

commit v2 on v1

v2 whole, which is shorter than its diff:
```python
import functools
import math

import jax
import jax.numpy as jnp
from jax import lax
from jax.experimental import pallas as pl
from jax.experimental.pallas import tpu as pltpu
from jax.sharding import PartitionSpec as P

HD = 64
EPS = 1e-05
THETA = 1000000.0
SCALE = 0.125
BF = jnp.bfloat16
F32 = jnp.float32


def ring():
    count = lax.axis_size("dp") // 2
    return [0] + list(range(1, count, 2)) + list(range(count - 2, 0, -2))


def ring_groups():
    return [[2 * k + x for k in ring()] for x in range(2)]


def swap(values):
    return lax.ppermute(values, "tensor", [(0, 1), (1, 0)])


def flip_x(values):
    n = lax.axis_size("dp")
    return lax.ppermute(values, "dp", [(i, i ^ 1) for i in range(n)])


def by_x(mine, theirs, axis):
    x_bit = lax.axis_index("dp") % 2
    return jnp.concatenate(
        [jnp.where(x_bit == 0, mine, theirs), jnp.where(x_bit == 0, theirs, mine)], axis=axis
    )


def halves(values, axis):
    x_bit = lax.axis_index("dp") % 2
    left, right = jnp.split(values, 2, axis=axis)
    return jnp.where(x_bit == 0, left, right), jnp.where(x_bit == 0, right, left)


def ring_gather(pair):
    return lax.all_gather(pair, "dp", axis=0, axis_index_groups=ring_groups(), tiled=True)


def ring_sum(grad):
    return lax.psum_scatter(
        grad, "dp", scatter_dimension=0, axis_index_groups=ring_groups(), tiled=True
    )


def ring_order(values, axis, back=False):
    order = ring()
    if back:
        order = [order.index(k) for k in range(len(order))]
    size = values.shape[axis] // len(order)
    return jnp.concatenate(
        [lax.slice_in_dim(values, k * size, (k + 1) * size, axis=axis) for k in order], axis=axis
    )


def dot_nn(a, w):
    return jnp.dot(a, w, preferred_element_type=F32)


def dot_nt(a, w):
    return lax.dot_general(a, w, (((1,), (1,)), ((), ())), preferred_element_type=F32)


def dot_tn(a, b):
    return lax.dot_general(a, b, (((0,), (0,)), ((), ())), preferred_element_type=F32)


def params(steps=1):
    return pltpu.CompilerParams(
        vmem_limit_bytes=48 * 2**20, dimension_semantics=("arbitrary",) * steps
    )


def whole(array):
    return pl.BlockSpec(array.shape, lambda *_: (0, 0), pipeline_mode=pl.Buffered(1))


def column(array, cols, at):
    return pl.BlockSpec((array.shape[0], cols), lambda *_: (0, at), pipeline_mode=pl.Buffered(1))


def cost(flops, *arrays):
    return pl.CostEstimate(
        flops=flops,
        bytes_accessed=sum(a.size * a.dtype.itemsize for a in arrays),
        transcendentals=0,
    )


def ff_up_kernel(h0, h1, wg, wu, gate_ref, up_ref, product_ref):
    i = pl.program_id(0)

    def step(h):
        gate = jnp.dot(h[...], wg[...], preferred_element_type=F32)
        up = jnp.dot(h[...], wu[...], preferred_element_type=F32)
        gate_ref[...] = gate.astype(BF)
        up_ref[...] = up.astype(BF)
        product_ref[...] = (gate / (1.0 + jnp.exp(-gate)) * up).astype(BF)

    pl.when(i == 0)(lambda: step(h0))
    pl.when(i == 1)(lambda: step(h1))


def ff_up(h0, h1, weights, cols):
    rows, depth = h0.shape
    out = jax.ShapeDtypeStruct((2 * rows, cols), BF)
    tile = pl.BlockSpec((rows, cols), lambda i: (i, 0))
    return pl.pallas_call(
        ff_up_kernel,
        grid=(2,),
        out_shape=(out, out, out),
        in_specs=[whole(h0), whole(h1), column(weights, cols, 0), column(weights, cols, 1)],
        out_specs=(tile, tile, tile),
        compiler_params=params(),
        cost_estimate=cost(8 * rows * depth * cols, h0, h1, out, out, out, out, out),
    )(h0, h1, weights, weights)


def ff_back_kernel(e0, e1, wd, gate_ref, up_ref, dgate_ref, dup_ref):
    i = pl.program_id(0)

    def step(e):
        da = jnp.dot(e[...], wd[...], preferred_element_type=F32)
        gate = gate_ref[...].astype(F32)
        up = up_ref[...].astype(F32)
        sig = 1.0 / (1.0 + jnp.exp(-gate))
        lit = gate * sig
        dup_ref[...] = (da * lit).astype(BF)
        dgate_ref[...] = (da * up * (sig + lit - lit * sig)).astype(BF)

    pl.when(i == 0)(lambda: step(e0))
    pl.when(i == 1)(lambda: step(e1))


def ff_back(e0, e1, weights, gate, up):
    rows, depth = e0.shape
    cols = gate.shape[1]
    out = jax.ShapeDtypeStruct((2 * rows, cols), BF)
    tile = pl.BlockSpec((rows, cols), lambda i: (i, 0))
    return pl.pallas_call(
        ff_back_kernel,
        grid=(2,),
        out_shape=(out, out),
        in_specs=[whole(e0), whole(e1), column(weights, cols, 2), tile, tile],
        out_specs=(tile, tile),
        compiler_params=params(),
        cost_estimate=cost(4 * rows * depth * cols, e0, e1, gate, gate, up, out, out),
    )(e0, e1, weights, gate, up)


def weight_grad_kernel(*refs):
    left, right, out_ref = refs[:4], refs[4:-1], refs[-1]
    rows = left[0].shape[0]
    cols = right[0].shape[1]
    turned = [l[...].T for l in left]
    for k in range(len(right) // 2):
        near, far = right[2 * k], right[2 * k + 1]
        total = jnp.dot(turned[0], near[:rows], preferred_element_type=F32)
        total += jnp.dot(turned[1], near[rows:], preferred_element_type=F32)
        total += jnp.dot(turned[2], far[:rows], preferred_element_type=F32)
        total += jnp.dot(turned[3], far[rows:], preferred_element_type=F32)
        out_ref[:, k * cols : (k + 1) * cols] = total.astype(BF)


def weight_grad(left, right):
    rows, depth = left[0].shape
    tile = 256
    cols = right[0][0].shape[1] * len(right)
    flat = [r for pair in right for r in pair]
    out = jax.ShapeDtypeStruct((depth, cols), BF)
    return pl.pallas_call(
        weight_grad_kernel,
        grid=(depth // tile,),
        out_shape=out,
        in_specs=[pl.BlockSpec((rows, tile), lambda i: (0, i))] * 4 + [whole(r) for r in flat],
        out_specs=pl.BlockSpec((tile, cols), lambda i: (i, 0)),
        compiler_params=params(),
        cost_estimate=cost(8 * rows * depth * cols, *left, *flat, out),
    )(*left, *flat)


def narrow_kernel(n, *refs):
    left, right, keep_ref, send_ref = refs[:n], refs[n : 2 * n], refs[2 * n], refs[2 * n + 1]
    rows = keep_ref.shape[0]

    def total(part):
        t = None
        for l, r in zip(left, right):
            v = lax.dot_general(l[part], r[...], (((1,), (1,)), ((), ())), preferred_element_type=F32)
            t = v if t is None else t + v
        return t

    send_ref[...] = total(pl.ds(rows, rows)).astype(BF)
    keep_ref[...] = total(pl.ds(0, rows))


def narrow(left, weights, places):
    rows, cols = left[0].shape
    depth = weights.shape[0]
    n = len(left)
    tile = 256
    keep = jax.ShapeDtypeStruct((rows // 2, depth), F32)
    send = jax.ShapeDtypeStruct((rows // 2, depth), BF)
    out = pl.BlockSpec((rows // 2, tile), lambda i: (0, i))
    parts = [pl.BlockSpec((tile, cols), functools.partial(lambda at, i: (i, at), p)) for p in places]
    return pl.pallas_call(
        functools.partial(narrow_kernel, n),
        grid=(depth // tile,),
        out_shape=(keep, send),
        in_specs=[whole(l) for l in left] + parts,
        out_specs=(out, out),
        compiler_params=params(),
        cost_estimate=cost(2 * rows * depth * cols * n, *left, *left, keep, send),
    )(*left, *[weights] * n)


def turn_heads(values, cosine, sine):
    half = HD // 2
    first, second = values[:half], values[half:]
    return jnp.concatenate([first * cosine - second * sine, second * cosine + first * sine], axis=0)


def allowed_keys(start_ref, begin, stop):
    shape = (stop, stop - begin)
    key = lax.broadcasted_iota(jnp.int32, shape, 0)
    query = begin + lax.broadcasted_iota(jnp.int32, shape, 1)
    return (key <= query) & (key >= start_ref[:, begin:stop])


def attend_kernel(block, start_ref, cos_ref, sin_ref, q_ref, k_ref, v_ref, qr_ref, kr_ref, vr_ref, o_ref, log_ref):
    length = q_ref.shape[1]
    cosine, sine = cos_ref[...], sin_ref[...]
    keys = turn_heads(k_ref[...], cosine, sine).astype(BF)
    values = v_ref[...].astype(BF)
    kr_ref[...] = keys
    vr_ref[...] = values
    keys_down = keys.T
    for g in range(q_ref.shape[0] // HD):
        head = slice(g * HD, (g + 1) * HD)
        query = turn_heads(q_ref[head, :], cosine, sine).astype(BF) * jnp.asarray(SCALE, BF)
        qr_ref[head, :] = query
        for begin in range(0, length, block):
            stop = begin + block
            scores = jnp.dot(keys_down[:stop], query[:, begin:stop], preferred_element_type=F32)
            scores = jnp.where(allowed_keys(start_ref, begin, stop), scores, -1e30)
            top = jnp.max(scores, axis=0, keepdims=True)
            lifted = jnp.exp(scores - top)
            total = jnp.sum(lifted, axis=0, keepdims=True)
            probs = (lifted * (1.0 / total)).astype(BF)
            out = jnp.dot(values[:, :stop], probs, preferred_element_type=F32)
            o_ref[head, begin:stop] = out.astype(BF)
            log_ref[0, g : g + 1, begin:stop] = top + jnp.log(total)


def attend(start, cosine, sine, qkv, query_rows, kv_rows):
    length = qkv.shape[1]
    heads = kv_rows // HD
    group = query_rows // heads
    q_spec = pl.BlockSpec((group, length), lambda h: (h, 0))
    out_spec = pl.BlockSpec((HD, length), lambda h: (h, 0))
    k_at, v_at = query_rows // HD, (query_rows + kv_rows) // HD
    q_out = jax.ShapeDtypeStruct((query_rows, length), BF)
    kv_out = jax.ShapeDtypeStruct((kv_rows, length), BF)
    return pl.pallas_call(
        functools.partial(attend_kernel, min(256, length)),
        grid=(heads,),
        out_shape=(q_out, kv_out, kv_out, q_out, jax.ShapeDtypeStruct((heads, group // HD, length), F32)),
        in_specs=[
            whole(start),
            whole(cosine),
            whole(sine),
            q_spec,
            pl.BlockSpec((HD, length), lambda h: (k_at + h, 0)),
            pl.BlockSpec((HD, length), lambda h: (v_at + h, 0)),
        ],
        out_specs=(
            q_spec,
            out_spec,
            out_spec,
            q_spec,
            pl.BlockSpec((1, group // HD, length), lambda h: (h, 0, 0)),
        ),
        compiler_params=params(),
        cost_estimate=cost(2 * query_rows * length * length, qkv, qkv),
    )(start, cosine, sine, qkv, qkv, qkv)


def attend_back_kernel(
    block, start_ref, cos_ref, sin_ref, q_ref, k_ref, v_ref, log_ref, do_ref, dq_ref, dk_ref, dv_ref, dk_sum, dv_sum
):
    length = q_ref.shape[1]
    cosine, sine = cos_ref[...], sin_ref[...]
    keys = k_ref[...]
    keys_down = keys.T
    values_down = v_ref[...].T
    dk_sum[...] = jnp.zeros_like(dk_sum)
    dv_sum[...] = jnp.zeros_like(dv_sum)
    over_rows = (((1,), (1,)), ((), ()))
    for g in range(q_ref.shape[0] // HD):
        head = slice(g * HD, (g + 1) * HD)
        parts = []
        for begin in range(0, length, block):
            stop = begin + block
            query = q_ref[head, begin:stop]
            grad = do_ref[head, begin:stop]
            scores = jnp.dot(keys_down[:stop], query, preferred_element_type=F32)
            scores = jnp.where(allowed_keys(start_ref, begin, stop), scores, -1e30)
            probs = jnp.exp(scores - log_ref[0, g : g + 1, begin:stop])
            grad_probs = jnp.dot(values_down[:stop], grad, preferred_element_type=F32)
            inner = jnp.sum(probs * grad_probs, axis=0, keepdims=True)
            grad_scores = (probs * (grad_probs - inner)).astype(BF)
            parts.append(jnp.dot(keys[:, :stop], grad_scores, preferred_element_type=F32))
            dk_sum[:, :stop] += lax.dot_general(query, grad_scores, over_rows, preferred_element_type=F32)
            dv_sum[:, :stop] += lax.dot_general(grad, probs.astype(BF), over_rows, preferred_element_type=F32)
        whole_head = SCALE * jnp.concatenate(parts, axis=1)
        dq_ref[head, :] = turn_heads(whole_head, cosine, -sine).astype(BF)
    dk_ref[...] = turn_heads(dk_sum[...], cosine, -sine).astype(BF)
    dv_ref[...] = dv_sum[...].astype(BF)


def attend_back(start, cosine, sine, query, keys, values, logs, grad):
    query_rows, length = query.shape
    kv_rows = keys.shape[0]
    heads = kv_rows // HD
    group = query_rows // heads
    q_spec = pl.BlockSpec((group, length), lambda h: (h, 0))
    kv_spec = pl.BlockSpec((HD, length), lambda h: (h, 0))
    q_out = jax.ShapeDtypeStruct((query_rows, length), BF)
    kv_out = jax.ShapeDtypeStruct((kv_rows, length), BF)
    return pl.pallas_call(
        functools.partial(attend_back_kernel, min(256, length)),
        grid=(heads,),
        out_shape=(q_out, kv_out, kv_out),
        in_specs=[
            whole(start),
            whole(cosine),
            whole(sine),
            q_spec,
            kv_spec,
            kv_spec,
            pl.BlockSpec((1, group // HD, length), lambda h: (h, 0, 0)),
            q_spec,
        ],
        out_specs=(q_spec, kv_spec, kv_spec),
        scratch_shapes=[pltpu.VMEM((HD, length), F32), pltpu.VMEM((HD, length), F32)],
        compiler_params=params(),
        cost_estimate=cost(6 * query_rows * length * length, query, query, grad, grad),
    )(start, cosine, sine, query, keys, values, logs, grad)


def second_grads_kernel(count, *refs):
    left0, left1, rights, out_ref = refs[0], refs[1], refs[2:-1], refs[-1]
    over_rows = (((1,), (1,)), ((), ()))
    turned = left0[...].T, left1[...].T
    at = 0
    for k, right in enumerate(rights):
        got = lax.dot_general(turned[k >= count], right[...], over_rows, preferred_element_type=F32)
        out_ref[:, at : at + got.shape[1]] = got.astype(BF)
        at += got.shape[1]


def second_grads(left0, rights0, left1, right1):
    length, depth = left0.shape
    tile = 256
    rights = [*rights0, right1]
    cols = sum(r.shape[0] for r in rights)
    out = jax.ShapeDtypeStruct((depth, cols), BF)
    left = pl.BlockSpec((length, tile), lambda i: (0, i))
    return pl.pallas_call(
        functools.partial(second_grads_kernel, len(rights0)),
        grid=(depth // tile,),
        out_shape=out,
        in_specs=[left, left] + [whole(r) for r in rights],
        out_specs=pl.BlockSpec((tile, cols), lambda i: (i, 0)),
        compiler_params=params(),
        cost_estimate=cost(2 * length * depth * cols, left0, left1, *rights, out),
    )(left0, left1, *rights)


def first_grads_kernel(left0, left1, g0, g1, g2, low, small, out_ref):
    cols = g0.shape[1]
    turned = left0[...].T
    for k, right in enumerate((g0, g1, g2)):
        got = jnp.dot(turned, right[...], preferred_element_type=F32)
        out_ref[:, k * cols : (k + 1) * cols] = got.astype(BF)
    got = jnp.dot(left1[...].T, low[...], preferred_element_type=F32)
    out_ref[:, 3 * cols : 4 * cols] = got.astype(BF)
    out_ref[:, 4 * cols :] = small[...]


def first_grads(left0, rights, left1, low, small):
    length, depth = left0.shape
    tile = 256
    cols = low.shape[1]
    width = 4 * cols + small.shape[1]
    out = jax.ShapeDtypeStruct((depth, width), BF)
    left = pl.BlockSpec((length, tile), lambda i: (0, i))
    return pl.pallas_call(
        first_grads_kernel,
        grid=(depth // tile,),
        out_shape=out,
        in_specs=[left, left]
        + [whole(r) for r in (*rights, low)]
        + [pl.BlockSpec((tile, small.shape[1]), lambda i: (i, 0))],
        out_specs=pl.BlockSpec((tile, width), lambda i: (i, 0)),
        compiler_params=params(),
        cost_estimate=cost(8 * length * depth * cols, left0, left1, *rights, low, out),
    )(left0, left1, *rights, low, small)


def inv_rms(values):
    return lax.rsqrt(jnp.mean(values * values, axis=-1, keepdims=True) + EPS)


def norm_low(values, gain):
    return (values * inv_rms(values) * gain).astype(BF)


def norm_back(grad_normed, values, gain, grad_out):
    q = inv_rms(values)
    grad_gain = jnp.sum(grad_normed * values * q, axis=0)
    a2 = grad_normed * gain
    inner = jnp.mean(a2 * values, axis=-1, keepdims=True)
    return grad_out + q * a2 - values * (q * q * q * inner), grad_gain


def rope_tables(positions):
    half = HD // 2
    freq = jnp.exp(jnp.arange(half, dtype=F32) * (-2.0 * math.log(THETA) / (2 * half)))
    angle = freq[:, None] * positions[None, :]
    return jnp.cos(angle), jnp.sin(angle)


def conv_mix(mixed, kernel, same_one, same_two):
    driven = mixed[0] * mixed[2]
    zero = jnp.zeros((2, driven.shape[1]), driven.dtype)
    back_one = jnp.concatenate([zero[:1], driven[:-1]], axis=0) * same_one
    back_two = jnp.concatenate([zero, driven[:-2]], axis=0) * same_two
    return mixed[1] * (kernel[0] * driven + kernel[1] * back_one + kernel[2] * back_two)


def per_device(
    tokens_in,
    segments,
    gains,
    taps,
    in_proj,
    out_proj,
    gate_up_a,
    down_a,
    query_w,
    key_value_w,
    attn_out_w,
    gate_up_b,
    down_b,
    cotangent,
):
    half = tokens_in.shape[1]
    segment_ids = segments[0]
    length = segment_ids.shape[0]
    rows = in_proj.shape[0]
    width = rows * lax.axis_size("dp")
    rank = lax.axis_index("tensor")

    def in_order(own):
        other = swap(own)
        first = jnp.where(rank == 0, own, other)
        second = jnp.where(rank == 0, other, own)
        return jnp.concatenate([first, second], axis=0)

    def own_half(full):
        return lax.dynamic_slice_in_dim(full, rank * half, half, 0)

    def other_half(full):
        return lax.dynamic_slice_in_dim(full, (1 - rank) * half, half, 0)

    def four(own):
        far = flip_x(own)
        return own, swap(own), far, swap(far)

    def four_back(near, far):
        far_sum = (far[0] + swap(far[1]).astype(F32)).astype(BF)
        return near[0] + swap(near[1]).astype(F32) + flip_x(far_sum).astype(F32)

    misc = jnp.concatenate(
        [gains.T, taps.T, jnp.zeros((rows, 128 - gains.shape[0] - taps.shape[0]), BF)], axis=1
    )
    conv_cols = in_proj.shape[2]
    query_cols = query_w.shape[1]
    kv_cols = key_value_w.shape[2]
    unit = down_a.shape[0] // 2

    def shared(gate_up, down):
        parts = [halves(v, 1) for v in (gate_up[:, 0], gate_up[:, 1], down.T)]
        mine = jnp.concatenate([p[0] for p in parts], axis=1)
        return by_x(mine, flip_x(jnp.concatenate([p[1] for p in parts], axis=1)), 0)

    own = jnp.concatenate([in_proj[:, 0], in_proj[:, 1], in_proj[:, 2], out_proj.T, misc], axis=1)
    conv_w = ring_gather(by_x(own, flip_x(own), 0))
    ff_a = ring_gather(shared(gate_up_a, down_a))
    own = jnp.concatenate(
        [query_w, key_value_w[:, 0], key_value_w[:, 1], attn_out_w.T], axis=1
    )
    attn_w = ring_gather(by_x(own, flip_x(own), 0))
    ff_b = ring_gather(shared(gate_up_b, down_b))
    w_qkv = attn_w[:, : query_cols + 2 * kv_cols]
    w_attn = attn_w[:, query_cols + 2 * kv_cols :]
    w_in = [conv_w[:, k * conv_cols : (k + 1) * conv_cols] for k in range(3)]
    w_out = conv_w[:, 3 * conv_cols : 4 * conv_cols]
    misc_all = conv_w[:, 4 * conv_cols :]

    gain_rows = misc_all[:, :4].T.astype(F32)
    taps_all = ring_order(misc_all[:, 4:7].T, 1, back=True).astype(F32)
    kernel = lax.dynamic_slice_in_dim(taps_all, rank * conv_cols, conv_cols, 1)

    index = jnp.arange(length)
    first_of_doc = jnp.sum((segment_ids[None, :] < segment_ids[:, None]).astype(jnp.int32), axis=1)
    positions = (index - first_of_doc).astype(F32)
    same_one = (positions >= 1).astype(F32)[:, None]
    same_two = (positions >= 2).astype(F32)[:, None]
    cosine, sine = rope_tables(positions)
    doc_start = first_of_doc[None, :]

    hidden_zero = ring_order(tokens_in[0], 1).astype(F32)
    first_full = in_order(norm_low(hidden_zero, gain_rows[0]))
    grad_blocks = four(ring_order(cotangent[0], 1))
    first_full, grad_blocks = lax.optimization_barrier((first_full, grad_blocks))
    mixed = [dot_nn(first_full, w) for w in w_in]
    conv_out, conv_pull = jax.vjp(
        lambda mixed_in, kernel_in: conv_mix(mixed_in, kernel_in, same_one, same_two), mixed, kernel
    )
    conv_low = conv_out.astype(BF)

    def collect(own, other, w):
        sent = swap(dot_nt(other, w).astype(BF))
        return dot_nt(own, w) + sent.astype(F32)

    hidden_one = hidden_zero + collect(own_half(conv_low), other_half(conv_low), w_out)

    def feed_forward(hidden, gain, weights):
        blocks = four(norm_low(hidden, gain))
        near = ff_up(blocks[0], blocks[1], weights, unit)
        far = ff_up(blocks[2], blocks[3], weights, unit)
        return blocks, near, far

    def down(kept, weights):
        return narrow([kept[1][2]], weights, [2]), narrow([kept[2][2]], weights, [2])

    def feed_back(grad_out, grads, hidden, gain, weights, kept, settle):
        blocks, near, far = kept
        if len(grads) == 1:
            (own,) = grads
            sibling, across = swap(own), flip_x(own)
            near_back = ff_back(own, sibling, weights, near[0], near[1])
            near_sum = narrow(near_back, weights, [0, 1])
            near_sum, across = lax.optimization_barrier((near_sum, across))
            grads = own, sibling, across, swap(across)
        else:
            near_back = ff_back(grads[0], grads[1], weights, near[0], near[1])
            near_sum = narrow(near_back, weights, [0, 1])
        far_in = grads[2:]
        near_sum, far_in, settle = lax.optimization_barrier((near_sum, far_in, settle))
        far_back = ff_back(*far_in, weights, far[0], far[1])
        far_sum = narrow(far_back, weights, [0, 1])
        g_down = weight_grad(grads, [(near[2], far[2])])
        g_gate_up = weight_grad(
            blocks, [(near_back[0], far_back[0]), (near_back[1], far_back[1])]
        )
        grad_normed = four_back(near_sum, far_sum)
        grad_normed, g_down, g_gate_up = lax.optimization_barrier((grad_normed, g_down, g_gate_up))
        grad_hidden, grad_gain = norm_back(grad_normed, hidden, gain, grad_out)
        return grad_hidden, grad_gain, ring_sum(g_gate_up), ring_sum(g_down), settle

    def finish_shared(summed):
        mine, theirs = halves(summed, 0)
        return mine.astype(F32), flip_x(theirs).astype(F32)

    def finish(summed):
        mine, theirs = halves(summed, 0)
        return mine.astype(F32) + flip_x(theirs).astype(F32)

    def finish_ff(g_gate_up, g_down):
        down = finish_shared(g_down)
        mine, theirs = finish_shared(g_gate_up)
        gate = by_x(mine[:, :unit], theirs[:, :unit], 1)
        up = by_x(mine[:, unit:], theirs[:, unit:], 1)
        return jnp.stack([gate, up], axis=1), by_x(*down, 1).T

    kept_a = feed_forward(hidden_one, gain_rows[1], ff_a)
    hidden_two = hidden_one + four_back(*down(kept_a, ff_a))

    def my_part(full, other=False):
        start = (1 - rank if other else rank) * half
        return lax.dynamic_slice_in_dim(full, start, half, 1)

    def from_heads(full, w):
        over = (((0,), (1,)), ((), ()))
        sent = lax.dot_general(my_part(full, True), w, over, preferred_element_type=F32).astype(BF)
        kept = lax.dot_general(my_part(full), w, over, preferred_element_type=F32)
        return kept + swap(sent).astype(F32)

    def to_heads(w, full):
        return lax.dot_general(w, full, (((0,), (1,)), ((), ())), preferred_element_type=F32)

    third_full = in_order(norm_low(hidden_two, gain_rows[2]))
    qkv = to_heads(w_qkv, third_full)
    query, keys, values, attended, logs = attend(doc_start, cosine, sine, qkv, query_cols, kv_cols)
    hidden_three = hidden_two + from_heads(attended, w_attn)
    kept_b = feed_forward(hidden_three, gain_rows[3], ff_b)

    grad_four = ring_order(cotangent[0], 1).astype(F32)
    grad_three, gain_grad_three, sum_gu_b, sum_dn_b, _ = feed_back(
        grad_four, grad_blocks, hidden_three, gain_rows[3], ff_b, kept_b, ()
    )
    attn_full = in_order(grad_three.astype(BF))
    near, far = down(kept_b, ff_b)
    far_sum = (far[0] + swap(far[1]).astype(F32)).astype(BF)
    grad_attended = to_heads(w_attn, attn_full).astype(BF)
    grad_attended, near, far_sum = lax.optimization_barrier((grad_attended, near, far_sum))
    grad_qkv = attend_back(doc_start, cosine, sine, query, keys, values, logs, grad_attended)
    grad_qkv, far_sum, sum_dn_b = lax.optimization_barrier((grad_qkv, flip_x(far_sum), sum_dn_b))
    hidden_four = hidden_three + (near[0] + swap(near[1]).astype(F32) + far_sum.astype(F32))
    output = ring_order(hidden_four.astype(BF), 1, back=True)[None]
    grad_third = from_heads(jnp.concatenate(grad_qkv, axis=0), w_qkv)
    sum_second = ring_sum(second_grads(third_full, grad_qkv, attn_full, attended))
    grad_two, gain_grad_two = norm_back(grad_third, hidden_two, gain_rows[2], grad_three)

    grad_one, gain_grad_one, sum_gu_a, sum_dn_a, (sum_gu_b,) = feed_back(
        grad_two,
        (grad_two.astype(BF),),
        hidden_one,
        gain_rows[1],
        ff_a,
        kept_a,
        (sum_gu_b,),
    )
    conv_full = in_order(grad_one.astype(BF))
    conv_full, sum_dn_a, sum_second = lax.optimization_barrier((conv_full, sum_dn_a, sum_second))
    grad_conv = dot_nn(conv_full, w_out)
    grad_mixed, grad_kernel = conv_pull(grad_conv)
    grad_mixed = [g.astype(BF) for g in grad_mixed]
    own_first = sum(dot_nt(own_half(g), w) for g, w in zip(grad_mixed, w_in))
    other_first = sum(dot_nt(other_half(g), w) for g, w in zip(grad_mixed, w_in))
    grad_first = own_first + swap(other_first.astype(BF)).astype(F32)
    grad_zero, gain_grad_zero = norm_back(grad_first, hidden_zero, gain_rows[0], grad_one)

    grad_input = ring_order(grad_zero, 1, back=True)[None]

    kernel_full = lax.dynamic_update_slice(
        jnp.zeros((3, width), F32), grad_kernel, (0, rank * conv_cols)
    )
    small = jnp.concatenate(
        [
            jnp.stack([gain_grad_zero, gain_grad_one, gain_grad_two, gain_grad_three]),
            ring_order(kernel_full, 1),
            jnp.zeros((128 - 7, width), F32),
        ],
        axis=0,
    ).T.astype(BF)
    grad_first_w = first_grads(first_full, grad_mixed, conv_full, conv_low, small)
    summed_gu_b, summed_dn_b = finish_ff(sum_gu_b, sum_dn_b)
    summed_attn_w = finish(sum_second)
    summed_gu_a, summed_dn_a = finish_ff(sum_gu_a, sum_dn_a)
    summed_conv = finish(ring_sum(grad_first_w))
    summed_qkv = summed_attn_w[:, : query_cols + 2 * kv_cols]
    summed_attn = summed_attn_w[:, query_cols + 2 * kv_cols :].T
    summed_win = summed_conv[:, : 3 * conv_cols].reshape(rows, 3, conv_cols)
    summed_wout = summed_conv[:, 3 * conv_cols : 4 * conv_cols].T
    small_sum = summed_conv[:, 4 * conv_cols :]
    small_sum = (small_sum + swap(small_sum)).T
    return (
        output,
        grad_input,
        small_sum[:4],
        small_sum[4:7],
        summed_win,
        summed_wout,
        summed_gu_a,
        summed_dn_a,
        summed_qkv[:, :query_cols],
        summed_qkv[:, query_cols:].reshape(rows, 2, kv_cols),
        summed_attn,
        summed_gu_b,
        summed_dn_b,
    )


def solution(mesh):
    return jax.shard_map(
        per_device,
        mesh=mesh,
        in_specs=(
            P("dp", "tensor", None),
            P("dp", None),
            P(None, "dp"),
            P(None, "dp"),
            P("dp", None, "tensor"),
            P("tensor", "dp"),
            P("dp", None, "tensor"),
            P("tensor", "dp"),
            P("dp", "tensor"),
            P("dp", None, "tensor"),
            P("tensor", "dp"),
            P("dp", None, "tensor"),
            P("tensor", "dp"),
            P("dp", "tensor", None),
        ),
        out_specs=(
            P("dp", "tensor", None),
            P("dp", "tensor", None),
            P(None, "dp"),
            P(None, "dp"),
            P("dp", None, "tensor"),
            P("tensor", "dp"),
            P("dp", None, "tensor"),
            P("tensor", "dp"),
            P("dp", "tensor"),
            P("dp", None, "tensor"),
            P("tensor", "dp"),
            P("dp", None, "tensor"),
            P("tensor", "dp"),
        ),
        check_vma=False,
    )
```

time: 1080 us -> 701 us (0.65)
  Pallas kernels: 0 us -> 241 us
  matrix products: 267 us -> 46 us
  waiting for transfers between devices: 434 us -> 219 us
  starting transfers between devices: 176 us -> 29.1 us
  other arithmetic: 99 us -> 53.3 us
  between operations: 4.55 us -> 16.3 us
    ppermute x144 -> x18, waiting for transfers between devices: 433 us -> 129 us  [flip_x(): return lax.ppermute(values, 'dp', [(i, i ^ 1) for i in range(n)])]
    pallas_call x0 -> x24, Pallas kernels: none -> 241 us  [the longest x8 59.7 us: narrow(): pl.pallas_call(functools.partial(narrow_kernel, n), grid=(depth // tile,)...]
    ppermute x144 -> x18, starting transfers between devices: 174 us -> 23.8 us  [flip_x(): return lax.ppermute(values, 'dp', [(i, i ^ 1) for i in range(n)])]
    dot_general x25 -> x6, matrix products: 102 us -> 14.7 us  [the longest x2 10 us: to_heads(): lax.dot_general(w, full, (((0,), (1,)), ((), ())), preferred_element_type...]
    dot_general x15 -> x4, matrix products: 93.8 us -> 15 us  [dot_nn(): return jnp.dot(a, w, preferred_element_type=F32)]
    dot_general x26 -> x8, matrix products: 70.5 us -> 16.3 us  [dot_nt(): lax.dot_general(a, w, (((1,), (1,)), ((), ())), preferred_element_type=F32)]
    reduce_scatter x0 -> x6, waiting for transfers between devices: none -> 51.6 us  [ring_sum(): lax.psum_scatter(grad, 'dp', scatter_dimension=0, axis_index_groups=ring_...]
    convert_element_type x40 -> x11, other arithmetic: 40.2 us -> 9.46 us  [the longest x1 3.84 us: per_device(): grad_two.astype(BF)]
  transfers between devices with their start and end apart: 161 -> 53, of which waited for: 65 -> 27; matrix products, arithmetic and copies ran while one was open for 36% -> 20% of each run, Pallas kernels for 0% -> 31%
where the time goes in v2:
time: 701 us; the launch traced here: 691 us
  Pallas kernels  241 us (34%)
  waiting for transfers between devices  219 us (31%)
  local copies, waits for them, and re-layouts  86 us (12%)
  other arithmetic  53.3 us (8%)
  matrix products  46 us (7%)
  starting transfers between devices  29.1 us (4%)
  between operations  16.3 us (2%)
    ppermute x18, waiting for transfers between devices, flip_x(): return lax.ppermute(values, 'dp', [(i, i ^ 1) for i in range(n)])  129 us
    unnamed x326, local copies, waits for them, and re-layouts  60 us
    pallas_call x8, Pallas kernels, narrow(): pl.pallas_call(functools.partial(narrow_kernel, n), grid=(depth // tile,)...  59.7 us
    pallas_call x4, Pallas kernels, weight_grad(): pl.pallas_call(weight_grad_kernel, grid=(depth // tile,), out_shape=out,...  54.4 us
    reduce_scatter x6, waiting for transfers between devices, ring_sum(): lax.psum_scatter(grad, 'dp', scatter_dimension=0, axis_index_groups=ring_...  51.6 us
    pallas_call x4, Pallas kernels, ff_up(): pl.pallas_call(ff_up_kernel, grid=(2,), out_shape=(out, out, out), in_spe...  40.3 us
    pallas_call x4, Pallas kernels, ff_back(): pl.pallas_call(ff_back_kernel, grid=(2,), out_shape=(out, out), in_specs=...  31.2 us
    ppermute x18, starting transfers between devices, flip_x(): return lax.ppermute(values, 'dp', [(i, i ^ 1) for i in range(n)])  23.8 us
  transfers between devices with their start and end apart: 53, of which 27 were waited for; matrix products, arithmetic and copies ran while one was open for 20% of the time, Pallas kernels for 31%

profile of v2, /device:TPU:0, one launch (start us, length us, event | category | flops | bytes accessed | tf_op | source)
XLA Modules:
  0.0 690.9 jit_solution(7596491387703582054)
XLA Ops:
  13.7 6.7 collective-permute-done
  24.3 9.6 %collective-permute-done.7 = bf16[64,3456]{1,0:T(8,128)(2,1)S(1)} collective-permute-done((bf16[64,3456]{1,0:T(8,128)(2,1)S(1)}, bf16[64,3456]{1,0:T(8,128)(2,1)S(1)}, u32[]{:S(2)}, u32[]{:S(2)}) %collective-permute-start.7) | collective-permute-done | bytes 442400 | tf_op jit(solution)/shard_map/ppermute | solution.py:34
  59.1 7.0 %collective-permute-done.13 = bf16[64,1536]{1,0:T(8,128)(2,1)} collective-permute-done((bf16[64,1536]{1,0:T(8,128)(2,1)S(1)}, bf16[64,1536]{1,0:T(8,128)(2,1)}, u32[]{:S(2)}, u32[]{:S(2)}) %collective-permute-start.13) | collective-permute-done | bytes 196640 | tf_op jit(solution)/shard_map/ppermute | solution.py:34
  106.1 23.9 %collective-permute-done.9.h0.refs_2_ = bf16[512,1024]{1,0:T(8,128)(2,1)S(1)} collective-permute-done((bf16[512,1024]{1,0:T(8,128)(2,1)S(1)}, bf16[512,1024]{1,0:T(8,128)(2,1)S(1)}, u32[]{:S(2)}, u32[]{:S(2)}) %collective-permute-start.9) | collective-permute-done | bytes 1048608 | tf_op jit(solution)/shard_map/ppermute | solution.py:34
  134.4 16.0 %all-gather.7.cloned.1.call-done.wg.wu.refs_1_.wd.refs_2_.refs_3_ = bf16[1024,3456]{1,0:T(8,128)(2,1)} async-done(((bf16[128,3456]{1,0:T(8,128)(2,1)}), bf16[1024,3456]{1,0:T(8,128)(2,1)}) %all-gather.7.cloned.1.call-update) | async-done | bytes 7077904 | tf_op jit(solution)/shard_map/all_gather | solution.py:51
  151.7 9.6 %shard_map.239 = (bf16[1024,1152]{1,0:T(8,128)(2,1)S(1)}, bf16[1024,1152]{1,0:T(8,128)(2,1)}, bf16[1024,1152]{1,0:T(8,128)(2,1)}) custom-call(bf16[512,1024]{1,0:T(8,128)(2,1)S(1)} %collective-permute-done.9.h0.refs_2_, bf16[512,1024]{1,0:T(8,128)(2,1)S(1)} %copy-done.44, bf16[1024,3456]{1,0:T(8,128)(2,1)} %all-gather.7.cloned.1.call-done.wg.wu.refs_1_.wd.refs_2_.refs_3_, ...), custom_call_target="tpu_custom_call" | custom-call | flops 4831838208 | bytes 13893632 | tf_op jit(solution)/shard_map/pallas_call | solution.py:122
  169.5 10.0 %shard_map.237 = (bf16[1024,1152]{1,0:T(8,128)(2,1)S(1)}, bf16[1024,1152]{1,0:T(8,128)(2,1)}, bf16[1024,1152]{1,0:T(8,128)(2,1)}) custom-call(bf16[512,1024]{1,0:T(8,128)(2,1)S(1)} %multiply_convert_fusion.5.h0.refs_0_, bf16[512,1024]{1,0:T(8,128)(2,1)} %collective-permute-done.6.h1.refs_1_, ...), custom_call_target="tpu_custom_call" | custom-call | flops 4831838208 | bytes 13893632 | tf_op jit(solution)/shard_map/pallas_call | solution.py:122
  182.6 5.4 shard_map.238
  190.8 23.2 %collective-permute-done.12 = bf16[512,1024]{1,0:T(8,128)(2,1)S(1)} collective-permute-done((bf16[512,1024]{1,0:T(8,128)(2,1)S(1)}, bf16[512,1024]{1,0:T(8,128)(2,1)S(1)}, u32[]{:S(2)}, u32[]{:S(2)}) %collective-permute-start.12) | collective-permute-done | bytes 1048608 | tf_op jit(solution)/shard_map/ppermute | solution.py:34
  219.6 6.7 fusion.13.q_ref.k_ref.v_ref
  226.2 19.9 %shard_map.241 = (bf16[512,1024]{1,0:T(8,128)(2,1)S(1)}, bf16[256,1024]{1,0:T(8,128)(2,1)S(1)}, bf16[256,1024]{1,0:T(8,128)(2,1)S(1)}, bf16[512,1024]{1,0:T(8,128)(2,1)S(1)}, f32[4,2,1024]{2,1,0:T(2,128)S(1)}) custom-call(s32[1,1024]{1,0:T(1,128)S(1)} %bitcast.75, f32[32,1024]{1,0:T(8,128)S(1)} %get-tuple-element.317.cos_ref, ...), custom_call_target="tpu_custom_call" | custom-call | flops 1073741824 | bytes 8388608 | tf_op jit(solution)/shard_map/pallas_call | solution.py:278
  253.1 23.9 %collective-permute-done.19.h0.refs_2_ = bf16[512,1024]{1,0:T(8,128)(2,1)} collective-permute-done((bf16[512,1024]{1,0:T(8,128)(2,1)S(1)}, bf16[512,1024]{1,0:T(8,128)(2,1)}, u32[]{:S(2)}, u32[]{:S(2)}) %collective-permute-start.19) | collective-permute-done | bytes 1048608 | tf_op jit(solution)/shard_map/ppermute | solution.py:34
  276.9 10.1 %shard_map.242 = (bf16[1024,1152]{1,0:T(8,128)(2,1)S(1)}, bf16[1024,1152]{1,0:T(8,128)(2,1)}, bf16[1024,1152]{1,0:T(8,128)(2,1)}) custom-call(bf16[512,1024]{1,0:T(8,128)(2,1)S(1)} %multiply_convert_fusion.3.h0.refs_0_, bf16[512,1024]{1,0:T(8,128)(2,1)S(1)} %collective-permute-done.17.h1.refs_1_, ...), custom_call_target="tpu_custom_call" | custom-call | flops 4831838208 | bytes 13893632 | tf_op jit(solution)/shard_map/pallas_call | solution.py:122
  289.7 7.7 %shard_map.243 = (bf16[1024,1152]{1,0:T(8,128)(2,1)S(1)}, bf16[1024,1152]{1,0:T(8,128)(2,1)}) custom-call(bf16[512,1024]{1,0:T(8,128)(2,1)S(1)} %slice_dynamic-update-slice_fusion.16.e0.refs_0_, bf16[512,1024]{1,0:T(8,128)(2,1)S(1)} %copy-done.25, bf16[1024,3456]{1,0:T(8,128)(2,1)} %all-gather.11.cloned.1.call-done.wg.wu.wd.refs_2_.refs_3_.refs_1_, ...), custom_call_target="tpu_custom_call" | custom-call | flops 2415919104 | bytes 13893632 | tf_op jit(solution)/shard_map/pallas_call | solution.py:154
  297.4 10.2 %shard_map.244 = (f32[512,1024]{1,0:T(8,128)S(1)}, bf16[512,1024]{1,0:T(8,128)(2,1)}) custom-call(bf16[1024,1152]{1,0:T(8,128)(2,1)S(1)} %get-tuple-element.104.refs_0_.refs_4_, bf16[1024,1152]{1,0:T(8,128)(2,1)} %get-tuple-element.105.refs_1_.refs_6_, bf16[1024,3456]{1,0:T(8,128)(2,1)} %all-gather.11.cloned.1.call-done.wg.wu.wd.refs_2_.refs_3_.refs_1_, ...), custom_call_target="tpu_custom_call" | custom-call | flops 4831838208 | bytes 12582912 | tf_op jit(solution)/shard_map/pallas_call | solution.py:220
  308.9 10.6 %shard_map.245 = (bf16[1024,1152]{1,0:T(8,128)(2,1)S(1)}, bf16[1024,1152]{1,0:T(8,128)(2,1)}, bf16[1024,1152]{1,0:T(8,128)(2,1)}) custom-call(bf16[512,1024]{1,0:T(8,128)(2,1)} %collective-permute-done.19.h0.refs_2_, bf16[512,1024]{1,0:T(8,128)(2,1)} %collective-permute-done.20.h1.refs_3_, ...), custom_call_target="tpu_custom_call" | custom-call | flops 4831838208 | bytes 13893632 | tf_op jit(solution)/shard_map/pallas_call | solution.py:122
  321.0 8.0 %shard_map.246 = (bf16[1024,1152]{1,0:T(8,128)(2,1)S(1)}, bf16[1024,1152]{1,0:T(8,128)(2,1)}) custom-call(bf16[512,1024]{1,0:T(8,128)(2,1)S(1)} %copy-done.28, bf16[512,1024]{1,0:T(8,128)(2,1)} %collective-permute-done.4.e1.refs_3_, bf16[1024,3456]{1,0:T(8,128)(2,1)} %all-gather.11.cloned.1.call-done.wg.wu.wd.refs_2_.refs_3_.refs_1_, ...), custom_call_target="tpu_custom_call" | custom-call | flops 2415919104 | bytes 13893632 | tf_op jit(solution)/shard_map/pallas_call | solution.py:154
  329.0 9.4 %shard_map.247 = (f32[512,1024]{1,0:T(8,128)S(1)}, bf16[512,1024]{1,0:T(8,128)(2,1)S(1)}) custom-call(bf16[1024,1152]{1,0:T(8,128)(2,1)S(1)} %get-tuple-element.116.refs_0_.refs_5_, bf16[1024,1152]{1,0:T(8,128)(2,1)} %get-tuple-element.117.refs_1_.refs_7_, bf16[1024,3456]{1,0:T(8,128)(2,1)} %all-gather.11.cloned.1.call-done.wg.wu.wd.refs_2_.refs_3_.refs_1_, ...), custom_call_target="tpu_custom_call" | custom-call | flops 4831838208 | bytes 12582912 | tf_op jit(solution)/shard_map/pallas_call | solution.py:220
  344.7 9.9 %shard_map.248 = bf16[1024,1152]{1,0:T(8,128)(2,1)} custom-call(bf16[512,1024]{1,0:T(8,128)(2,1)S(1)} %slice_dynamic-update-slice_fusion.16.e0.refs_0_, bf16[512,1024]{1,0:T(8,128)(2,1)S(1)} %copy-done.26, bf16[512,1024]{1,0:T(8,128)(2,1)S(1)} %copy-done.28, bf16[512,1024]{1,0:T(8,128)(2,1)} %collective-permute-done.4.e1.refs_3_, ...), custom_call_target="tpu_custom_call" | custom-call | flops 4831838208 | bytes 11272192 | tf_op jit(solution)/shard_map/pallas_call | solution.py:185
  357.0 17.4 %shard_map.249 = bf16[1024,2304]{1,0:T(8,128)(2,1)} custom-call(bf16[512,1024]{1,0:T(8,128)(2,1)S(1)} %copy-done.21, bf16[512,1024]{1,0:T(8,128)(2,1)S(1)} %copy-done.51, bf16[512,1024]{1,0:T(8,128)(2,1)} %collective-permute-done.19.h0.refs_2_, bf16[512,1024]{1,0:T(8,128)(2,1)} %collective-permute-done.20.h1.refs_3_, bf16[1024,1152]{1,0:T(8,128)(2,1)} %copy-done.1, ...), custom_call_target="tpu_custom_call" | custom-call | flops 9663676416 | bytes 18350080 | tf_op jit(solution)/shard_map/pallas_call | solution.py:185
  398.0 21.1 %shard_map.252 = (bf16[512,1024]{1,0:T(8,128)(2,1)S(1)}, bf16[256,1024]{1,0:T(8,128)(2,1)S(1)}, bf16[256,1024]{1,0:T(8,128)(2,1)S(1)}) custom-call(s32[1,1024]{1,0:T(1,128)S(1)} %bitcast.76, f32[32,1024]{1,0:T(8,128)S(1)} %copy-done.34, f32[32,1024]{1,0:T(8,128)S(1)} %get-tuple-element.316.sin_ref, bf16[512,1024]{1,0:T(8,128)(2,1)S(1)} %copy-done.47, ...), custom_call_target="tpu_custom_call" | custom-call | flops 3221225472 | bytes 4194304 | tf_op jit(solution)/shard_map/pallas_call | solution.py:344
  436.5 6.5 shard_map.259
  443.6 7.7 %shard_map.253 = (bf16[1024,1152]{1,0:T(8,128)(2,1)S(1)}, bf16[1024,1152]{1,0:T(8,128)(2,1)}) custom-call(bf16[512,1024]{1,0:T(8,128)(2,1)S(1)} %get-tuple-element.243.e0.refs_0_, bf16[512,1024]{1,0:T(8,128)(2,1)S(1)} %collective-permute-done.28.e1.refs_1_, bf16[1024,3456]{1,0:T(8,128)(2,1)} %all-gather.7.cloned.1.call-done.wg.wu.refs_1_.wd.refs_2_.refs_3_, ...), custom_call_target="tpu_custom_call" | custom-call | flops 2415919104 | bytes 13893632 | tf_op jit(solution)/shard_map/pallas_call | solution.py:154
  451.3 10.2 %shard_map.254 = (f32[512,1024]{1,0:T(8,128)S(1)}, bf16[512,1024]{1,0:T(8,128)(2,1)}) custom-call(bf16[1024,1152]{1,0:T(8,128)(2,1)S(1)} %get-tuple-element.145.refs_0_.refs_4_, bf16[1024,1152]{1,0:T(8,128)(2,1)} %get-tuple-element.146.refs_1_.refs_6_, bf16[1024,3456]{1,0:T(8,128)(2,1)} %all-gather.7.cloned.1.call-done.wg.wu.refs_1_.wd.refs_2_.refs_3_, ...), custom_call_target="tpu_custom_call" | custom-call | flops 4831838208 | bytes 12582912 | tf_op jit(solution)/shard_map/pallas_call | solution.py:220
  462.8 5.9 collective-permute-done.29.e0.refs_2_
  473.6 7.9 %shard_map.255 = (bf16[1024,1152]{1,0:T(8,128)(2,1)S(1)}, bf16[1024,1152]{1,0:T(8,128)(2,1)}) custom-call(bf16[512,1024]{1,0:T(8,128)(2,1)S(1)} %collective-permute-done.29.e0.refs_2_, bf16[512,1024]{1,0:T(8,128)(2,1)S(1)} %copy-done.32, bf16[1024,3456]{1,0:T(8,128)(2,1)} %all-gather.7.cloned.1.call-done.wg.wu.refs_1_.wd.refs_2_.refs_3_, ...), custom_call_target="tpu_custom_call" | custom-call | flops 2415919104 | bytes 13893632 | tf_op jit(solution)/shard_map/pallas_call | solution.py:154
  481.5 9.4 %shard_map.256 = (f32[512,1024]{1,0:T(8,128)S(1)}, bf16[512,1024]{1,0:T(8,128)(2,1)S(1)}) custom-call(bf16[1024,1152]{1,0:T(8,128)(2,1)S(1)} %get-tuple-element.159.refs_0_.refs_5_, bf16[1024,1152]{1,0:T(8,128)(2,1)} %get-tuple-element.160.refs_1_.refs_7_, bf16[1024,3456]{1,0:T(8,128)(2,1)} %all-gather.7.cloned.1.call-done.wg.wu.refs_1_.wd.refs_2_.refs_3_, ...), custom_call_target="tpu_custom_call" | custom-call | flops 4831838208 | bytes 12582912 | tf_op jit(solution)/shard_map/pallas_call | solution.py:220
  495.7 9.9 %shard_map.257 = bf16[1024,1152]{1,0:T(8,128)(2,1)} custom-call(bf16[512,1024]{1,0:T(8,128)(2,1)S(1)} %get-tuple-element.243.e0.refs_0_, bf16[512,1024]{1,0:T(8,128)(2,1)S(1)} %collective-permute-done.28.e1.refs_1_, bf16[512,1024]{1,0:T(8,128)(2,1)S(1)} %copy-done.30, bf16[512,1024]{1,0:T(8,128)(2,1)S(1)} %copy-done.32, ...), custom_call_target="tpu_custom_call" | custom-call | flops 4831838208 | bytes 11272192 | tf_op jit(solution)/shard_map/pallas_call | solution.py:185
  508.1 17.2 %shard_map.258 = bf16[1024,2304]{1,0:T(8,128)(2,1)} custom-call(bf16[512,1024]{1,0:T(8,128)(2,1)S(1)} %copy-done.19, bf16[512,1024]{1,0:T(8,128)(2,1)} %collective-permute-done.6.h1.refs_1_, bf16[512,1024]{1,0:T(8,128)(2,1)S(1)} %copy-done.42, bf16[512,1024]{1,0:T(8,128)(2,1)S(1)} %copy-done.45, bf16[1024,1152]{1,0:T(8,128)(2,1)} %copy-done, ...), custom_call_target="tpu_custom_call" | custom-call | flops 9663676416 | bytes 18350080 | tf_op jit(solution)/shard_map/pallas_call | solution.py:185
  546.2 17.1 %reduce-scatter.11.cloned.1.call-done = bf16[128,1152]{1,0:T(8,128)(2,1)} async-done(((bf16[1024,1152]{1,0:T(8,128)(2,1)}), bf16[128,1152]{1,0:T(8,128)(2,1)}) %reduce-scatter.11.cloned.1.call-update) | async-done | bytes 294928 | tf_op jit(solution)/shard_map/reduce_scatter | solution.py:55
  591.4 7.8 %shard_map.260 = bf16[1024,2176]{1,0:T(8,128)(2,1)} custom-call(bf16[1024,1024]{1,0:T(8,128)(2,1)} %copy-done.70, bf16[1024,1024]{1,0:T(8,128)(2,1)} %pad_maximum_fusion.3.left1, bf16[1024,512]{1,0:T(8,128)(2,1)S(1)} %multiply_convert_fusion.2.g0, bf16[1024,512]{1,0:T(8,128)(2,1)S(1)} %get-tuple-element.249.g1, bf16[1024,512]{1,0:T(8,128)(2,1)S(1)} %get-tuple-element.239.g2, ...), custom_call_target="tpu_custom_call" | custom-call | flops 4294967296 | bytes 12845056 | tf_op jit(solution)/shard_map/pallas_call | solution.py:412
  636.7 34.5 %reduce-scatter.15.cloned.1.call-done = bf16[128,2176]{1,0:T(8,128)(2,1)} async-done(((bf16[1024,2176]{1,0:T(8,128)(2,1)}), bf16[128,2176]{1,0:T(8,128)(2,1)}) %reduce-scatter.15.cloned.1.call-update) | async-done | bytes 557072 | tf_op jit(solution)/shard_map/reduce_scatter | solution.py:55
  (581 shorter events, 274.3 us)
Async XLA Ops:
  7.2 66.2 %all-gather.5.cloned.1.call-start = ((), (), s32[]{:S(2)}) async-start(), calls=%async_computation.6 | async-start | bytes 5013504 | tf_op jit(solution)/shard_map/all_gather | solution.py:51
  10.7 9.7 %collective-permute-start = (bf16[64,2176]{1,0:T(8,128)(2,1)S(1)}, bf16[64,2176]{1,0:T(8,128)(2,1)S(1)}, u32[]{:S(2)}, u32[]{:S(2)}) collective-permute-start(bf16[64,2176]{1,0:T(8,128)(2,1)S(1)} %concatenate.100), channel_id=1, source_target_pairs={{0,2},{2,0},{4,6},{6,4},{8,10},{10,8},{12,14},{14,12},{16,18},{18,... | collective-permute-start | bytes 835592 | tf_op jit(solution)/shard_map/ppermute | solution.py:34
  21.3 129.1 %all-gather.7.cloned.1.call-start = ((), (), s32[]{:S(2)}) async-start(), calls=%async_computation.7 | async-start | bytes 7962624 | tf_op jit(solution)/shard_map/all_gather | solution.py:51
  22.5 11.4 %collective-permute-start.7 = (bf16[64,3456]{1,0:T(8,128)(2,1)S(1)}, bf16[64,3456]{1,0:T(8,128)(2,1)S(1)}, u32[]{:S(2)}, u32[]{:S(2)}) collective-permute-start(bf16[64,3456]{1,0:T(8,128)(2,1)S(1)} %pad_maximum_fusion.10), channel_id=1, source_target_pairs={{0,2},{2,0},{4,6},{6,4},{8,10},{10,8},{12,14},{14,12},{16,18},{18,... | collective-permute-start | bytes 1327112 | tf_op jit(solution)/shard_map/ppermute | solution.py:34
  35.1 184.5 %all-gather.9.cloned.1.call-start = ((), (), s32[]{:S(2)}) async-start(), calls=%async_computation.8 | async-start | bytes 3538944 | tf_op jit(solution)/shard_map/all_gather | solution.py:51
  35.7 50.2 %collective-permute-start.2 = (bf16[512,1024]{1,0:T(8,128)(2,1)S(1)}, bf16[512,1024]{1,0:T(8,128)(2,1)S(1)}, u32[]{:S(2)}, u32[]{:S(2)}) collective-permute-start(bf16[512,1024]{1,0:T(8,128)(2,1)S(1)} %slice_dynamic-update-slice_fusion.16.e0.refs_0_), channel_id=1, source_target_pairs={{0,1},{1,0},{2,3},{3,2},{4,5},{5,4},{6,7},{7,6},{8,9},{9,8},{10,11... | collective-permute-start | bytes 3145736 | tf_op jit(solution)/shard_map/ppermute | solution.py:29
  35.8 32.3 %collective-permute-start.3 = (bf16[512,1024]{1,0:T(8,128)(2,1)S(1)}, bf16[512,1024]{1,0:T(8,128)(2,1)S(1)}, u32[]{:S(2)}, u32[]{:S(2)}) collective-permute-start(bf16[512,1024]{1,0:T(8,128)(2,1)S(1)} %slice_dynamic-update-slice_fusion.16.e0.refs_0_), channel_id=1, source_target_pairs={{0,2},{2,0},{4,6},{6,4},{8,10},{10,8},{12,14},{14,12},{16,18},{18,... | collective-permute-start | bytes 3145736 | tf_op jit(solution)/shard_map/ppermute | solution.py:34
  38.0 28.1 %collective-permute-start.13 = (bf16[64,1536]{1,0:T(8,128)(2,1)S(1)}, bf16[64,1536]{1,0:T(8,128)(2,1)}, u32[]{:S(2)}, u32[]{:S(2)}) collective-permute-start(bf16[64,1536]{1,0:T(8,128)(2,1)S(1)} %pad_maximum_fusion.14), channel_id=1, source_target_pairs={{0,2},{2,0},{4,6},{6,4},{8,10},{10,8},{12,14},{14,12},{16,18},{18,... | collective-permute-start | bytes 589832 | tf_op jit(solution)/shard_map/ppermute | solution.py:34
  43.4 54.9 %collective-permute-start.16 = (bf16[64,3456]{1,0:T(8,128)(2,1)}, bf16[64,3456]{1,0:T(8,128)(2,1)}, u32[]{:S(2)}, u32[]{:S(2)}) collective-permute-start(bf16[64,3456]{1,0:T(8,128)(2,1)} %pad_maximum_fusion.12), channel_id=1, source_target_pairs={{0,2},{2,0},{4,6},{6,4},{8,10},{10,8},{12,14},{14,12},{16,18},{18,... | collective-permute-start | bytes 1327112 | tf_op jit(solution)/shard_map/ppermute | solution.py:34
  68.0 208.9 %all-gather.11.cloned.1.call-start = ((), (), s32[]{:S(2)}) async-start(), calls=%async_computation.9 | async-start | bytes 7962624 | tf_op jit(solution)/shard_map/all_gather | solution.py:51
  68.1 17.9 %collective-permute-start.4 = (bf16[512,1024]{1,0:T(8,128)(2,1)S(1)}, bf16[512,1024]{1,0:T(8,128)(2,1)}, u32[]{:S(2)}, u32[]{:S(2)}) collective-permute-start(bf16[512,1024]{1,0:T(8,128)(2,1)S(1)} %collective-permute-done.3.e0.refs_2_), channel_id=1, source_target_pairs={{0,1},{1,0},{2,3},{3,2},{4,5},{5,4},{6,7},{7,6},{8,9},{9,8},{10,11... | collective-permute-start | bytes 3145736 | tf_op jit(solution)/shard_map/ppermute | solution.py:29
  100.4 322.6 %reduce-scatter.7.cloned.1.call-start = ((), (), s32[]{:S(2)}) async-start(), calls=%async_computation.10 | async-start | bytes 2654208 | tf_op jit(solution)/shard_map/reduce_scatter | solution.py:55
  104.5 25.5 %collective-permute-start.9 = (bf16[512,1024]{1,0:T(8,128)(2,1)S(1)}, bf16[512,1024]{1,0:T(8,128)(2,1)S(1)}, u32[]{:S(2)}, u32[]{:S(2)}) collective-permute-start(bf16[512,1024]{1,0:T(8,128)(2,1)S(1)} %multiply_convert_fusion.5.h0.refs_0_), channel_id=1, source_target_pairs={{0,2},{2,0},{4,6},{6,4},{8,10},{10,8},{12,14},{14,12},{16,18},{18,... | collective-permute-start | bytes 3145736 | tf_op jit(solution)/shard_map/ppermute | solution.py:34
  130.0 39.5 %collective-permute-start.6 = (bf16[512,1024]{1,0:T(8,128)(2,1)S(1)}, bf16[512,1024]{1,0:T(8,128)(2,1)}, u32[]{:S(2)}, u32[]{:S(2)}) collective-permute-start(bf16[512,1024]{1,0:T(8,128)(2,1)S(1)} %multiply_convert_fusion.5.h0.refs_0_), channel_id=1, source_target_pairs={{0,1},{1,0},{2,3},{3,2},{4,5},{5,4},{6,7},{7,6},{8,9},{9,8},{10,11... | collective-permute-start | bytes 3145736 | tf_op jit(solution)/shard_map/ppermute | solution.py:29
  169.4 19.2 %collective-permute-start.11 = (bf16[512,1024]{1,0:T(8,128)(2,1)S(1)}, bf16[512,1024]{1,0:T(8,128)(2,1)S(1)}, u32[]{:S(2)}, u32[]{:S(2)}) collective-permute-start(bf16[512,1024]{1,0:T(8,128)(2,1)S(1)} %get-tuple-element.98), channel_id=1, source_target_pairs={{0,1},{1,0},{2,3},{3,2},{4,5},{5,4},{6,7},{7,6},{8,9},{9,8},{10,11... | collective-permute-start | bytes 3145736 | tf_op jit(solution)/shard_map/ppermute | solution.py:29
  188.9 25.2 %collective-permute-start.12 = (bf16[512,1024]{1,0:T(8,128)(2,1)S(1)}, bf16[512,1024]{1,0:T(8,128)(2,1)S(1)}, u32[]{:S(2)}, u32[]{:S(2)}) collective-permute-start(bf16[512,1024]{1,0:T(8,128)(2,1)S(1)} %add_convert_fusion.5), channel_id=1, source_target_pairs={{0,2},{2,0},{4,6},{6,4},{8,10},{10,8},{12,14},{14,12},{16,18},{18,... | collective-permute-start | bytes 3145736 | tf_op jit(solution)/shard_map/ppermute | solution.py:34
  251.5 25.4 %collective-permute-start.19 = (bf16[512,1024]{1,0:T(8,128)(2,1)S(1)}, bf16[512,1024]{1,0:T(8,128)(2,1)}, u32[]{:S(2)}, u32[]{:S(2)}) collective-permute-start(bf16[512,1024]{1,0:T(8,128)(2,1)S(1)} %multiply_convert_fusion.3.h0.refs_0_), channel_id=1, source_target_pairs={{0,2},{2,0},{4,6},{6,4},{8,10},{10,8},{12,14},{14,12},{16,18},{18,... | collective-permute-start | bytes 3145736 | tf_op jit(solution)/shard_map/ppermute | solution.py:34
  253.1 23.9 %collective-permute-start.17 = (bf16[512,1024]{1,0:T(8,128)(2,1)S(1)}, bf16[512,1024]{1,0:T(8,128)(2,1)S(1)}, u32[]{:S(2)}, u32[]{:S(2)}) collective-permute-start(bf16[512,1024]{1,0:T(8,128)(2,1)S(1)} %multiply_convert_fusion.3.h0.refs_0_), channel_id=1, source_target_pairs={{0,1},{1,0},{2,3},{3,2},{4,5},{5,4},{6,7},{7,6},{8,9},{9,8},{10,11... | collective-permute-start | bytes 3145736 | tf_op jit(solution)/shard_map/ppermute | solution.py:29
  276.9 32.0 %collective-permute-start.20 = (bf16[512,1024]{1,0:T(8,128)(2,1)}, bf16[512,1024]{1,0:T(8,128)(2,1)}, u32[]{:S(2)}, u32[]{:S(2)}) collective-permute-start(bf16[512,1024]{1,0:T(8,128)(2,1)} %collective-permute-done.19.h0.refs_2_), channel_id=1, source_target_pairs={{0,1},{1,0},{2,3},{3,2},{4,5},{5,4},{6,7},{7,6},{8,9},{9,8},{10,11... | collective-permute-start | bytes 3145736 | tf_op jit(solution)/shard_map/ppermute | solution.py:29
  338.9 35.6 %collective-permute-start.18 = (bf16[512,1024]{1,0:T(8,128)(2,1)}, bf16[512,1024]{1,0:T(8,128)(2,1)}, u32[]{:S(2)}, u32[]{:S(2)}) collective-permute-start(bf16[512,1024]{1,0:T(8,128)(2,1)} %get-tuple-element.111), channel_id=1, source_target_pairs={{0,1},{1,0},{2,3},{3,2},{4,5},{5,4},{6,7},{7,6},{8,9},{9,8},{10,11... | collective-permute-start | bytes 3145736 | tf_op jit(solution)/shard_map/ppermute | solution.py:29
  343.2 31.3 %collective-permute-start.22 = (bf16[512,1024]{1,0:T(8,128)(2,1)}, bf16[512,1024]{1,0:T(8,128)(2,1)}, u32[]{:S(2)}, u32[]{:S(2)}) collective-permute-start(bf16[512,1024]{1,0:T(8,128)(2,1)} %add_convert_fusion.4), channel_id=1, source_target_pairs={{0,2},{2,0},{4,6},{6,4},{8,10},{10,8},{12,14},{14,12},{16,18},{18,... | collective-permute-start | bytes 3145736 | tf_op jit(solution)/shard_map/ppermute | solution.py:34
  377.9 94.5 %reduce-scatter.9.cloned.1.call-start = ((), (), s32[]{:S(2)}) async-start(), calls=%async_computation.11 | async-start | bytes 5308416 | tf_op jit(solution)/shard_map/reduce_scatter | solution.py:55
  378.4 167.7 %reduce-scatter.13.cloned.1.call-start = ((), (), s32[]{:S(2)}) async-start(), calls=%async_computation.13 | async-start | bytes 3538944 | tf_op jit(solution)/shard_map/reduce_scatter | solution.py:55
  397.5 25.6 %collective-permute-start.26 = (bf16[512,1024]{1,0:T(8,128)(2,1)S(1)}, bf16[512,1024]{1,0:T(8,128)(2,1)}, u32[]{:S(2)}, u32[]{:S(2)}) collective-permute-start(bf16[512,1024]{1,0:T(8,128)(2,1)S(1)} %add_convert_fusion.3), channel_id=1, source_target_pairs={{0,2},{2,0},{4,6},{6,4},{8,10},{10,8},{12,14},{14,12},{16,18},{18,... | collective-permute-start | bytes 3145736 | tf_op jit(solution)/shard_map/ppermute | solution.py:34
  443.0 120.3 %reduce-scatter.11.cloned.1.call-start = ((), (), s32[]{:S(2)}) async-start(), calls=%async_computation.12 | async-start | bytes 2654208 | tf_op jit(solution)/shard_map/reduce_scatter | solution.py:55
  443.1 25.6 %collective-permute-start.29 = (bf16[512,1024]{1,0:T(8,128)(2,1)S(1)}, bf16[512,1024]{1,0:T(8,128)(2,1)S(1)}, u32[]{:S(2)}, u32[]{:S(2)}) collective-permute-start(bf16[512,1024]{1,0:T(8,128)(2,1)S(1)} %get-tuple-element.243.e0.refs_0_), channel_id=1, source_target_pairs={{0,2},{2,0},{4,6},{6,4},{8,10},{10,8},{12,14},{14,12},{16,18},{18,... | collective-permute-start | bytes 3145736 | tf_op jit(solution)/shard_map/ppermute | solution.py:34
  491.2 34.1 %collective-permute-start.31 = (bf16[512,1024]{1,0:T(8,128)(2,1)}, bf16[512,1024]{1,0:T(8,128)(2,1)}, u32[]{:S(2)}, u32[]{:S(2)}) collective-permute-start(bf16[512,1024]{1,0:T(8,128)(2,1)} %get-tuple-element.154), channel_id=1, source_target_pairs={{0,1},{1,0},{2,3},{3,2},{4,5},{5,4},{6,7},{7,6},{8,9},{9,8},{10,11... | collective-permute-start | bytes 3145736 | tf_op jit(solution)/shard_map/ppermute | solution.py:29
  495.0 30.3 %collective-permute-start.33 = (bf16[512,1024]{1,0:T(8,128)(2,1)}, bf16[512,1024]{1,0:T(8,128)(2,1)}, u32[]{:S(2)}, u32[]{:S(2)}) collective-permute-start(bf16[512,1024]{1,0:T(8,128)(2,1)} %add_convert_fusion.1), channel_id=1, source_target_pairs={{0,2},{2,0},{4,6},{6,4},{8,10},{10,8},{12,14},{14,12},{16,18},{18,... | collective-permute-start | bytes 3145736 | tf_op jit(solution)/shard_map/ppermute | solution.py:34
  528.7 98.7 %reduce-scatter.17.cloned.1.call-start = ((), (), s32[]{:S(2)}) async-start(), calls=%async_computation.15 | async-start | bytes 5308416 | tf_op jit(solution)/shard_map/reduce_scatter | solution.py:55
  532.2 139.1 %reduce-scatter.15.cloned.1.call-start = ((), (), s32[]{:S(2)}) async-start(), calls=%async_computation.14 | async-start | bytes 5013504 | tf_op jit(solution)/shard_map/reduce_scatter | solution.py:55
  600.3 9.5 %collective-permute-start.41 = (bf16[64,2304]{1,0:T(8,128)(2,1)S(1)}, bf16[64,2304]{1,0:T(8,128)(2,1)S(1)}, u32[]{:S(2)}, u32[]{:S(2)}) collective-permute-start(bf16[64,2304]{1,0:T(8,128)(2,1)S(1)} %get-tuple-element.272), channel_id=1, source_target_pairs={{0,2},{2,0},{4,6},{6,4},{8,10},{10,8},{12,14},{14,12},{16,18},{18,... | collective-permute-start | bytes 884744 | tf_op jit(solution)/shard_map/ppermute | solution.py:34
  672.3 8.5 %collective-permute-start.36 = (bf16[64,2176]{1,0:T(8,128)(2,1)S(1)}, bf16[64,2176]{1,0:T(8,128)(2,1)S(1)}, u32[]{:S(2)}, u32[]{:S(2)}) collective-permute-start(bf16[64,2176]{1,0:T(8,128)(2,1)S(1)} %broadcast_select_fusion.14), channel_id=1, source_target_pairs={{0,2},{2,0},{4,6},{6,4},{8,10},{10,8},{12,14},{14,12},{16,18},{18,... | collective-permute-start | bytes 835592 | tf_op jit(solution)/shard_map/ppermute | solution.py:34
  (160 other events, 963.8 us)
Sparse Core Ops, SparseCore 0:
  21.4 51.8 all-gather.4
  75.5 74.9 all-gather.6
  152.5 38.3 all-gather.8
  192.3 74.6 all-gather.10
  378.0 33.4 reduce-scatter.6
  413.6 52.5 reduce-scatter.8
  468.5 38.6 reduce-scatter.12
  528.8 34.4 reduce-scatter.10
  565.6 52.4 reduce-scatter.16
  620.3 50.9 reduce-scatter.14

commit v3 on v2

--- a/solution.py
+++ b/solution.py
@@ -45,6 +45,16 @@
     x_bit = lax.axis_index("dp") % 2
     left, right = jnp.split(values, 2, axis=axis)
     return jnp.where(x_bit == 0, left, right), jnp.where(x_bit == 0, right, left)
+
+
+def between(mine, theirs):
+    x_bit = lax.axis_index("dp") % 2
+    count = lax.axis_size("dp") // 2
+    mine, theirs = (v.reshape(count, -1, v.shape[1]) for v in (mine, theirs))
+    pair = jnp.stack(
+        [jnp.where(x_bit == 0, mine, theirs), jnp.where(x_bit == 0, theirs, mine)], axis=1
+    )
+    return pair.reshape(-1, mine.shape[2])
 
 
 def ring_gather(pair):
@@ -81,7 +91,7 @@
 
 def params(steps=1):
     return pltpu.CompilerParams(
-        vmem_limit_bytes=48 * 2**20, dimension_semantics=("arbitrary",) * steps
+        vmem_limit_bytes=56 * 2**20, dimension_semantics=("arbitrary",) * steps
     )
 
 
@@ -101,131 +111,143 @@
     )
 
 
-def ff_up_kernel(h0, h1, wg, wu, gate_ref, up_ref, product_ref):
+def split_sums(i, product, keep_ref, send_ref):
+    @pl.when(i == 0)
+    def _():
+        keep_ref[...] = product
+
+    @pl.when(i == 1)
+    def _():
+        send_ref[...] = product.astype(BF)
+
+
+def dot_over_columns(left, right):
+    return lax.dot_general(left, right, (((1,), (1,)), ((), ())), preferred_element_type=F32)
+
+
+def pick(i, first, second, step):
+    pl.when(i == 0)(lambda: step(first))
+    pl.when(i == 1)(lambda: step(second))
+
+
+def lit_parts(gate):
+    sig = 1.0 / (1.0 + jnp.exp(-gate))
+    return sig, gate * sig
+
+
+def ff_ahead_kernel(h0, h1, w_both, w_down, both_ref, product_ref, keep_ref, send_ref):
     i = pl.program_id(0)
+    unit = w_down.shape[1]
 
     def step(h):
-        gate = jnp.dot(h[...], wg[...], preferred_element_type=F32)
-        up = jnp.dot(h[...], wu[...], preferred_element_type=F32)
-        gate_ref[...] = gate.astype(BF)
-        up_ref[...] = up.astype(BF)
-        product_ref[...] = (gate / (1.0 + jnp.exp(-gate)) * up).astype(BF)
-
-    pl.when(i == 0)(lambda: step(h0))
-    pl.when(i == 1)(lambda: step(h1))
-
-
-def ff_up(h0, h1, weights, cols):
-    rows, depth = h0.shape
-    out = jax.ShapeDtypeStruct((2 * rows, cols), BF)
-    tile = pl.BlockSpec((rows, cols), lambda i: (i, 0))
+        both = jnp.dot(h[...], w_both[...], preferred_element_type=F32)
+        both_ref[...] = both.astype(BF)
+        product = (lit_parts(both[:, :unit])[1] * both[:, unit:]).astype(BF)
+        product_ref[...] = product
+        split_sums(i, dot_over_columns(product, w_down[...]), keep_ref, send_ref)
+
+    pick(i, h0, h1, step)
+
+
+def ff_back_kernel(e0, e1, w_both, w_down, both_ref, dboth_ref, keep_ref, send_ref):
+    i = pl.program_id(0)
+    unit = w_down.shape[1]
+
+    def step(e):
+        grad = jnp.dot(e[...], w_down[...], preferred_element_type=F32)
+        sig, lit = lit_parts(both_ref[:, :unit].astype(F32))
+        dgate = (grad * both_ref[:, unit:].astype(F32) * (sig + lit - lit * sig)).astype(BF)
+        dboth = jnp.concatenate([dgate, (grad * lit).astype(BF)], axis=1)
+        dboth_ref[...] = dboth
+        split_sums(i, dot_over_columns(dboth, w_both[...]), keep_ref, send_ref)
+
+    pick(i, e0, e1, step)
+
+
+def ff_both_kernel(
+    h0, h1, e0, e1, w_both, w_down, product_ref, dboth_ref, keep_ref, send_ref, back_keep_ref, back_send_ref
+):
+    i = pl.program_id(0)
+    unit = w_down.shape[1]
+
+    def step(refs):
+        h, e = refs
+        both = jnp.dot(h[...], w_both[...], preferred_element_type=F32)
+        grad = jnp.dot(e[...], w_down[...], preferred_element_type=F32)
+        up = both[:, unit:]
+        sig, lit = lit_parts(both[:, :unit])
+        product = (lit * up).astype(BF)
+        product_ref[...] = product
+        dgate = (grad * up * (sig + lit - lit * sig)).astype(BF)
+        dboth = jnp.concatenate([dgate, (grad * lit).astype(BF)], axis=1)
+        dboth_ref[...] = dboth
+        split_sums(i, dot_over_columns(dboth, w_both[...]), back_keep_ref, back_send_ref)
+        split_sums(i, dot_over_columns(product, w_down[...]), keep_ref, send_ref)
+
+    pick(i, (h0, e0), (h1, e1), step)
+
+
+def ff_call(kernel, blocks, weights, unit, kept, out_cols, sums):
+    rows, depth = blocks[0].shape
+
+    def tile(cols):
+        return pl.BlockSpec((rows, cols), lambda i: (i, 0))
+
+    outs = [jax.ShapeDtypeStruct((2 * rows, cols), BF) for cols in out_cols]
+    ends = [jax.ShapeDtypeStruct((rows, depth), kind) for kind in (F32, BF)] * sums
     return pl.pallas_call(
-        ff_up_kernel,
+        kernel,
         grid=(2,),
-        out_shape=(out, out, out),
-        in_specs=[whole(h0), whole(h1), column(weights, cols, 0), column(weights, cols, 1)],
-        out_specs=(tile, tile, tile),
+        out_shape=[*outs, *ends],
+        in_specs=[whole(b) for b in blocks]
+        + [column(weights, 2 * unit, 0), column(weights, unit, 2)]
+        + [tile(k.shape[1]) for k in kept],
+        out_specs=[tile(cols) for cols in out_cols] + [pl.BlockSpec((rows, depth), lambda i: (0, 0))] * len(ends),
         compiler_params=params(),
-        cost_estimate=cost(8 * rows * depth * cols, h0, h1, out, out, out, out, out),
-    )(h0, h1, weights, weights)
-
-
-def ff_back_kernel(e0, e1, wd, gate_ref, up_ref, dgate_ref, dup_ref):
-    i = pl.program_id(0)
-
-    def step(e):
-        da = jnp.dot(e[...], wd[...], preferred_element_type=F32)
-        gate = gate_ref[...].astype(F32)
-        up = up_ref[...].astype(F32)
-        sig = 1.0 / (1.0 + jnp.exp(-gate))
-        lit = gate * sig
-        dup_ref[...] = (da * lit).astype(BF)
-        dgate_ref[...] = (da * up * (sig + lit - lit * sig)).astype(BF)
-
-    pl.when(i == 0)(lambda: step(e0))
-    pl.when(i == 1)(lambda: step(e1))
-
-
-def ff_back(e0, e1, weights, gate, up):
-    rows, depth = e0.shape
-    cols = gate.shape[1]
-    out = jax.ShapeDtypeStruct((2 * rows, cols), BF)
-    tile = pl.BlockSpec((rows, cols), lambda i: (i, 0))
-    return pl.pallas_call(
-        ff_back_kernel,
-        grid=(2,),
-        out_shape=(out, out),
-        in_specs=[whole(e0), whole(e1), column(weights, cols, 2), tile, tile],
-        out_specs=(tile, tile),
-        compiler_params=params(),
-        cost_estimate=cost(4 * rows * depth * cols, e0, e1, gate, gate, up, out, out),
-    )(e0, e1, weights, gate, up)
-
-
-def weight_grad_kernel(*refs):
-    left, right, out_ref = refs[:4], refs[4:-1], refs[-1]
-    rows = left[0].shape[0]
-    cols = right[0].shape[1]
-    turned = [l[...].T for l in left]
-    for k in range(len(right) // 2):
-        near, far = right[2 * k], right[2 * k + 1]
-        total = jnp.dot(turned[0], near[:rows], preferred_element_type=F32)
-        total += jnp.dot(turned[1], near[rows:], preferred_element_type=F32)
-        total += jnp.dot(turned[2], far[:rows], preferred_element_type=F32)
-        total += jnp.dot(turned[3], far[rows:], preferred_element_type=F32)
-        out_ref[:, k * cols : (k + 1) * cols] = total.astype(BF)
-
-
-def weight_grad(left, right):
+        cost_estimate=cost(6 * len(blocks) * rows * depth * unit, *blocks, *kept, *outs, *ends, weights),
+    )(*blocks, weights, weights, *kept)
+
+
+def ff_ahead(h0, h1, weights, unit):
+    both, product, *sums = ff_call(ff_ahead_kernel, (h0, h1), weights, unit, (), (2 * unit, unit), 1)
+    return both, product, sums
+
+
+def ff_back(e0, e1, weights, unit, both):
+    dboth, *sums = ff_call(ff_back_kernel, (e0, e1), weights, unit, (both,), (2 * unit,), 1)
+    return dboth, sums
+
+
+def ff_both(h0, h1, e0, e1, weights, unit):
+    product, dboth, *sums = ff_call(
+        ff_both_kernel, (h0, h1, e0, e1), weights, unit, (), (unit, 2 * unit), 2
+    )
+    return product, dboth, sums[:2], sums[2:]
+
+
+def weight_grad_kernel(l0, l1, l2, l3, near, far, out_ref):
+    rows = l0.shape[0]
+    total = jnp.dot(l0[...].T, near[:rows], preferred_element_type=F32)
+    total += jnp.dot(l1[...].T, near[rows:], preferred_element_type=F32)
+    total += jnp.dot(l2[...].T, far[:rows], preferred_element_type=F32)
+    total += jnp.dot(l3[...].T, far[rows:], preferred_element_type=F32)
+    out_ref[...] = total.astype(BF)
+
+
+def weight_grad(left, near, far):
     rows, depth = left[0].shape
     tile = 256
-    cols = right[0][0].shape[1] * len(right)
-    flat = [r for pair in right for r in pair]
+    cols = near.shape[1]
     out = jax.ShapeDtypeStruct((depth, cols), BF)
     return pl.pallas_call(
         weight_grad_kernel,
         grid=(depth // tile,),
         out_shape=out,
-        in_specs=[pl.BlockSpec((rows, tile), lambda i: (0, i))] * 4 + [whole(r) for r in flat],
+        in_specs=[pl.BlockSpec((rows, tile), lambda i: (0, i))] * 4 + [whole(near), whole(far)],
         out_specs=pl.BlockSpec((tile, cols), lambda i: (i, 0)),
         compiler_params=params(),
-        cost_estimate=cost(8 * rows * depth * cols, *left, *flat, out),
-    )(*left, *flat)
-
-
-def narrow_kernel(n, *refs):
-    left, right, keep_ref, send_ref = refs[:n], refs[n : 2 * n], refs[2 * n], refs[2 * n + 1]
-    rows = keep_ref.shape[0]
-
-    def total(part):
-        t = None
-        for l, r in zip(left, right):
-            v = lax.dot_general(l[part], r[...], (((1,), (1,)), ((), ())), preferred_element_type=F32)
-            t = v if t is None else t + v
-        return t
-
-    send_ref[...] = total(pl.ds(rows, rows)).astype(BF)
-    keep_ref[...] = total(pl.ds(0, rows))
-
-
-def narrow(left, weights, places):
-    rows, cols = left[0].shape
-    depth = weights.shape[0]
-    n = len(left)
-    tile = 256
-    keep = jax.ShapeDtypeStruct((rows // 2, depth), F32)
-    send = jax.ShapeDtypeStruct((rows // 2, depth), BF)
-    out = pl.BlockSpec((rows // 2, tile), lambda i: (0, i))
-    parts = [pl.BlockSpec((tile, cols), functools.partial(lambda at, i: (i, at), p)) for p in places]
-    return pl.pallas_call(
-        functools.partial(narrow_kernel, n),
-        grid=(depth // tile,),
-        out_shape=(keep, send),
-        in_specs=[whole(l) for l in left] + parts,
-        out_specs=(out, out),
-        compiler_params=params(),
-        cost_estimate=cost(2 * rows * depth * cols * n, *left, *left, keep, send),
-    )(*left, *[weights] * n)
+        cost_estimate=cost(8 * rows * depth * cols, *left, near, far, out),
+    )(*left, near, far)
 
 
 def turn_heads(values, cosine, sine):
@@ -509,19 +531,25 @@
         mine = jnp.concatenate([p[0] for p in parts], axis=1)
         return by_x(mine, flip_x(jnp.concatenate([p[1] for p in parts], axis=1)), 0)
 
-    own = jnp.concatenate([in_proj[:, 0], in_proj[:, 1], in_proj[:, 2], out_proj.T, misc], axis=1)
-    conv_w = ring_gather(by_x(own, flip_x(own), 0))
+    own = jnp.concatenate([misc, in_proj[:, 0], in_proj[:, 1], in_proj[:, 2], out_proj.T], axis=1)
+    conv_w = ring_gather(own)
+    in_w, w_out = conv_w[:, : 128 + 3 * conv_cols], conv_w[:, 128 + 3 * conv_cols :]
     ff_a = ring_gather(shared(gate_up_a, down_a))
     own = jnp.concatenate(
         [query_w, key_value_w[:, 0], key_value_w[:, 1], attn_out_w.T], axis=1
     )
-    attn_w = ring_gather(by_x(own, flip_x(own), 0))
-    ff_b = ring_gather(shared(gate_up_b, down_b))
+    attn_pair, ff_b_pair = by_x(own, flip_x(own), 0), shared(gate_up_b, down_b)
+    attn_w = ring_gather(attn_pair)
+    ff_b = ring_gather(ff_b_pair)
+    sent, _, _ = lax.optimization_barrier((in_w, attn_pair, ff_b_pair))
+    in_other = flip_x(sent)
+    sent, in_other = lax.optimization_barrier((w_out, in_other))
+    in_w = between(in_w, in_other)
+    out_other = flip_x(sent)
     w_qkv = attn_w[:, : query_cols + 2 * kv_cols]
     w_attn = attn_w[:, query_cols + 2 * kv_cols :]
-    w_in = [conv_w[:, k * conv_cols : (k + 1) * conv_cols] for k in range(3)]
-    w_out = conv_w[:, 3 * conv_cols : 4 * conv_cols]
-    misc_all = conv_w[:, 4 * conv_cols :]
+    w_in = [in_w[:, 128 + k * conv_cols : 128 + (k + 1) * conv_cols] for k in range(3)]
+    misc_all = in_w[:, :128]
 
     gain_rows = misc_all[:, :4].T.astype(F32)
     taps_all = ring_order(misc_all[:, 4:7].T, 1, back=True).astype(F32)
@@ -537,13 +565,12 @@
 
     hidden_zero = ring_order(tokens_in[0], 1).astype(F32)
     first_full = in_order(norm_low(hidden_zero, gain_rows[0]))
-    grad_blocks = four(ring_order(cotangent[0], 1))
-    first_full, grad_blocks = lax.optimization_barrier((first_full, grad_blocks))
     mixed = [dot_nn(first_full, w) for w in w_in]
     conv_out, conv_pull = jax.vjp(
         lambda mixed_in, kernel_in: conv_mix(mixed_in, kernel_in, same_one, same_two), mixed, kernel
     )
-    conv_low = conv_out.astype(BF)
+    conv_low, out_other = lax.optimization_barrier((conv_out.astype(BF), out_other))
+    w_out = between(w_out, out_other)
 
     def collect(own, other, w):
         sent = swap(dot_nt(other, w).astype(BF))
@@ -552,38 +579,44 @@
     hidden_one = hidden_zero + collect(own_half(conv_low), other_half(conv_low), w_out)
 
     def feed_forward(hidden, gain, weights):
-        blocks = four(norm_low(hidden, gain))
-        near = ff_up(blocks[0], blocks[1], weights, unit)
-        far = ff_up(blocks[2], blocks[3], weights, unit)
-        return blocks, near, far
-
-    def down(kept, weights):
-        return narrow([kept[1][2]], weights, [2]), narrow([kept[2][2]], weights, [2])
-
-    def feed_back(grad_out, grads, hidden, gain, weights, kept, settle):
+        own = norm_low(hidden, gain)
+        sibling, across = swap(own), flip_x(own)
+        near = ff_ahead(own, sibling, weights, unit)
+        near, across = lax.optimization_barrier((near, across))
+        blocks = own, sibling, across, swap(across)
+        far = ff_ahead(*blocks[2:], weights, unit)
+        return hidden + four_back(near[2], far[2]), (blocks, near, far)
+
+    def feed_back(grad_out, hidden, gain, weights, kept, settle):
         blocks, near, far = kept
-        if len(grads) == 1:
-            (own,) = grads
-            sibling, across = swap(own), flip_x(own)
-            near_back = ff_back(own, sibling, weights, near[0], near[1])
-            near_sum = narrow(near_back, weights, [0, 1])
-            near_sum, across = lax.optimization_barrier((near_sum, across))
-            grads = own, sibling, across, swap(across)
-        else:
-            near_back = ff_back(grads[0], grads[1], weights, near[0], near[1])
-            near_sum = narrow(near_back, weights, [0, 1])
-        far_in = grads[2:]
-        near_sum, far_in, settle = lax.optimization_barrier((near_sum, far_in, settle))
-        far_back = ff_back(*far_in, weights, far[0], far[1])
-        far_sum = narrow(far_back, weights, [0, 1])
-        g_down = weight_grad(grads, [(near[2], far[2])])
-        g_gate_up = weight_grad(
-            blocks, [(near_back[0], far_back[0]), (near_back[1], far_back[1])]
-        )
+        own = grad_out.astype(BF)
+        sibling, across = swap(own), flip_x(own)
+        near_back, near_sum = ff_back(own, sibling, weights, unit, near[0])
+        near_sum, across, settle = lax.optimization_barrier((near_sum, across, settle))
+        far_in = across, swap(across)
+        g_down = weight_grad([own, sibling, *far_in], near[1], far[1])
+        far_in, g_down = lax.optimization_barrier((far_in, g_down))
+        far_back, far_sum = ff_back(*far_in, weights, unit, far[0])
+        g_gate_up = weight_grad(blocks, near_back, far_back)
         grad_normed = four_back(near_sum, far_sum)
-        grad_normed, g_down, g_gate_up = lax.optimization_barrier((grad_normed, g_down, g_gate_up))
+        grad_normed, g_gate_up = lax.optimization_barrier((grad_normed, g_gate_up))
         grad_hidden, grad_gain = norm_back(grad_normed, hidden, gain, grad_out)
         return grad_hidden, grad_gain, ring_sum(g_gate_up), ring_sum(g_down), settle
+
+    def feed_both(hidden, gain, weights, grad_out, grads):
+        own = norm_low(hidden, gain)
+        sibling, across = swap(own), flip_x(own)
+        near, near_back, near_down, near_sum = ff_both(own, sibling, *grads[:2], weights, unit)
+        near_sum, across, grads_across = lax.optimization_barrier((near_sum, across, grads[2]))
+        grads = [*grads[:2], grads_across, swap(grads_across)]
+        blocks = own, sibling, across, swap(across)
+        far, far_back, far_down, far_sum = ff_both(*blocks[2:], *grads[2:], weights, unit)
+        g_down = weight_grad(grads, near, far)
+        g_gate_up = weight_grad(blocks, near_back, far_back)
+        grad_normed = four_back(near_sum, far_sum)
+        grad_normed, g_gate_up = lax.optimization_barrier((grad_normed, g_gate_up))
+        grad_hidden, grad_gain = norm_back(grad_normed, hidden, gain, grad_out)
+        return grad_hidden, grad_gain, ring_sum(g_gate_up), ring_sum(g_down), near_down, far_down
 
     def finish_shared(summed):
         mine, theirs = halves(summed, 0)
@@ -600,8 +633,7 @@
         up = by_x(mine[:, unit:], theirs[:, unit:], 1)
         return jnp.stack([gate, up], axis=1), by_x(*down, 1).T
 
-    kept_a = feed_forward(hidden_one, gain_rows[1], ff_a)
-    hidden_two = hidden_one + four_back(*down(kept_a, ff_a))
+    hidden_two, kept_a = feed_forward(hidden_one, gain_rows[1], ff_a)
 
     def my_part(full, other=False):
         start = (1 - rank if other else rank) * half
@@ -618,16 +650,17 @@
 
     third_full = in_order(norm_low(hidden_two, gain_rows[2]))
     qkv = to_heads(w_qkv, third_full)
+    grad_own, hidden_two = lax.optimization_barrier((ring_order(cotangent[0], 1), hidden_two))
+    grad_blocks = [grad_own, swap(grad_own), flip_x(grad_own)]
     query, keys, values, attended, logs = attend(doc_start, cosine, sine, qkv, query_cols, kv_cols)
+    attended, grad_blocks = lax.optimization_barrier((attended, grad_blocks))
     hidden_three = hidden_two + from_heads(attended, w_attn)
-    kept_b = feed_forward(hidden_three, gain_rows[3], ff_b)
 
     grad_four = ring_order(cotangent[0], 1).astype(F32)
-    grad_three, gain_grad_three, sum_gu_b, sum_dn_b, _ = feed_back(
-        grad_four, grad_blocks, hidden_three, gain_rows[3], ff_b, kept_b, ()
+    grad_three, gain_grad_three, sum_gu_b, sum_dn_b, near, far = feed_both(
+        hidden_three, gain_rows[3], ff_b, grad_four, grad_blocks
     )
     attn_full = in_order(grad_three.astype(BF))
-    near, far = down(kept_b, ff_b)
     far_sum = (far[0] + swap(far[1]).astype(F32)).astype(BF)
     grad_attended = to_heads(w_attn, attn_full).astype(BF)
     grad_attended, near, far_sum = lax.optimization_barrier((grad_attended, near, far_sum))
@@ -641,7 +674,6 @@
 
     grad_one, gain_grad_one, sum_gu_a, sum_dn_a, (sum_gu_b,) = feed_back(
         grad_two,
-        (grad_two.astype(BF),),
         hidden_one,
         gain_rows[1],
         ff_a,
@@ -649,10 +681,11 @@
         (sum_gu_b,),
     )
     conv_full = in_order(grad_one.astype(BF))
-    conv_full, sum_dn_a, sum_second = lax.optimization_barrier((conv_full, sum_dn_a, sum_second))
+    conv_full, sum_second = lax.optimization_barrier((conv_full, sum_second))
     grad_conv = dot_nn(conv_full, w_out)
     grad_mixed, grad_kernel = conv_pull(grad_conv)
     grad_mixed = [g.astype(BF) for g in grad_mixed]
+    grad_mixed, sum_dn_a = lax.optimization_barrier((grad_mixed, sum_dn_a))
     own_first = sum(dot_nt(own_half(g), w) for g, w in zip(grad_mixed, w_in))
     other_first = sum(dot_nt(other_half(g), w) for g, w in zip(grad_mixed, w_in))
     grad_first = own_first + swap(other_first.astype(BF)).astype(F32)

time: 701 us -> 630 us (0.90)
  waiting for transfers between devices: 219 us -> 177 us
  local copies, waits for them, and re-layouts: 86 us -> 68.6 us
  Pallas kernels: 241 us -> 226 us
  other arithmetic: 53.3 us -> 66 us
    reduce_scatter x6, waiting for transfers between devices: 51.6 us -> 20.2 us  [ring_sum(): lax.psum_scatter(grad, 'dp', scatter_dimension=0, axis_index_groups=ring_...]
    unnamed x326 -> x264, local copies, waits for them, and re-layouts: 60 us -> 39.4 us
    all_gather x4, waiting for transfers between devices: 21.3 us -> 1.2 us  [ring_gather(): lax.all_gather(pair, 'dp', axis=0, axis_index_groups=ring_groups(), tiled...]
    pallas_call x16 -> x6, Pallas kernels: 131 us -> 113 us  [ff_call(): pl.pallas_call(kernel, grid=(2,), out_shape=[*outs, *ends], in_specs=[who...]
    ppermute x25, waiting for transfers between devices: 17 us -> 29 us  [swap(): return lax.ppermute(values, 'tensor', [(0, 1), (1, 0)])]
    ppermute x18 -> x19, starting transfers between devices: 23.8 us -> 21.4 us  [flip_x(): return lax.ppermute(values, 'dp', [(i, i ^ 1) for i in range(n)])]
    ppermute x18 -> x19, waiting for transfers between devices: 129 us -> 127 us  [flip_x(): return lax.ppermute(values, 'dp', [(i, i ^ 1) for i in range(n)])]
  transfers between devices with their start and end apart: 53 -> 54, of which waited for: 27 -> 31; matrix products, arithmetic and copies ran while one was open for 20% -> 24% of each run, Pallas kernels for 31% -> 30%
where the time goes in v3:
time: 630 us; the launch traced here: 624 us
  Pallas kernels  226 us (36%)
  waiting for transfers between devices  177 us (28%)
  local copies, waits for them, and re-layouts  68.6 us (11%)
  other arithmetic  66 us (10%)
  matrix products  42.1 us (7%)
  starting transfers between devices  27.2 us (4%)
  between operations  16.2 us (3%)
    ppermute x19, waiting for transfers between devices, flip_x(): return lax.ppermute(values, 'dp', [(i, i ^ 1) for i in range(n)])  127 us
    pallas_call x6, Pallas kernels, ff_call(): pl.pallas_call(kernel, grid=(2,), out_shape=[*outs, *ends], in_specs=[who...  113 us
    pallas_call x4, Pallas kernels, weight_grad(): pl.pallas_call(weight_grad_kernel, grid=(depth // tile,), out_shape=out,...  51.8 us
    unnamed x264, local copies, waits for them, and re-layouts  39.4 us
    ppermute x25, waiting for transfers between devices, swap(): return lax.ppermute(values, 'tensor', [(0, 1), (1, 0)])  29 us
    pallas_call x1, Pallas kernels, attend_back(): pl.pallas_call(functools.partial(attend_back_kernel, min(256, length)), g...  23.1 us
    ppermute x19, starting transfers between devices, flip_x(): return lax.ppermute(values, 'dp', [(i, i ^ 1) for i in range(n)])  21.4 us
    pallas_call x1, Pallas kernels, attend(): pl.pallas_call(functools.partial(attend_kernel, min(256, length)), grid=(...  21 us
  transfers between devices with their start and end apart: 54, of which 31 were waited for; matrix products, arithmetic and copies ran while one was open for 24% of the time, Pallas kernels for 30%

profile of v3, /device:TPU:0, one launch (start us, length us, event | category | flops | bytes accessed | tf_op | source)
XLA Modules:
  0.0 624.1 jit_solution(11134695613327538940)
XLA Ops:
  15.6 10.2 %collective-permute-done.7 = bf16[64,3456]{1,0:T(8,128)(2,1)S(1)} collective-permute-done((bf16[64,3456]{1,0:T(8,128)(2,1)S(1)}, bf16[64,3456]{1,0:T(8,128)(2,1)S(1)}, u32[]{:S(2)}, u32[]{:S(2)}) %collective-permute-start.7) | collective-permute-done | bytes 442400 | tf_op jit(solution)/shard_map/ppermute | solution.py:34
  31.4 12.6 %collective-permute-done = bf16[64,1536]{1,0:T(8,128)(2,1)} collective-permute-done((bf16[64,1536]{1,0:T(8,128)(2,1)}, bf16[64,1536]{1,0:T(8,128)(2,1)}, u32[]{:S(2)}, u32[]{:S(2)}) %collective-permute-start) | collective-permute-done | bytes 196640 | tf_op jit(solution)/shard_map/ppermute | solution.py:34
  59.2 28.4 %collective-permute-done.2 = bf16[512,1664]{1,0:T(8,128)(2,1)} collective-permute-done((bf16[512,1664]{1,0:T(8,128)(2,1)}, bf16[512,1664]{1,0:T(8,128)(2,1)}, u32[]{:S(2)}, u32[]{:S(2)}) %collective-permute-start.2) | collective-permute-done | bytes 1703968 | tf_op jit(solution)/shard_map/ppermute | solution.py:34
  112.8 4.7 multiply_convert_fusion.6
  131.1 14.8 %shard_map.237 = (bf16[1024,2304]{1,0:T(8,128)(2,1)}, bf16[1024,1152]{1,0:T(8,128)(2,1)}, f32[512,1024]{1,0:T(8,128)}, bf16[512,1024]{1,0:T(8,128)(2,1)}) custom-call(bf16[512,1024]{1,0:T(8,128)(2,1)} %copy-done.59, bf16[512,1024]{1,0:T(8,128)(2,1)} %copy-done.98, bf16[1024,3456]{1,0:T(8,128)(2,1)} %all-gather.7.cloned.1.call-done.w_both.w_down, ...), custom_call_target="tpu_custom_call" | custom-call | flops 7247757312 | bytes 19398656 | tf_op jit(solution)/shard_map/pallas_call | solution.py:198
  145.9 7.1 %collective-permute-done.8.h0.l2 = bf16[512,1024]{1,0:T(8,128)(2,1)S(1)} collective-permute-done((bf16[512,1024]{1,0:T(8,128)(2,1)S(1)}, bf16[512,1024]{1,0:T(8,128)(2,1)S(1)}, u32[]{:S(2)}, u32[]{:S(2)}) %collective-permute-start.8) | collective-permute-done | bytes 1048608 | tf_op jit(solution)/shard_map/ppermute | solution.py:34
  156.7 15.2 %shard_map.238 = (bf16[1024,2304]{1,0:T(8,128)(2,1)}, bf16[1024,1152]{1,0:T(8,128)(2,1)}, f32[512,1024]{1,0:T(8,128)}, bf16[512,1024]{1,0:T(8,128)(2,1)}) custom-call(bf16[512,1024]{1,0:T(8,128)(2,1)} %copy-done.99, bf16[512,1024]{1,0:T(8,128)(2,1)} %copy-done.100, bf16[1024,3456]{1,0:T(8,128)(2,1)} %all-gather.7.cloned.1.call-done.w_both.w_down, ...), custom_call_target="tpu_custom_call" | custom-call | flops 7247757312 | bytes 19398656 | tf_op jit(solution)/shard_map/pallas_call | solution.py:198
  177.9 24.8 %collective-permute-done.12 = bf16[512,1024]{1,0:T(8,128)(2,1)S(1)} collective-permute-done((bf16[512,1024]{1,0:T(8,128)(2,1)S(1)}, bf16[512,1024]{1,0:T(8,128)(2,1)S(1)}, u32[]{:S(2)}, u32[]{:S(2)}) %collective-permute-start.12) | collective-permute-done | bytes 1048608 | tf_op jit(solution)/shard_map/ppermute | solution.py:34
  208.0 6.6 %fusion.13.q_ref.k_ref.v_ref = f32[1024,1024]{1,0:T(8,128)} fusion(bf16[1024,1536]{1,0:T(8,128)(2,1)} %all-gather.9.cloned.1.call-done, bf16[512,1024]{1,0:T(8,128)(2,1)} %get-tuple-element.262, bf16[512,1024]{1,0:T(8,128)(2,1)} %get-tuple-element.261), kind=kOutput, calls=%fused_computation.68 | convolution fusion | flops 2151677952 | bytes 8388608 | tf_op jit(solution)/shard_map/dot_general | solution.py:649
  214.6 21.0 %shard_map.239 = (bf16[512,1024]{1,0:T(8,128)(2,1)}, bf16[256,1024]{1,0:T(8,128)(2,1)}, bf16[256,1024]{1,0:T(8,128)(2,1)}, bf16[512,1024]{1,0:T(8,128)(2,1)}, f32[4,2,1024]{2,1,0:T(2,128)}) custom-call(s32[1,1024]{1,0:T(1,128)} %bitcast.129, f32[32,1024]{1,0:T(8,128)} %get-tuple-element.321.cos_ref, f32[32,1024]{1,0:T(8,128)} %get-tuple-element.320.sin_ref, ...), custom_call_target="tpu_custom_call" | custom-call | flops 1073741824 | bytes 8388608 | tf_op jit(solution)/shard_map/pallas_call | solution.py:300
  245.7 25.7 %shard_map.240 = (bf16[1024,1152]{1,0:T(8,128)(2,1)}, bf16[1024,2304]{1,0:T(8,128)(2,1)}, f32[512,1024]{1,0:T(8,128)}, bf16[512,1024]{1,0:T(8,128)(2,1)}, f32[51...) custom-call(bf16[512,1024]{1,0:T(8,128)(2,1)} %copy-done.60, bf16[512,1024]{1,0:T(8,128)(2,1)} %collective-permute-done.17.h1.l1, ...), custom_call_target="tpu_custom_call" | custom-call | flops 14495514624 | bytes 24641536 | tf_op jit(solution)/shard_map/pallas_call | solution.py:198
  276.8 26.2 %shard_map.241 = (bf16[1024,1152]{1,0:T(8,128)(2,1)}, bf16[1024,2304]{1,0:T(8,128)(2,1)}, f32[512,1024]{1,0:T(8,128)}, bf16[512,1024]{1,0:T(8,128)(2,1)}, f32[51...) custom-call(bf16[512,1024]{1,0:T(8,128)(2,1)} %collective-permute-done.18.h0.l2, bf16[512,1024]{1,0:T(8,128)(2,1)} %copy-done.102, ...), custom_call_target="tpu_custom_call" | custom-call | flops 14495514624 | bytes 24641536 | tf_op jit(solution)/shard_map/pallas_call | solution.py:198
  303.1 9.9 %shard_map.244 = bf16[1024,1152]{1,0:T(8,128)(2,1)} custom-call(bf16[512,1024]{1,0:T(8,128)(2,1)} %copy-done.31, bf16[512,1024]{1,0:T(8,128)(2,1)} %collective-permute-done.14.e1.l1, bf16[512,1024]{1,0:T(8,128)(2,1)} %collective-permute-done.15.e0.l2, bf16[512,1024]{1,0:T(8,128)(2,1)} %copy-done.107, bf16[1024,1152]{1,0:T(8,128)(2,1)} %get-tuple-element.140.near, ...), custom_call_target="tpu_custom_call" | custom-call | flops 4831838208 | bytes 11272192 | tf_op jit(solution)/shard_map/pallas_call | solution.py:242
  320.4 15.8 %shard_map.242 = bf16[1024,2304]{1,0:T(8,128)(2,1)} custom-call(bf16[512,1024]{1,0:T(8,128)(2,1)} %copy-done.60, bf16[512,1024]{1,0:T(8,128)(2,1)} %collective-permute-done.17.h1.l1, bf16[512,1024]{1,0:T(8,128)(2,1)} %collective-permute-done.18.h0.l2, bf16[512,1024]{1,0:T(8,128)(2,1)} %copy-done.102, bf16[1024,2304]{1,0:T(8,128)(2,1)} %get-tuple-element.122.near, ...), custom_call_target="tpu_custom_call" | custom-call | flops 9663676416 | bytes 18350080 | tf_op jit(solution)/shard_map/pallas_call | solution.py:242
  336.3 8.3 %collective-permute-done.23 = bf16[512,1024]{1,0:T(8,128)(2,1)} collective-permute-done((bf16[512,1024]{1,0:T(8,128)(2,1)}, bf16[512,1024]{1,0:T(8,128)(2,1)}, u32[]{:S(2)}, u32[]{:S(2)}) %collective-permute-start.23) | collective-permute-done | bytes 1048608 | tf_op jit(solution)/shard_map/ppermute | solution.py:34
  344.6 3.9 convert_add_fusion.4
  355.7 3.7 convolution_convert_fusion.do_ref
  364.0 23.1 %shard_map.243 = (bf16[512,1024]{1,0:T(8,128)(2,1)}, bf16[256,1024]{1,0:T(8,128)(2,1)}, bf16[256,1024]{1,0:T(8,128)(2,1)}) custom-call(s32[1,1024]{1,0:T(1,128)} %bitcast.130, f32[32,1024]{1,0:T(8,128)} %get-tuple-element.321.cos_ref, f32[32,1024]{1,0:T(8,128)} %get-tuple-element.320.sin_ref, bf16[512,1024]{1,0:T(8,128)(2,1)} %get-tuple-element.131.q_ref, ...), custom_call_target="tpu_custom_call" | custom-call | flops 3221225472 | bytes 4194304 | tf_op jit(solution)/shard_map/pallas_call | solution.py:366
  387.1 7.8 %shard_map.249 = bf16[1024,1536]{1,0:T(8,128)(2,1)} custom-call(bf16[1024,1024]{1,0:T(8,128)(2,1)} %pad_maximum_fusion.2.refs_0_, bf16[1024,1024]{1,0:T(8,128)(2,1)} %pad_maximum_fusion.3.refs_1_, bf16[512,1024]{1,0:T(8,128)(2,1)} %get-tuple-element.143.refs_2_, bf16[256,1024]{1,0:T(8,128)(2,1)} %get-tuple-element.144.refs_3_, ...), custom_call_target="tpu_custom_call" | custom-call | flops 3221225472 | bytes 10485760 | tf_op jit(solution)/shard_map/pallas_call | solution.py:405
  403.3 4.0 fusion.69
  411.0 15.3 %shard_map.245 = (bf16[1024,2304]{1,0:T(8,128)(2,1)}, f32[512,1024]{1,0:T(8,128)}, bf16[512,1024]{1,0:T(8,128)(2,1)}) custom-call(bf16[512,1024]{1,0:T(8,128)(2,1)} %copy-done.54, bf16[512,1024]{1,0:T(8,128)(2,1)} %copy-done.105, bf16[1024,3456]{1,0:T(8,128)(2,1)} %all-gather.7.cloned.1.call-done.w_both.w_down, ...), custom_call_target="tpu_custom_call" | custom-call | flops 7247757312 | bytes 21757952 | tf_op jit(solution)/shard_map/pallas_call | solution.py:198
  426.3 6.7 %collective-permute-done.30.l2.e0 = bf16[512,1024]{1,0:T(8,128)(2,1)S(1)} collective-permute-done((bf16[512,1024]{1,0:T(8,128)(2,1)S(1)}, bf16[512,1024]{1,0:T(8,128)(2,1)S(1)}, u32[]{:S(2)}, u32[]{:S(2)}) %collective-permute-start.30) | collective-permute-done | bytes 1048608 | tf_op jit(solution)/shard_map/ppermute | solution.py:34
  436.6 10.0 %shard_map.246 = bf16[1024,1152]{1,0:T(8,128)(2,1)} custom-call(bf16[512,1024]{1,0:T(8,128)(2,1)} %copy-done.54, bf16[512,1024]{1,0:T(8,128)(2,1)} %copy-done.105, bf16[512,1024]{1,0:T(8,128)(2,1)} %copy-done.104, bf16[512,1024]{1,0:T(8,128)(2,1)} %copy-done.106, bf16[1024,1152]{1,0:T(8,128)(2,1)} %get-tuple-element.153.near, ...), custom_call_target="tpu_custom_call" | custom-call | flops 4831838208 | bytes 11272192 | tf_op jit(solution)/shard_map/pallas_call | solution.py:242
  446.7 15.9 %shard_map.247 = (bf16[1024,2304]{1,0:T(8,128)(2,1)}, f32[512,1024]{1,0:T(8,128)}, bf16[512,1024]{1,0:T(8,128)(2,1)}) custom-call(bf16[512,1024]{1,0:T(8,128)(2,1)} %copy-done.104, bf16[512,1024]{1,0:T(8,128)(2,1)} %copy-done.106, bf16[1024,3456]{1,0:T(8,128)(2,1)} %all-gather.7.cloned.1.call-done.w_both.w_down, ...), custom_call_target="tpu_custom_call" | custom-call | flops 7247757312 | bytes 21757952 | tf_op jit(solution)/shard_map/pallas_call | solution.py:198
  472.1 16.1 %shard_map.248 = bf16[1024,2304]{1,0:T(8,128)(2,1)} custom-call(bf16[512,1024]{1,0:T(8,128)(2,1)} %copy-done.59, bf16[512,1024]{1,0:T(8,128)(2,1)} %copy-done.98, bf16[512,1024]{1,0:T(8,128)(2,1)} %copy-done.99, bf16[512,1024]{1,0:T(8,128)(2,1)} %copy-done.100, bf16[1024,2304]{1,0:T(8,128)(2,1)} %get-tuple-element.160.near, ...), custom_call_target="tpu_custom_call" | custom-call | flops 9663676416 | bytes 18350080 | tf_op jit(solution)/shard_map/pallas_call | solution.py:242
  488.2 6.0 collective-permute-done.34
  530.5 3.8 fusion.6
  537.0 9.6 %shard_map.250 = bf16[1024,2176]{1,0:T(8,128)(2,1)} custom-call(bf16[1024,1024]{1,0:T(8,128)(2,1)} %pad_maximum_fusion.1.left0, bf16[1024,1024]{1,0:T(8,128)(2,1)} %pad_maximum_fusion.4.left1, bf16[1024,512]{1,0:T(8,128)(2,1)} %multiply_convert_fusion.2.g0, bf16[1024,512]{1,0:T(8,128)(2,1)} %get-tuple-element.166.g1, ...), custom_call_target="tpu_custom_call" | custom-call | flops 4294967296 | bytes 12845056 | tf_op jit(solution)/shard_map/pallas_call | solution.py:434
  551.5 5.5 collective-permute-done.42
  580.1 3.8 collective-permute-done.39
  584.2 20.2 %reduce-scatter.15.cloned.1.call-done = bf16[128,2176]{1,0:T(8,128)(2,1)} async-done(((bf16[1024,2176]{1,0:T(8,128)(2,1)}), bf16[128,2176]{1,0:T(8,128)(2,1)}) %reduce-scatter.15.cloned.1.call-update) | async-done | bytes 557072 | tf_op jit(solution)/shard_map/reduce_scatter | solution.py:65
  609.0 5.0 collective-permute-done.37
  (516 shorter events, 216.4 us)
Async XLA Ops:
  7.2 40.9 %all-gather.5.cloned.1.call-start = ((), (), s32[]{:S(2)}) async-start(), calls=%async_computation.6 | async-start | bytes 2506752 | tf_op jit(solution)/shard_map/all_gather | solution.py:61
  11.5 118.6 %all-gather.7.cloned.1.call-start = ((), (), s32[]{:S(2)}) async-start(), calls=%async_computation.7 | async-start | bytes 7962624 | tf_op jit(solution)/shard_map/all_gather | solution.py:61
  12.6 13.2 %collective-permute-start.7 = (bf16[64,3456]{1,0:T(8,128)(2,1)S(1)}, bf16[64,3456]{1,0:T(8,128)(2,1)S(1)}, u32[]{:S(2)}, u32[]{:S(2)}) collective-permute-start(bf16[64,3456]{1,0:T(8,128)(2,1)S(1)} %pad_maximum_fusion.13), channel_id=1, source_target_pairs={{0,2},{2,0},{4,6},{6,4},{8,10},{10,8},{12,14},{14,12},{16,18},{18,... | collective-permute-start | bytes 1327112 | tf_op jit(solution)/shard_map/ppermute | solution.py:34
  27.0 181.0 %all-gather.9.cloned.1.call-start = ((), (), s32[]{:S(2)}) async-start(), calls=%async_computation.8 | async-start | bytes 3538944 | tf_op jit(solution)/shard_map/all_gather | solution.py:61
  28.2 17.6 %collective-permute-start.1 = (bf16[64,3456]{1,0:T(8,128)(2,1)S(1)}, bf16[64,3456]{1,0:T(8,128)(2,1)S(1)}, u32[]{:S(2)}, u32[]{:S(2)}) collective-permute-start(bf16[64,3456]{1,0:T(8,128)(2,1)S(1)} %pad_maximum_fusion.11), channel_id=1, source_target_pairs={{0,2},{2,0},{4,6},{6,4},{8,10},{10,8},{12,14},{14,12},{16,18},{18,... | collective-permute-start | bytes 1327112 | tf_op jit(solution)/shard_map/ppermute | solution.py:34
  30.8 13.2 %collective-permute-start = (bf16[64,1536]{1,0:T(8,128)(2,1)}, bf16[64,1536]{1,0:T(8,128)(2,1)}, u32[]{:S(2)}, u32[]{:S(2)}) collective-permute-start(bf16[64,1536]{1,0:T(8,128)(2,1)} %pad_maximum_fusion.15), channel_id=1, source_target_pairs={{0,2},{2,0},{4,6},{6,4},{8,10},{10,8},{12,14},{14,12},{16,18},{18,... | collective-permute-start | bytes 589832 | tf_op jit(solution)/shard_map/ppermute | solution.py:34
  50.9 36.7 %collective-permute-start.2 = (bf16[512,1664]{1,0:T(8,128)(2,1)}, bf16[512,1664]{1,0:T(8,128)(2,1)}, u32[]{:S(2)}, u32[]{:S(2)}) collective-permute-start(bf16[512,1664]{1,0:T(8,128)(2,1)} %slice.391), channel_id=1, source_target_pairs={{0,2},{2,0},{4,6},{6,4},{8,10},{10,8},{12,14},{14,12},{16,18},{18,... | collective-permute-start | bytes 5111816 | tf_op jit(solution)/shard_map/ppermute | solution.py:34
  57.8 186.7 %all-gather.11.cloned.1.call-start = ((), (), s32[]{:S(2)}) async-start(), calls=%async_computation.9 | async-start | bytes 7962624 | tf_op jit(solution)/shard_map/all_gather | solution.py:61
  94.2 12.5 %collective-permute-start.3 = (bf16[512,1024]{1,0:T(8,128)(2,1)}, bf16[512,1024]{1,0:T(8,128)(2,1)}, u32[]{:S(2)}, u32[]{:S(2)}) collective-permute-start(bf16[512,1024]{1,0:T(8,128)(2,1)} %fusion.2), channel_id=1, source_target_pairs={{0,1},{1,0},{2,3},{3,2},{4,5},{5,4},{6,7},{7,6},{8,9},{9,8},{10,11... | collective-permute-start | bytes 3145736 | tf_op jit(solution)/shard_map/ppermute | solution.py:29
  99.2 18.4 %collective-permute-start.4 = (bf16[512,512]{1,0:T(8,128)(2,1)}, bf16[512,512]{1,0:T(8,128)(2,1)S(1)}, u32[]{:S(2)}, u32[]{:S(2)}) collective-permute-start(bf16[512,512]{1,0:T(8,128)(2,1)} %slice.392), channel_id=1, source_target_pairs={{0,2},{2,0},{4,6},{6,4},{8,10},{10,8},{12,14},{14,12},{16,18},{18,... | collective-permute-start | bytes 1572872 | tf_op jit(solution)/shard_map/ppermute | solution.py:34
  121.2 265.9 %reduce-scatter.7.cloned.1.call-start = ((), (), s32[]{:S(2)}) async-start(), calls=%async_computation.10 | async-start | bytes 2654208 | tf_op jit(solution)/shard_map/reduce_scatter | solution.py:65
  127.7 25.3 %collective-permute-start.8 = (bf16[512,1024]{1,0:T(8,128)(2,1)S(1)}, bf16[512,1024]{1,0:T(8,128)(2,1)S(1)}, u32[]{:S(2)}, u32[]{:S(2)}) collective-permute-start(bf16[512,1024]{1,0:T(8,128)(2,1)S(1)} %multiply_convert_fusion.5.h0.l0), channel_id=1, source_target_pairs={{0,2},{2,0},{4,6},{6,4},{8,10},{10,8},{12,14},{14,12},{16,18},{18,... | collective-permute-start | bytes 3145736 | tf_op jit(solution)/shard_map/ppermute | solution.py:34
  177.4 25.3 %collective-permute-start.12 = (bf16[512,1024]{1,0:T(8,128)(2,1)S(1)}, bf16[512,1024]{1,0:T(8,128)(2,1)S(1)}, u32[]{:S(2)}, u32[]{:S(2)}) collective-permute-start(bf16[512,1024]{1,0:T(8,128)(2,1)S(1)} %add_convert_fusion.5), channel_id=1, source_target_pairs={{0,2},{2,0},{4,6},{6,4},{8,10},{10,8},{12,14},{14,12},{16,18},{18,... | collective-permute-start | bytes 3145736 | tf_op jit(solution)/shard_map/ppermute | solution.py:34
  203.7 31.9 %collective-permute-start.14 = (bf16[512,1024]{1,0:T(8,128)(2,1)S(1)}, bf16[512,1024]{1,0:T(8,128)(2,1)}, u32[]{:S(2)}, u32[]{:S(2)}) collective-permute-start(bf16[512,1024]{1,0:T(8,128)(2,1)S(1)} %slice_dynamic-update-slice_fusion.22.e0.l0), channel_id=1, source_target_pairs={{0,1},{1,0},{2,3},{3,2},{4,5},{5,4},{6,7},{7,6},{8,9},{9,8},{10,11... | collective-permute-start | bytes 3145736 | tf_op jit(solution)/shard_map/ppermute | solution.py:29
  204.3 31.4 %collective-permute-start.15 = (bf16[512,1024]{1,0:T(8,128)(2,1)S(1)}, bf16[512,1024]{1,0:T(8,128)(2,1)}, u32[]{:S(2)}, u32[]{:S(2)}) collective-permute-start(bf16[512,1024]{1,0:T(8,128)(2,1)S(1)} %slice_dynamic-update-slice_fusion.22.e0.l0), channel_id=1, source_target_pairs={{0,2},{2,0},{4,6},{6,4},{8,10},{10,8},{12,14},{14,12},{16,18},{18,... | collective-permute-start | bytes 3145736 | tf_op jit(solution)/shard_map/ppermute | solution.py:34
  243.0 28.3 %collective-permute-start.18 = (bf16[512,1024]{1,0:T(8,128)(2,1)S(1)}, bf16[512,1024]{1,0:T(8,128)(2,1)}, u32[]{:S(2)}, u32[]{:S(2)}) collective-permute-start(bf16[512,1024]{1,0:T(8,128)(2,1)S(1)} %multiply_convert_fusion.3.h0.l0), channel_id=1, source_target_pairs={{0,2},{2,0},{4,6},{6,4},{8,10},{10,8},{12,14},{14,12},{16,18},{18,... | collective-permute-start | bytes 3145736 | tf_op jit(solution)/shard_map/ppermute | solution.py:34
  313.0 119.9 %reduce-scatter.9.cloned.1.call-start = ((), (), s32[]{:S(2)}) async-start(), calls=%async_computation.11 | async-start | bytes 5308416 | tf_op jit(solution)/shard_map/reduce_scatter | solution.py:65
  313.3 23.0 %collective-permute-start.19 = (bf16[512,1024]{1,0:T(8,128)(2,1)}, bf16[512,1024]{1,0:T(8,128)(2,1)S(1)}, u32[]{:S(2)}, u32[]{:S(2)}) collective-permute-start(bf16[512,1024]{1,0:T(8,128)(2,1)} %get-tuple-element.117), channel_id=1, source_target_pairs={{0,1},{1,0},{2,3},{3,2},{4,5},{5,4},{6,7},{7,6},{8,9},{9,8},{10,11... | collective-permute-start | bytes 3145736 | tf_op jit(solution)/shard_map/ppermute | solution.py:29
  319.0 25.5 %collective-permute-start.23 = (bf16[512,1024]{1,0:T(8,128)(2,1)}, bf16[512,1024]{1,0:T(8,128)(2,1)}, u32[]{:S(2)}, u32[]{:S(2)}) collective-permute-start(bf16[512,1024]{1,0:T(8,128)(2,1)} %add_convert_fusion.4), channel_id=1, source_target_pairs={{0,2},{2,0},{4,6},{6,4},{8,10},{10,8},{12,14},{14,12},{16,18},{18,... | collective-permute-start | bytes 3145736 | tf_op jit(solution)/shard_map/ppermute | solution.py:34
  348.4 160.1 %reduce-scatter.11.cloned.1.call-start = ((), (), s32[]{:S(2)}) async-start(), calls=%async_computation.12 | async-start | bytes 3538944 | tf_op jit(solution)/shard_map/reduce_scatter | solution.py:65
  359.4 27.6 %collective-permute-start.27 = (bf16[512,1024]{1,0:T(8,128)(2,1)S(1)}, bf16[512,1024]{1,0:T(8,128)(2,1)}, u32[]{:S(2)}, u32[]{:S(2)}) collective-permute-start(bf16[512,1024]{1,0:T(8,128)(2,1)S(1)} %add_convert_fusion.3), channel_id=1, source_target_pairs={{0,2},{2,0},{4,6},{6,4},{8,10},{10,8},{12,14},{14,12},{16,18},{18,... | collective-permute-start | bytes 3145736 | tf_op jit(solution)/shard_map/ppermute | solution.py:34
  394.9 125.3 %reduce-scatter.13.cloned.1.call-start = ((), (), s32[]{:S(2)}) async-start(), calls=%async_computation.13 | async-start | bytes 2654208 | tf_op jit(solution)/shard_map/reduce_scatter | solution.py:65
  407.5 25.4 %collective-permute-start.30 = (bf16[512,1024]{1,0:T(8,128)(2,1)S(1)}, bf16[512,1024]{1,0:T(8,128)(2,1)S(1)}, u32[]{:S(2)}, u32[]{:S(2)}) collective-permute-start(bf16[512,1024]{1,0:T(8,128)(2,1)S(1)} %get-tuple-element.245.e0.l0), channel_id=1, source_target_pairs={{0,2},{2,0},{4,6},{6,4},{8,10},{10,8},{12,14},{14,12},{16,18},{18,... | collective-permute-start | bytes 3145736 | tf_op jit(solution)/shard_map/ppermute | solution.py:34
  446.6 129.4 %reduce-scatter.17.cloned.1.call-start = ((), (), s32[]{:S(2)}) async-start(), calls=%async_computation.15 | async-start | bytes 5308416 | tf_op jit(solution)/shard_map/reduce_scatter | solution.py:65
  465.3 6.7 %collective-permute-start.43 = (bf16[64,1152]{1,0:T(8,128)(2,1)S(1)}, bf16[64,1152]{1,0:T(8,128)(2,1)S(1)}, u32[]{:S(2)}, u32[]{:S(2)}) collective-permute-start(bf16[64,1152]{1,0:T(8,128)(2,1)S(1)} %broadcast_select_fusion.22), channel_id=1, source_target_pairs={{0,2},{2,0},{4,6},{6,4},{8,10},{10,8},{12,14},{14,12},{16,18},{18,... | collective-permute-start | bytes 442376 | tf_op jit(solution)/shard_map/ppermute | solution.py:34
  466.1 22.1 %collective-permute-start.31 = (bf16[512,1024]{1,0:T(8,128)(2,1)}, bf16[512,1024]{1,0:T(8,128)(2,1)}, u32[]{:S(2)}, u32[]{:S(2)}) collective-permute-start(bf16[512,1024]{1,0:T(8,128)(2,1)} %get-tuple-element.151), channel_id=1, source_target_pairs={{0,1},{1,0},{2,3},{3,2},{4,5},{5,4},{6,7},{7,6},{8,9},{9,8},{10,11... | collective-permute-start | bytes 3145736 | tf_op jit(solution)/shard_map/ppermute | solution.py:29
  467.6 26.6 %collective-permute-start.34 = (bf16[512,1024]{1,0:T(8,128)(2,1)}, bf16[512,1024]{1,0:T(8,128)(2,1)}, u32[]{:S(2)}, u32[]{:S(2)}) collective-permute-start(bf16[512,1024]{1,0:T(8,128)(2,1)} %add_convert_fusion.1), channel_id=1, source_target_pairs={{0,2},{2,0},{4,6},{6,4},{8,10},{10,8},{12,14},{14,12},{16,18},{18,... | collective-permute-start | bytes 3145736 | tf_op jit(solution)/shard_map/ppermute | solution.py:34
  497.6 106.8 %reduce-scatter.15.cloned.1.call-start = ((), (), s32[]{:S(2)}) async-start(), calls=%async_computation.14 | async-start | bytes 5013504 | tf_op jit(solution)/shard_map/reduce_scatter | solution.py:65
  547.7 9.3 %collective-permute-start.42 = (bf16[64,2304]{1,0:T(8,128)(2,1)S(1)}, bf16[64,2304]{1,0:T(8,128)(2,1)S(1)}, u32[]{:S(2)}, u32[]{:S(2)}) collective-permute-start(bf16[64,2304]{1,0:T(8,128)(2,1)S(1)} %get-tuple-element.278), channel_id=1, source_target_pairs={{0,2},{2,0},{4,6},{6,4},{8,10},{10,8},{12,14},{14,12},{16,18},{18,... | collective-permute-start | bytes 884744 | tf_op jit(solution)/shard_map/ppermute | solution.py:34
  558.0 6.4 %collective-permute-start.41 = (bf16[64,1536]{1,0:T(8,128)(2,1)S(1)}, bf16[64,1536]{1,0:T(8,128)(2,1)S(1)}, u32[]{:S(2)}, u32[]{:S(2)}) collective-permute-start(bf16[64,1536]{1,0:T(8,128)(2,1)S(1)} %broadcast_select_fusion.19), channel_id=1, source_target_pairs={{0,2},{2,0},{4,6},{6,4},{8,10},{10,8},{12,14},{14,12},{16,18},{18,... | collective-permute-start | bytes 589832 | tf_op jit(solution)/shard_map/ppermute | solution.py:34
  577.2 6.8 %collective-permute-start.39 = (bf16[64,2304]{1,0:T(8,128)(2,1)S(1)}, bf16[64,2304]{1,0:T(8,128)(2,1)S(1)}, u32[]{:S(2)}, u32[]{:S(2)}) collective-permute-start(bf16[64,2304]{1,0:T(8,128)(2,1)S(1)} %get-tuple-element.280), channel_id=1, source_target_pairs={{0,2},{2,0},{4,6},{6,4},{8,10},{10,8},{12,14},{14,12},{16,18},{18,... | collective-permute-start | bytes 884744 | tf_op jit(solution)/shard_map/ppermute | solution.py:34
  605.4 8.5 %collective-permute-start.37 = (bf16[64,2176]{1,0:T(8,128)(2,1)S(1)}, bf16[64,2176]{1,0:T(8,128)(2,1)S(1)}, u32[]{:S(2)}, u32[]{:S(2)}) collective-permute-start(bf16[64,2176]{1,0:T(8,128)(2,1)S(1)} %broadcast_select_fusion.18), channel_id=1, source_target_pairs={{0,2},{2,0},{4,6},{6,4},{8,10},{10,8},{12,14},{14,12},{16,18},{18,... | collective-permute-start | bytes 835592 | tf_op jit(solution)/shard_map/ppermute | solution.py:34
  (130 other events, 894.8 us)
Sparse Core Ops, SparseCore 0:
  11.6 36.5 all-gather.4
  49.7 73.9 all-gather.6
  125.8 38.3 all-gather.8
  165.5 74.6 all-gather.10
  313.2 35.0 reduce-scatter.6
  350.5 52.4 reduce-scatter.8
  405.3 38.7 reduce-scatter.10
  446.7 34.4 reduce-scatter.12
  497.7 53.4 reduce-scatter.16
  553.4 50.9 reduce-scatter.14

commit v4 on v3

--- a/solution.py
+++ b/solution.py
@@ -225,29 +225,36 @@
     return product, dboth, sums[:2], sums[2:]
 
 
-def weight_grad_kernel(l0, l1, l2, l3, near, far, out_ref):
+def weight_grad_kernel(l0, l1, l2, l3, near, far, *rest):
+    out_ref = rest[-1]
     rows = l0.shape[0]
     total = jnp.dot(l0[...].T, near[:rows], preferred_element_type=F32)
     total += jnp.dot(l1[...].T, near[rows:], preferred_element_type=F32)
     total += jnp.dot(l2[...].T, far[:rows], preferred_element_type=F32)
     total += jnp.dot(l3[...].T, far[rows:], preferred_element_type=F32)
-    out_ref[...] = total.astype(BF)
-
-
-def weight_grad(left, near, far):
+    out_ref[:, : total.shape[1]] = total.astype(BF)
+    if len(rest) > 1:
+        out_ref[:, total.shape[1] :] = rest[0][...]
+
+
+def weight_grad(left, near, far, flops_per_term=8, beside=None):
     rows, depth = left[0].shape
     tile = 256
     cols = near.shape[1]
-    out = jax.ShapeDtypeStruct((depth, cols), BF)
+    more = [] if beside is None else [beside]
+    width = cols + sum(m.shape[1] for m in more)
+    out = jax.ShapeDtypeStruct((depth, width), BF)
     return pl.pallas_call(
         weight_grad_kernel,
         grid=(depth // tile,),
         out_shape=out,
-        in_specs=[pl.BlockSpec((rows, tile), lambda i: (0, i))] * 4 + [whole(near), whole(far)],
-        out_specs=pl.BlockSpec((tile, cols), lambda i: (i, 0)),
+        in_specs=[pl.BlockSpec((rows, tile), lambda i: (0, i))] * 4
+        + [whole(near), whole(far)]
+        + [pl.BlockSpec((tile, m.shape[1]), lambda i: (i, 0)) for m in more],
+        out_specs=pl.BlockSpec((tile, width), lambda i: (i, 0)),
         compiler_params=params(),
-        cost_estimate=cost(8 * rows * depth * cols, *left, near, far, out),
-    )(*left, near, far)
+        cost_estimate=cost(flops_per_term * rows * depth * cols, out),
+    )(*left, near, far, *more)
 
 
 def turn_heads(values, cosine, sine):
@@ -413,7 +420,7 @@
     )(left0, left1, *rights)
 
 
-def first_grads_kernel(left0, left1, g0, g1, g2, low, small, out_ref):
+def first_grads_kernel(left0, left1, g0, g1, g2, low, extra, out_ref):
     cols = g0.shape[1]
     turned = left0[...].T
     for k, right in enumerate((g0, g1, g2)):
@@ -421,14 +428,14 @@
         out_ref[:, k * cols : (k + 1) * cols] = got.astype(BF)
     got = jnp.dot(left1[...].T, low[...], preferred_element_type=F32)
     out_ref[:, 3 * cols : 4 * cols] = got.astype(BF)
-    out_ref[:, 4 * cols :] = small[...]
-
-
-def first_grads(left0, rights, left1, low, small):
+    out_ref[:, 4 * cols :] = extra[...]
+
+
+def first_grads(left0, rights, left1, low, extra):
     length, depth = left0.shape
     tile = 256
     cols = low.shape[1]
-    width = 4 * cols + small.shape[1]
+    width = 4 * cols + extra.shape[1]
     out = jax.ShapeDtypeStruct((depth, width), BF)
     left = pl.BlockSpec((length, tile), lambda i: (0, i))
     return pl.pallas_call(
@@ -437,11 +444,11 @@
         out_shape=out,
         in_specs=[left, left]
         + [whole(r) for r in (*rights, low)]
-        + [pl.BlockSpec((tile, small.shape[1]), lambda i: (i, 0))],
+        + [pl.BlockSpec((tile, extra.shape[1]), lambda i: (i, 0))],
         out_specs=pl.BlockSpec((tile, width), lambda i: (i, 0)),
         compiler_params=params(),
         cost_estimate=cost(8 * length * depth * cols, left0, left1, *rights, low, out),
-    )(left0, left1, *rights, low, small)
+    )(left0, left1, *rights, low, extra)
 
 
 def inv_rms(values):
@@ -514,9 +521,14 @@
         far = flip_x(own)
         return own, swap(own), far, swap(far)
 
+    def far_total(far):
+        return (far[0] + swap(far[1]).astype(F32)).astype(BF)
+
+    def four_total(near, far_sum):
+        return near[0] + swap(near[1]).astype(F32) + flip_x(far_sum).astype(F32)
+
     def four_back(near, far):
-        far_sum = (far[0] + swap(far[1]).astype(F32)).astype(BF)
-        return near[0] + swap(near[1]).astype(F32) + flip_x(far_sum).astype(F32)
+        return four_total(near, far_total(far))
 
     misc = jnp.concatenate(
         [gains.T, taps.T, jnp.zeros((rows, 128 - gains.shape[0] - taps.shape[0]), BF)], axis=1
@@ -587,36 +599,41 @@
         far = ff_ahead(*blocks[2:], weights, unit)
         return hidden + four_back(near[2], far[2]), (blocks, near, far)
 
-    def feed_back(grad_out, hidden, gain, weights, kept, settle):
+    def feed_back(grad_out, hidden, gain, weights, kept, settle, other):
         blocks, near, far = kept
         own = grad_out.astype(BF)
         sibling, across = swap(own), flip_x(own)
         near_back, near_sum = ff_back(own, sibling, weights, unit, near[0])
-        near_sum, across, settle = lax.optimization_barrier((near_sum, across, settle))
+        inputs, near_sum = lax.optimization_barrier((other[1:], near_sum))
+        other = other[0](*inputs)
+        near_sum, across, settle, other = lax.optimization_barrier((near_sum, across, settle, other))
         far_in = across, swap(across)
-        g_down = weight_grad([own, sibling, *far_in], near[1], far[1])
-        far_in, g_down = lax.optimization_barrier((far_in, g_down))
         far_back, far_sum = ff_back(*far_in, weights, unit, far[0])
+        far_sum, far_back = lax.optimization_barrier((far_total(far_sum), far_back))
         g_gate_up = weight_grad(blocks, near_back, far_back)
-        grad_normed = four_back(near_sum, far_sum)
-        grad_normed, g_gate_up = lax.optimization_barrier((grad_normed, g_gate_up))
+        product, g_gate_up = lax.optimization_barrier((near[1], g_gate_up))
+        g_down = weight_grad([own, sibling, *far_in], product, far[1], 0)
+        grad_normed = four_total(near_sum, far_sum)
+        grad_normed, g_down = lax.optimization_barrier((grad_normed, g_down))
         grad_hidden, grad_gain = norm_back(grad_normed, hidden, gain, grad_out)
-        return grad_hidden, grad_gain, ring_sum(g_gate_up), ring_sum(g_down), settle
+        return grad_hidden, grad_gain, ring_sum(g_gate_up), g_down, settle, ring_sum(other)
 
     def feed_both(hidden, gain, weights, grad_out, grads):
         own = norm_low(hidden, gain)
         sibling, across = swap(own), flip_x(own)
         near, near_back, near_down, near_sum = ff_both(own, sibling, *grads[:2], weights, unit)
-        near_sum, across, grads_across = lax.optimization_barrier((near_sum, across, grads[2]))
-        grads = [*grads[:2], grads_across, swap(grads_across)]
+        near_sum, across = lax.optimization_barrier((near_sum, across))
         blocks = own, sibling, across, swap(across)
         far, far_back, far_down, far_sum = ff_both(*blocks[2:], *grads[2:], weights, unit)
-        g_down = weight_grad(grads, near, far)
+        far_sum, far = lax.optimization_barrier((far_total(far_sum), far))
         g_gate_up = weight_grad(blocks, near_back, far_back)
-        grad_normed = four_back(near_sum, far_sum)
-        grad_normed, g_gate_up = lax.optimization_barrier((grad_normed, g_gate_up))
+        near, g_gate_up = lax.optimization_barrier((near, g_gate_up))
+        grad_w = weight_grad(grads, near, far, 0, g_gate_up)
+        grad_normed = four_total(near_sum, far_sum)
+        grad_normed, grad_w = lax.optimization_barrier((grad_normed, grad_w))
         grad_hidden, grad_gain = norm_back(grad_normed, hidden, gain, grad_out)
-        return grad_hidden, grad_gain, ring_sum(g_gate_up), ring_sum(g_down), near_down, far_down
+        sums = ring_sum(grad_w)
+        return grad_hidden, grad_gain, sums, near_down, far_down
 
     def finish_shared(summed):
         mine, theirs = halves(summed, 0)
@@ -626,12 +643,19 @@
         mine, theirs = halves(summed, 0)
         return mine.astype(F32) + flip_x(theirs).astype(F32)
 
-    def finish_ff(g_gate_up, g_down):
-        down = finish_shared(g_down)
-        mine, theirs = finish_shared(g_gate_up)
+    def finish_all(summed):
+        mine, theirs = finish_shared(summed)
+        down, gate, up = (
+            by_x(mine[:, k * unit : (k + 1) * unit], theirs[:, k * unit : (k + 1) * unit], 1)
+            for k in range(3)
+        )
+        return jnp.stack([gate, up], axis=1), down.T
+
+    def finish_gate_up(summed):
+        mine, theirs = finish_shared(summed)
         gate = by_x(mine[:, :unit], theirs[:, :unit], 1)
         up = by_x(mine[:, unit:], theirs[:, unit:], 1)
-        return jnp.stack([gate, up], axis=1), by_x(*down, 1).T
+        return jnp.stack([gate, up], axis=1)
 
     hidden_two, kept_a = feed_forward(hidden_one, gain_rows[1], ff_a)
 
@@ -653,39 +677,42 @@
     grad_own, hidden_two = lax.optimization_barrier((ring_order(cotangent[0], 1), hidden_two))
     grad_blocks = [grad_own, swap(grad_own), flip_x(grad_own)]
     query, keys, values, attended, logs = attend(doc_start, cosine, sine, qkv, query_cols, kv_cols)
-    attended, grad_blocks = lax.optimization_barrier((attended, grad_blocks))
+    attended, grads_across = lax.optimization_barrier((attended, grad_blocks[2]))
+    grad_blocks = [*grad_blocks[:2], grads_across, swap(grads_across)]
     hidden_three = hidden_two + from_heads(attended, w_attn)
 
     grad_four = ring_order(cotangent[0], 1).astype(F32)
-    grad_three, gain_grad_three, sum_gu_b, sum_dn_b, near, far = feed_both(
+    grad_three, gain_grad_three, sum_b, near, far = feed_both(
         hidden_three, gain_rows[3], ff_b, grad_four, grad_blocks
     )
     attn_full = in_order(grad_three.astype(BF))
-    far_sum = (far[0] + swap(far[1]).astype(F32)).astype(BF)
+    far_sum = far_total(far)
     grad_attended = to_heads(w_attn, attn_full).astype(BF)
     grad_attended, near, far_sum = lax.optimization_barrier((grad_attended, near, far_sum))
     grad_qkv = attend_back(doc_start, cosine, sine, query, keys, values, logs, grad_attended)
-    grad_qkv, far_sum, sum_dn_b = lax.optimization_barrier((grad_qkv, flip_x(far_sum), sum_dn_b))
+    grad_qkv, far_sum = lax.optimization_barrier((grad_qkv, flip_x(far_sum)))
     hidden_four = hidden_three + (near[0] + swap(near[1]).astype(F32) + far_sum.astype(F32))
     output = ring_order(hidden_four.astype(BF), 1, back=True)[None]
     grad_third = from_heads(jnp.concatenate(grad_qkv, axis=0), w_qkv)
-    sum_second = ring_sum(second_grads(third_full, grad_qkv, attn_full, attended))
     grad_two, gain_grad_two = norm_back(grad_third, hidden_two, gain_rows[2], grad_three)
 
-    grad_one, gain_grad_one, sum_gu_a, sum_dn_a, (sum_gu_b,) = feed_back(
+    grad_one, gain_grad_one, sum_gu_a, g_down_a, (sum_b,), sum_second = feed_back(
         grad_two,
         hidden_one,
         gain_rows[1],
         ff_a,
         kept_a,
-        (sum_gu_b,),
+        (sum_b,),
+        (second_grads, third_full, grad_qkv, attn_full, attended),
     )
     conv_full = in_order(grad_one.astype(BF))
     conv_full, sum_second = lax.optimization_barrier((conv_full, sum_second))
     grad_conv = dot_nn(conv_full, w_out)
     grad_mixed, grad_kernel = conv_pull(grad_conv)
     grad_mixed = [g.astype(BF) for g in grad_mixed]
-    grad_mixed, sum_dn_a = lax.optimization_barrier((grad_mixed, sum_dn_a))
+    grad_first_w = first_grads(first_full, grad_mixed, conv_full, conv_low, g_down_a)
+    sum_conv = ring_sum(grad_first_w)
+    grad_mixed, sum_gu_a, _ = lax.optimization_barrier((grad_mixed, sum_gu_a, grad_first_w))
     own_first = sum(dot_nt(own_half(g), w) for g, w in zip(grad_mixed, w_in))
     other_first = sum(dot_nt(other_half(g), w) for g, w in zip(grad_mixed, w_in))
     grad_first = own_first + swap(other_first.astype(BF)).astype(F32)
@@ -698,23 +725,32 @@
     )
     small = jnp.concatenate(
         [
-            jnp.stack([gain_grad_zero, gain_grad_one, gain_grad_two, gain_grad_three]),
-            ring_order(kernel_full, 1),
-            jnp.zeros((128 - 7, width), F32),
+            ring_order(
+                jnp.stack([gain_grad_zero, gain_grad_one, gain_grad_two, gain_grad_three]), 1, back=True
+            ),
+            kernel_full,
+            jnp.zeros((1, width), F32),
         ],
         axis=0,
-    ).T.astype(BF)
-    grad_first_w = first_grads(first_full, grad_mixed, conv_full, conv_low, small)
-    summed_gu_b, summed_dn_b = finish_ff(sum_gu_b, sum_dn_b)
+    )
+    step, count = 1, lax.axis_size("dp")
+    small = small + swap(small)
+    while step < count:
+        small = small + lax.ppermute(small, "dp", [(i, i ^ step) for i in range(count)])
+        step *= 2
+    small_sum = lax.dynamic_slice_in_dim(small, lax.axis_index("dp") * rows, rows, 1)
+    sum_b, sum_second, sum_gu_a = lax.optimization_barrier((sum_b, sum_second, sum_gu_a))
+    summed_gu_b, summed_dn_b = finish_all(sum_b)
     summed_attn_w = finish(sum_second)
-    summed_gu_a, summed_dn_a = finish_ff(sum_gu_a, sum_dn_a)
-    summed_conv = finish(ring_sum(grad_first_w))
+    summed_gu_a = finish_gate_up(sum_gu_a)
+    mine, theirs = halves(sum_conv, 0)
+    mine, theirs = mine.astype(F32), flip_x(theirs).astype(F32)
+    summed_conv = mine[:, : 4 * conv_cols] + theirs[:, : 4 * conv_cols]
+    summed_dn_a = by_x(mine[:, 4 * conv_cols :], theirs[:, 4 * conv_cols :], 1).T
     summed_qkv = summed_attn_w[:, : query_cols + 2 * kv_cols]
     summed_attn = summed_attn_w[:, query_cols + 2 * kv_cols :].T
     summed_win = summed_conv[:, : 3 * conv_cols].reshape(rows, 3, conv_cols)
-    summed_wout = summed_conv[:, 3 * conv_cols : 4 * conv_cols].T
-    small_sum = summed_conv[:, 4 * conv_cols :]
-    small_sum = (small_sum + swap(small_sum)).T
+    summed_wout = summed_conv[:, 3 * conv_cols :].T
     return (
         output,
         grad_input,

time: 630 us -> 619 us (0.983)
  waiting for transfers between devices: 177 us -> 163 us
  local copies, waits for them, and re-layouts: 68.6 us -> 59.6 us
  other arithmetic: 66 us -> 72.5 us
    ppermute x19 -> x17, waiting for transfers between devices: 127 us -> 107 us  [flip_x(): return lax.ppermute(values, 'dp', [(i, i ^ 1) for i in range(n)])]
    ppermute x0 -> x4, waiting for transfers between devices: none -> 8.81 us  [per_device(): lax.ppermute(small, 'dp', [(i, i ^ step) for i in range(count)])]
    reduce_scatter x6 -> x4, waiting for transfers between devices: 20.2 us -> 17.6 us  [ring_sum(): lax.psum_scatter(grad, 'dp', scatter_dimension=0, axis_index_groups=ring_...]
    unnamed x264 -> x237, local copies, waits for them, and re-layouts: 39.4 us -> 37.1 us
    ppermute x19 -> x17, starting transfers between devices: 21.4 us -> 19.2 us  [flip_x(): return lax.ppermute(values, 'dp', [(i, i ^ 1) for i in range(n)])]
  transfers between devices with their start and end apart: 54 -> 54, of which waited for: 31 -> 30; matrix products, arithmetic and copies ran while one was open for 24% -> 24% of each run, Pallas kernels for 30% -> 33%
where the time goes in v4:
time: 619 us; the launch traced here: 613 us
  Pallas kernels  230 us (37%)
  waiting for transfers between devices  163 us (26%)
  other arithmetic  72.5 us (12%)
  local copies, waits for them, and re-layouts  59.6 us (10%)
  matrix products  43.3 us (7%)
  starting transfers between devices  29.5 us (5%)
  between operations  15.9 us (3%)
    pallas_call x6, Pallas kernels, ff_call(): pl.pallas_call(kernel, grid=(2,), out_shape=[*outs, *ends], in_specs=[who...  114 us
    ppermute x17, waiting for transfers between devices, flip_x(): return lax.ppermute(values, 'dp', [(i, i ^ 1) for i in range(n)])  107 us
    pallas_call x4, Pallas kernels, weight_grad(): pl.pallas_call(weight_grad_kernel, grid=(depth // tile,), out_shape=out,...  53.6 us
    unnamed x237, local copies, waits for them, and re-layouts  37.1 us
    ppermute x25, waiting for transfers between devices, swap(): return lax.ppermute(values, 'tensor', [(0, 1), (1, 0)])  27.5 us
    pallas_call x1, Pallas kernels, attend_back(): pl.pallas_call(functools.partial(attend_back_kernel, min(256, length)), g...  23.1 us
    pallas_call x1, Pallas kernels, attend(): pl.pallas_call(functools.partial(attend_kernel, min(256, length)), grid=(...  21 us
    ppermute x17, starting transfers between devices, flip_x(): return lax.ppermute(values, 'dp', [(i, i ^ 1) for i in range(n)])  19.2 us
  transfers between devices with their start and end apart: 54, of which 30 were waited for; matrix products, arithmetic and copies ran while one was open for 24% of the time, Pallas kernels for 33%

profile of v4, /device:TPU:0, one launch (start us, length us, event | category | flops | bytes accessed | tf_op | source)
XLA Modules:
  0.0 613.4 jit_solution(15872446770789463124)
XLA Ops:
  12.6 3.0 collective-permute-start.7
  15.6 10.2 %collective-permute-done.7 = bf16[64,3456]{1,0:T(8,128)(2,1)S(1)} collective-permute-done((bf16[64,3456]{1,0:T(8,128)(2,1)S(1)}, bf16[64,3456]{1,0:T(8,128)(2,1)S(1)}, u32[]{:S(2)}, u32[]{:S(2)}) %collective-permute-start.7) | collective-permute-done | bytes 442400 | tf_op jit(solution)/shard_map/ppermute | solution.py:34
  31.4 12.6 %collective-permute-done = bf16[64,1536]{1,0:T(8,128)(2,1)} collective-permute-done((bf16[64,1536]{1,0:T(8,128)(2,1)}, bf16[64,1536]{1,0:T(8,128)(2,1)}, u32[]{:S(2)}, u32[]{:S(2)}) %collective-permute-start) | collective-permute-done | bytes 196640 | tf_op jit(solution)/shard_map/ppermute | solution.py:34
  59.2 28.4 %collective-permute-done.2 = bf16[512,1664]{1,0:T(8,128)(2,1)} collective-permute-done((bf16[512,1664]{1,0:T(8,128)(2,1)}, bf16[512,1664]{1,0:T(8,128)(2,1)}, u32[]{:S(2)}, u32[]{:S(2)}) %collective-permute-start.2) | collective-permute-done | bytes 1703968 | tf_op jit(solution)/shard_map/ppermute | solution.py:34
  112.8 4.7 multiply_convert_fusion.6
  131.1 15.0 %shard_map.237 = (bf16[1024,2304]{1,0:T(8,128)(2,1)}, bf16[1024,1152]{1,0:T(8,128)(2,1)}, f32[512,1024]{1,0:T(8,128)}, bf16[512,1024]{1,0:T(8,128)(2,1)}) custom-call(bf16[512,1024]{1,0:T(8,128)(2,1)} %copy-done.55, bf16[512,1024]{1,0:T(8,128)(2,1)} %copy-done.91, bf16[1024,3456]{1,0:T(8,128)(2,1)} %all-gather.7.cloned.1.call-done.w_both.w_down, ...), custom_call_target="tpu_custom_call" | custom-call | flops 7247757312 | bytes 19398656 | tf_op jit(solution)/shard_map/pallas_call | solution.py:198
  146.1 6.9 %collective-permute-done.8.h0.l2 = bf16[512,1024]{1,0:T(8,128)(2,1)S(1)} collective-permute-done((bf16[512,1024]{1,0:T(8,128)(2,1)S(1)}, bf16[512,1024]{1,0:T(8,128)(2,1)S(1)}, u32[]{:S(2)}, u32[]{:S(2)}) %collective-permute-start.8) | collective-permute-done | bytes 1048608 | tf_op jit(solution)/shard_map/ppermute | solution.py:34
  156.6 15.3 %shard_map.238 = (bf16[1024,2304]{1,0:T(8,128)(2,1)}, bf16[1024,1152]{1,0:T(8,128)(2,1)}, f32[512,1024]{1,0:T(8,128)}, bf16[512,1024]{1,0:T(8,128)(2,1)}) custom-call(bf16[512,1024]{1,0:T(8,128)(2,1)} %copy-done.92, bf16[512,1024]{1,0:T(8,128)(2,1)} %copy-done.93, bf16[1024,3456]{1,0:T(8,128)(2,1)} %all-gather.7.cloned.1.call-done.w_both.w_down, ...), custom_call_target="tpu_custom_call" | custom-call | flops 7247757312 | bytes 19398656 | tf_op jit(solution)/shard_map/pallas_call | solution.py:198
  178.0 24.3 %collective-permute-done.12 = bf16[512,1024]{1,0:T(8,128)(2,1)S(1)} collective-permute-done((bf16[512,1024]{1,0:T(8,128)(2,1)S(1)}, bf16[512,1024]{1,0:T(8,128)(2,1)S(1)}, u32[]{:S(2)}, u32[]{:S(2)}) %collective-permute-start.12) | collective-permute-done | bytes 1048608 | tf_op jit(solution)/shard_map/ppermute | solution.py:34
  207.6 6.7 %fusion.13.q_ref.k_ref.v_ref = f32[1024,1024]{1,0:T(8,128)} fusion(bf16[1024,1536]{1,0:T(8,128)(2,1)} %all-gather.9.cloned.1.call-done, bf16[512,1024]{1,0:T(8,128)(2,1)} %get-tuple-element.288, bf16[512,1024]{1,0:T(8,128)(2,1)} %get-tuple-element.287), kind=kOutput, calls=%fused_computation.68 | convolution fusion | flops 2151677952 | bytes 8388608 | tf_op jit(solution)/shard_map/dot_general | solution.py:673
  214.3 21.0 %shard_map.239 = (bf16[512,1024]{1,0:T(8,128)(2,1)}, bf16[256,1024]{1,0:T(8,128)(2,1)}, bf16[256,1024]{1,0:T(8,128)(2,1)}, bf16[512,1024]{1,0:T(8,128)(2,1)}, f32[4,2,1024]{2,1,0:T(2,128)}) custom-call(s32[1,1024]{1,0:T(1,128)} %bitcast.156, f32[32,1024]{1,0:T(8,128)} %get-tuple-element.349.cos_ref, f32[32,1024]{1,0:T(8,128)} %get-tuple-element.348.sin_ref, ...), custom_call_target="tpu_custom_call" | custom-call | flops 1073741824 | bytes 8388608 | tf_op jit(solution)/shard_map/pallas_call | solution.py:307
  246.9 25.8 %shard_map.240 = (bf16[1024,1152]{1,0:T(8,128)(2,1)}, bf16[1024,2304]{1,0:T(8,128)(2,1)}, f32[512,1024]{1,0:T(8,128)}, bf16[512,1024]{1,0:T(8,128)(2,1)}, f32[51...) custom-call(bf16[512,1024]{1,0:T(8,128)(2,1)} %multiply_convert_fusion.3.h0.l0, ...), custom_call_target="tpu_custom_call" | custom-call | flops 14495514624 | bytes 24641536 | tf_op jit(solution)/shard_map/pallas_call | solution.py:198
  276.6 26.3 %shard_map.241 = (bf16[1024,1152]{1,0:T(8,128)(2,1)}, bf16[1024,2304]{1,0:T(8,128)(2,1)}, f32[512,1024]{1,0:T(8,128)}, bf16[512,1024]{1,0:T(8,128)(2,1)}, f32[51...) custom-call(bf16[512,1024]{1,0:T(8,128)(2,1)} %collective-permute-done.18.h0.l2, bf16[512,1024]{1,0:T(8,128)(2,1)} %copy-done.97, ...), custom_call_target="tpu_custom_call" | custom-call | flops 14495514624 | bytes 24641536 | tf_op jit(solution)/shard_map/pallas_call | solution.py:198
  305.9 3.0 add_convert_fusion.4
  309.4 15.8 %shard_map.242.rest_0_ = bf16[1024,2304]{1,0:T(8,128)(2,1)} custom-call(bf16[512,1024]{1,0:T(8,128)(2,1)} %multiply_convert_fusion.3.h0.l0, bf16[512,1024]{1,0:T(8,128)(2,1)} %collective-permute-done.16.h1.l1, bf16[512,1024]{1,0:T(8,128)(2,1)} %collective-permute-done.18.h0.l2, bf16[512,1024]{1,0:T(8,128)(2,1)} %copy-done.97, ...), custom_call_target="tpu_custom_call" | custom-call | flops 9663676416 | bytes 4718592 | tf_op jit(solution)/shard_map/pallas_call | solution.py:247
  325.2 11.6 %shard_map.243 = bf16[1024,3456]{1,0:T(8,128)(2,1)} custom-call(bf16[512,1024]{1,0:T(8,128)(2,1)} %copy-done.18, bf16[512,1024]{1,0:T(8,128)(2,1)} %collective-permute-done.17.e1.l1, bf16[512,1024]{1,0:T(8,128)(2,1)} %collective-permute-done.14.e0.l2, bf16[512,1024]{1,0:T(8,128)(2,1)} %collective-permute-done.21.e1.l3, ...), custom_call_target="tpu_custom_call" | custom-call | bytes 7077888 | tf_op jit(solution)/shard_map/pallas_call | solution.py:247
  336.8 3.8 convert_add_fusion.4
  347.9 4.2 convolution_convert_fusion.do_ref
  353.8 23.1 %shard_map.244 = (bf16[512,1024]{1,0:T(8,128)(2,1)}, bf16[256,1024]{1,0:T(8,128)(2,1)}, bf16[256,1024]{1,0:T(8,128)(2,1)}) custom-call(s32[1,1024]{1,0:T(1,128)} %bitcast.157, f32[32,1024]{1,0:T(8,128)} %get-tuple-element.349.cos_ref, f32[32,1024]{1,0:T(8,128)} %get-tuple-element.348.sin_ref, bf16[512,1024]{1,0:T(8,128)(2,1)} %get-tuple-element.147.q_ref, ...), custom_call_target="tpu_custom_call" | custom-call | flops 3221225472 | bytes 4194304 | tf_op jit(solution)/shard_map/pallas_call | solution.py:373
  385.8 4.2 fusion.69
  395.6 15.6 %shard_map.245 = (bf16[1024,2304]{1,0:T(8,128)(2,1)}, f32[512,1024]{1,0:T(8,128)}, bf16[512,1024]{1,0:T(8,128)(2,1)}) custom-call(bf16[512,1024]{1,0:T(8,128)(2,1)} %get-tuple-element.271.e0.l0, bf16[512,1024]{1,0:T(8,128)(2,1)} %copy-done.56, bf16[1024,3456]{1,0:T(8,128)(2,1)} %all-gather.7.cloned.1.call-done.w_both.w_down, ...), custom_call_target="tpu_custom_call" | custom-call | flops 7247757312 | bytes 21757952 | tf_op jit(solution)/shard_map/pallas_call | solution.py:198
  411.2 7.8 %shard_map.246 = bf16[1024,1536]{1,0:T(8,128)(2,1)} custom-call(bf16[1024,1024]{1,0:T(8,128)(2,1)} %pad_maximum_fusion.2.refs_0_, bf16[1024,1024]{1,0:T(8,128)(2,1)} %pad_maximum_fusion.3.refs_1_, bf16[512,1024]{1,0:T(8,128)(2,1)} %get-tuple-element.168.refs_2_, bf16[256,1024]{1,0:T(8,128)(2,1)} %get-tuple-element.169.refs_3_, ...), custom_call_target="tpu_custom_call" | custom-call | flops 3221225472 | bytes 10485760 | tf_op jit(solution)/shard_map/pallas_call | solution.py:412
  422.9 16.0 %shard_map.247 = (bf16[1024,2304]{1,0:T(8,128)(2,1)}, f32[512,1024]{1,0:T(8,128)}, bf16[512,1024]{1,0:T(8,128)(2,1)}) custom-call(bf16[512,1024]{1,0:T(8,128)(2,1)} %copy-done.57, bf16[512,1024]{1,0:T(8,128)(2,1)} %copy-done.58, bf16[1024,3456]{1,0:T(8,128)(2,1)} %all-gather.7.cloned.1.call-done.w_both.w_down, ...), custom_call_target="tpu_custom_call" | custom-call | flops 7247757312 | bytes 21757952 | tf_op jit(solution)/shard_map/pallas_call | solution.py:198
  443.7 16.0 %shard_map.248 = bf16[1024,2304]{1,0:T(8,128)(2,1)} custom-call(bf16[512,1024]{1,0:T(8,128)(2,1)} %copy-done.55, bf16[512,1024]{1,0:T(8,128)(2,1)} %copy-done.91, bf16[512,1024]{1,0:T(8,128)(2,1)} %copy-done.92, bf16[512,1024]{1,0:T(8,128)(2,1)} %copy-done.93, bf16[1024,2304]{1,0:T(8,128)(2,1)} %get-tuple-element.181.near, ...), custom_call_target="tpu_custom_call" | custom-call | flops 9663676416 | bytes 4718592 | tf_op jit(solution)/shard_map/pallas_call | solution.py:247
  461.8 10.2 %shard_map.249.extra = bf16[1024,1152]{1,0:T(8,128)(2,1)} custom-call(bf16[512,1024]{1,0:T(8,128)(2,1)} %get-tuple-element.271.e0.l0, bf16[512,1024]{1,0:T(8,128)(2,1)} %copy-done.56, bf16[512,1024]{1,0:T(8,128)(2,1)} %copy-done.57, bf16[512,1024]{1,0:T(8,128)(2,1)} %copy-done.58, bf16[1024,1152]{1,0:T(8,128)(2,1)} %get-tuple-element.183.near, ...), custom_call_target="tpu_custom_call" | custom-call | bytes 2359296 | tf_op jit(solution)/shard_map/pallas_call | solution.py:247
  472.0 14.6 %collective-permute-done.34 = bf16[512,1024]{1,0:T(8,128)(2,1)S(1)} collective-permute-done((bf16[512,1024]{1,0:T(8,128)(2,1)S(1)}, bf16[512,1024]{1,0:T(8,128)(2,1)S(1)}, u32[]{:S(2)}, u32[]{:S(2)}) %collective-permute-start.34) | collective-permute-done | bytes 1048608 | tf_op jit(solution)/shard_map/ppermute | solution.py:34
  497.1 3.3 fusion.76
  508.9 10.4 %shard_map.250 = bf16[1024,3200]{1,0:T(8,128)(2,1)} custom-call(bf16[1024,1024]{1,0:T(8,128)(2,1)} %pad_maximum_fusion.1.left0, bf16[1024,1024]{1,0:T(8,128)(2,1)} %pad_maximum_fusion.4.left1, bf16[1024,512]{1,0:T(8,128)(2,1)} %multiply_convert_fusion.2.g0, bf16[1024,512]{1,0:T(8,128)(2,1)} %get-tuple-element.191.g1, ...), custom_call_target="tpu_custom_call" | custom-call | flops 4294967296 | bytes 14942208 | tf_op jit(solution)/shard_map/pallas_call | solution.py:441
  545.4 4.3 collective-permute-done.43
  565.2 3.2 collective-permute-done.38
  569.7 3.5 collective-permute-done.39
  573.6 17.6 %reduce-scatter.11.cloned.1.call-done = bf16[128,3200]{1,0:T(8,128)(2,1)} async-done(((bf16[1024,3200]{1,0:T(8,128)(2,1)}), bf16[128,3200]{1,0:T(8,128)(2,1)}) %reduce-scatter.11.cloned.1.call-update) | async-done | bytes 819216 | tf_op jit(solution)/shard_map/reduce_scatter | solution.py:65
  (490 shorter events, 209.2 us)
Async XLA Ops:
  7.2 40.9 %all-gather.5.cloned.1.call-start = ((), (), s32[]{:S(2)}) async-start(), calls=%async_computation.4 | async-start | bytes 2506752 | tf_op jit(solution)/shard_map/all_gather | solution.py:61
  11.5 118.6 %all-gather.7.cloned.1.call-start = ((), (), s32[]{:S(2)}) async-start(), calls=%async_computation.5 | async-start | bytes 7962624 | tf_op jit(solution)/shard_map/all_gather | solution.py:61
  12.6 13.2 %collective-permute-start.7 = (bf16[64,3456]{1,0:T(8,128)(2,1)S(1)}, bf16[64,3456]{1,0:T(8,128)(2,1)S(1)}, u32[]{:S(2)}, u32[]{:S(2)}) collective-permute-start(bf16[64,3456]{1,0:T(8,128)(2,1)S(1)} %pad_maximum_fusion.13), channel_id=1, source_target_pairs={{0,2},{2,0},{4,6},{6,4},{8,10},{10,8},{12,14},{14,12},{16,18},{18,... | collective-permute-start | bytes 1327112 | tf_op jit(solution)/shard_map/ppermute | solution.py:34
  27.0 180.7 %all-gather.9.cloned.1.call-start = ((), (), s32[]{:S(2)}) async-start(), calls=%async_computation.6 | async-start | bytes 3538944 | tf_op jit(solution)/shard_map/all_gather | solution.py:61
  28.1 17.6 %collective-permute-start.1 = (bf16[64,3456]{1,0:T(8,128)(2,1)S(1)}, bf16[64,3456]{1,0:T(8,128)(2,1)S(1)}, u32[]{:S(2)}, u32[]{:S(2)}) collective-permute-start(bf16[64,3456]{1,0:T(8,128)(2,1)S(1)} %pad_maximum_fusion.11), channel_id=1, source_target_pairs={{0,2},{2,0},{4,6},{6,4},{8,10},{10,8},{12,14},{14,12},{16,18},{18,... | collective-permute-start | bytes 1327112 | tf_op jit(solution)/shard_map/ppermute | solution.py:34
  30.8 13.2 %collective-permute-start = (bf16[64,1536]{1,0:T(8,128)(2,1)}, bf16[64,1536]{1,0:T(8,128)(2,1)}, u32[]{:S(2)}, u32[]{:S(2)}) collective-permute-start(bf16[64,1536]{1,0:T(8,128)(2,1)} %pad_maximum_fusion.15), channel_id=1, source_target_pairs={{0,2},{2,0},{4,6},{6,4},{8,10},{10,8},{12,14},{14,12},{16,18},{18,... | collective-permute-start | bytes 589832 | tf_op jit(solution)/shard_map/ppermute | solution.py:34
  50.9 36.7 %collective-permute-start.2 = (bf16[512,1664]{1,0:T(8,128)(2,1)}, bf16[512,1664]{1,0:T(8,128)(2,1)}, u32[]{:S(2)}, u32[]{:S(2)}) collective-permute-start(bf16[512,1664]{1,0:T(8,128)(2,1)} %slice.404), channel_id=1, source_target_pairs={{0,2},{2,0},{4,6},{6,4},{8,10},{10,8},{12,14},{14,12},{16,18},{18,... | collective-permute-start | bytes 5111816 | tf_op jit(solution)/shard_map/ppermute | solution.py:34
  57.7 187.1 %all-gather.11.cloned.1.call-start = ((), (), s32[]{:S(2)}) async-start(), calls=%async_computation.7 | async-start | bytes 7962624 | tf_op jit(solution)/shard_map/all_gather | solution.py:61
  94.2 12.5 %collective-permute-start.3 = (bf16[512,1024]{1,0:T(8,128)(2,1)}, bf16[512,1024]{1,0:T(8,128)(2,1)}, u32[]{:S(2)}, u32[]{:S(2)}) collective-permute-start(bf16[512,1024]{1,0:T(8,128)(2,1)} %fusion.2), channel_id=1, source_target_pairs={{0,1},{1,0},{2,3},{3,2},{4,5},{5,4},{6,7},{7,6},{8,9},{9,8},{10,11... | collective-permute-start | bytes 3145736 | tf_op jit(solution)/shard_map/ppermute | solution.py:29
  99.1 18.4 %collective-permute-start.4 = (bf16[512,512]{1,0:T(8,128)(2,1)}, bf16[512,512]{1,0:T(8,128)(2,1)S(1)}, u32[]{:S(2)}, u32[]{:S(2)}) collective-permute-start(bf16[512,512]{1,0:T(8,128)(2,1)} %slice.405), channel_id=1, source_target_pairs={{0,2},{2,0},{4,6},{6,4},{8,10},{10,8},{12,14},{14,12},{16,18},{18,... | collective-permute-start | bytes 1572872 | tf_op jit(solution)/shard_map/ppermute | solution.py:34
  121.2 297.9 %reduce-scatter.5.cloned.1.call-start = ((), (), s32[]{:S(2)}) async-start(), calls=%async_computation.8 | async-start | bytes 7962624 | tf_op jit(solution)/shard_map/reduce_scatter | solution.py:65
  127.6 25.3 %collective-permute-start.8 = (bf16[512,1024]{1,0:T(8,128)(2,1)S(1)}, bf16[512,1024]{1,0:T(8,128)(2,1)S(1)}, u32[]{:S(2)}, u32[]{:S(2)}) collective-permute-start(bf16[512,1024]{1,0:T(8,128)(2,1)S(1)} %multiply_convert_fusion.5.h0.l0), channel_id=1, source_target_pairs={{0,2},{2,0},{4,6},{6,4},{8,10},{10,8},{12,14},{14,12},{16,18},{18,... | collective-permute-start | bytes 3145736 | tf_op jit(solution)/shard_map/ppermute | solution.py:34
  177.0 25.3 %collective-permute-start.12 = (bf16[512,1024]{1,0:T(8,128)(2,1)S(1)}, bf16[512,1024]{1,0:T(8,128)(2,1)S(1)}, u32[]{:S(2)}, u32[]{:S(2)}) collective-permute-start(bf16[512,1024]{1,0:T(8,128)(2,1)S(1)} %add_convert_fusion.5), channel_id=1, source_target_pairs={{0,2},{2,0},{4,6},{6,4},{8,10},{10,8},{12,14},{14,12},{16,18},{18,... | collective-permute-start | bytes 3145736 | tf_op jit(solution)/shard_map/ppermute | solution.py:34
  203.4 32.0 %collective-permute-start.14 = (bf16[512,1024]{1,0:T(8,128)(2,1)S(1)}, bf16[512,1024]{1,0:T(8,128)(2,1)}, u32[]{:S(2)}, u32[]{:S(2)}) collective-permute-start(bf16[512,1024]{1,0:T(8,128)(2,1)S(1)} %slice_dynamic-update-slice_fusion.22.e0.l0), channel_id=1, source_target_pairs={{0,2},{2,0},{4,6},{6,4},{8,10},{10,8},{12,14},{14,12},{16,18},{18,... | collective-permute-start | bytes 3145736 | tf_op jit(solution)/shard_map/ppermute | solution.py:34
  237.5 7.4 %collective-permute-start.17 = (bf16[512,1024]{1,0:T(8,128)(2,1)S(1)}, bf16[512,1024]{1,0:T(8,128)(2,1)}, u32[]{:S(2)}, u32[]{:S(2)}) collective-permute-start(bf16[512,1024]{1,0:T(8,128)(2,1)S(1)} %slice_dynamic-update-slice_fusion.22.e0.l0), channel_id=1, source_target_pairs={{0,1},{1,0},{2,3},{3,2},{4,5},{5,4},{6,7},{7,6},{8,9},{9,8},{10,11... | collective-permute-start | bytes 3145736 | tf_op jit(solution)/shard_map/ppermute | solution.py:29
  244.0 28.9 %collective-permute-start.21 = (bf16[512,1024]{1,0:T(8,128)(2,1)}, bf16[512,1024]{1,0:T(8,128)(2,1)}, u32[]{:S(2)}, u32[]{:S(2)}) collective-permute-start(bf16[512,1024]{1,0:T(8,128)(2,1)} %collective-permute-done.14.e0.l2), channel_id=1, source_target_pairs={{0,1},{1,0},{2,3},{3,2},{4,5},{5,4},{6,7},{7,6},{8,9},{9,8},{10,11... | collective-permute-start | bytes 3145736 | tf_op jit(solution)/shard_map/ppermute | solution.py:29
  244.4 28.3 %collective-permute-start.18 = (bf16[512,1024]{1,0:T(8,128)(2,1)}, bf16[512,1024]{1,0:T(8,128)(2,1)}, u32[]{:S(2)}, u32[]{:S(2)}) collective-permute-start(bf16[512,1024]{1,0:T(8,128)(2,1)} %multiply_convert_fusion.3.h0.l0), channel_id=1, source_target_pairs={{0,2},{2,0},{4,6},{6,4},{8,10},{10,8},{12,14},{14,12},{16,18},{18,... | collective-permute-start | bytes 3145736 | tf_op jit(solution)/shard_map/ppermute | solution.py:34
  303.2 33.6 %collective-permute-start.19 = (bf16[512,1024]{1,0:T(8,128)(2,1)}, bf16[512,1024]{1,0:T(8,128)(2,1)S(1)}, u32[]{:S(2)}, u32[]{:S(2)}) collective-permute-start(bf16[512,1024]{1,0:T(8,128)(2,1)} %get-tuple-element.127), channel_id=1, source_target_pairs={{0,1},{1,0},{2,3},{3,2},{4,5},{5,4},{6,7},{7,6},{8,9},{9,8},{10,11... | collective-permute-start | bytes 3145736 | tf_op jit(solution)/shard_map/ppermute | solution.py:29
  308.9 27.8 %collective-permute-start.23 = (bf16[512,1024]{1,0:T(8,128)(2,1)}, bf16[512,1024]{1,0:T(8,128)(2,1)}, u32[]{:S(2)}, u32[]{:S(2)}) collective-permute-start(bf16[512,1024]{1,0:T(8,128)(2,1)} %add_convert_fusion.4), channel_id=1, source_target_pairs={{0,2},{2,0},{4,6},{6,4},{8,10},{10,8},{12,14},{14,12},{16,18},{18,... | collective-permute-start | bytes 3145736 | tf_op jit(solution)/shard_map/ppermute | solution.py:34
  340.6 156.5 %reduce-scatter.7.cloned.1.call-start = ((), (), s32[]{:S(2)}) async-start(), calls=%async_computation.9 | async-start | bytes 3538944 | tf_op jit(solution)/shard_map/reduce_scatter | solution.py:65
  352.2 25.5 %collective-permute-start.27 = (bf16[512,1024]{1,0:T(8,128)(2,1)}, bf16[512,1024]{1,0:T(8,128)(2,1)}, u32[]{:S(2)}, u32[]{:S(2)}) collective-permute-start(bf16[512,1024]{1,0:T(8,128)(2,1)} %add_convert_fusion.3), channel_id=1, source_target_pairs={{0,2},{2,0},{4,6},{6,4},{8,10},{10,8},{12,14},{14,12},{16,18},{18,... | collective-permute-start | bytes 3145736 | tf_op jit(solution)/shard_map/ppermute | solution.py:34
  391.6 27.4 %collective-permute-start.30 = (bf16[512,1024]{1,0:T(8,128)(2,1)}, bf16[512,1024]{1,0:T(8,128)(2,1)S(1)}, u32[]{:S(2)}, u32[]{:S(2)}) collective-permute-start(bf16[512,1024]{1,0:T(8,128)(2,1)} %get-tuple-element.271.e0.l0), channel_id=1, source_target_pairs={{0,2},{2,0},{4,6},{6,4},{8,10},{10,8},{12,14},{14,12},{16,18},{18,... | collective-permute-start | bytes 3145736 | tf_op jit(solution)/shard_map/ppermute | solution.py:34
  419.1 104.9 %reduce-scatter.9.cloned.1.call-start = ((), (), s32[]{:S(2)}) async-start(), calls=%async_computation.10 | async-start | bytes 5308416 | tf_op jit(solution)/shard_map/reduce_scatter | solution.py:65
  459.8 131.4 %reduce-scatter.11.cloned.1.call-start = ((), (), s32[]{:S(2)}) async-start(), calls=%async_computation.11 | async-start | bytes 7372800 | tf_op jit(solution)/shard_map/reduce_scatter | solution.py:65
  461.0 11.0 %collective-permute-start.31 = (bf16[512,1024]{1,0:T(8,128)(2,1)S(1)}, bf16[512,1024]{1,0:T(8,128)(2,1)S(1)}, u32[]{:S(2)}, u32[]{:S(2)}) collective-permute-start(bf16[512,1024]{1,0:T(8,128)(2,1)S(1)} %copy-done.95), channel_id=1, source_target_pairs={{0,1},{1,0},{2,3},{3,2},{4,5},{5,4},{6,7},{7,6},{8,9},{9,8},{10,11... | collective-permute-start | bytes 3145736 | tf_op jit(solution)/shard_map/ppermute | solution.py:29
  461.2 25.4 %collective-permute-start.34 = (bf16[512,1024]{1,0:T(8,128)(2,1)S(1)}, bf16[512,1024]{1,0:T(8,128)(2,1)S(1)}, u32[]{:S(2)}, u32[]{:S(2)}) collective-permute-start(bf16[512,1024]{1,0:T(8,128)(2,1)S(1)} %add_convert_fusion.1), channel_id=1, source_target_pairs={{0,2},{2,0},{4,6},{6,4},{8,10},{10,8},{12,14},{14,12},{16,18},{18,... | collective-permute-start | bytes 3145736 | tf_op jit(solution)/shard_map/ppermute | solution.py:34
  526.4 27.5 %collective-permute-start.45 = (bf16[64,3456]{1,0:T(8,128)(2,1)}, bf16[64,3456]{1,0:T(8,128)(2,1)}, u32[]{:S(2)}, u32[]{:S(2)}) collective-permute-start(bf16[64,3456]{1,0:T(8,128)(2,1)} %get-tuple-element.304), channel_id=1, source_target_pairs={{0,2},{2,0},{4,6},{6,4},{8,10},{10,8},{12,14},{14,12},{16,18},{18,... | collective-permute-start | bytes 1327112 | tf_op jit(solution)/shard_map/ppermute | solution.py:34
  528.1 15.8 %collective-permute-start.44 = (bf16[64,1536]{1,0:T(8,128)(2,1)S(1)}, bf16[64,1536]{1,0:T(8,128)(2,1)S(1)}, u32[]{:S(2)}, u32[]{:S(2)}) collective-permute-start(bf16[64,1536]{1,0:T(8,128)(2,1)S(1)} %broadcast_select_fusion.19), channel_id=1, source_target_pairs={{0,2},{2,0},{4,6},{6,4},{8,10},{10,8},{12,14},{14,12},{16,18},{18,... | collective-permute-start | bytes 589832 | tf_op jit(solution)/shard_map/ppermute | solution.py:34
  531.6 18.1 %collective-permute-start.43 = (bf16[64,2304]{1,0:T(8,128)(2,1)}, bf16[64,2304]{1,0:T(8,128)(2,1)}, u32[]{:S(2)}, u32[]{:S(2)}) collective-permute-start(bf16[64,2304]{1,0:T(8,128)(2,1)} %get-tuple-element.312), channel_id=1, source_target_pairs={{0,2},{2,0},{4,6},{6,4},{8,10},{10,8},{12,14},{14,12},{16,18},{18,... | collective-permute-start | bytes 884744 | tf_op jit(solution)/shard_map/ppermute | solution.py:34
  537.0 21.2 %collective-permute-start.36 = (bf16[512,1024]{1,0:T(8,128)(2,1)}, bf16[512,1024]{1,0:T(8,128)(2,1)}, u32[]{:S(2)}, u32[]{:S(2)}) collective-permute-start(bf16[512,1024]{1,0:T(8,128)(2,1)} %add_convert_fusion), channel_id=1, source_target_pairs={{0,1},{1,0},{2,3},{3,2},{4,5},{5,4},{6,7},{7,6},{8,9},{9,8},{10,11... | collective-permute-start | bytes 3145736 | tf_op jit(solution)/shard_map/ppermute | solution.py:29
  573.1 21.6 %collective-permute-start.40 = (f32[8,1024]{1,0:T(8,128)S(1)}, f32[8,1024]{1,0:T(8,128)S(1)}, u32[]{:S(2)}, u32[]{:S(2)}) collective-permute-start(f32[8,1024]{1,0:T(8,128)S(1)} %add.273), channel_id=1, source_target_pairs={{0,8},{2,10},{4,12},{6,14},{8,0},{10,2},{12,4},{14,6},{16,24},{18,... | collective-permute-start | bytes 98312 | tf_op jit(solution)/shard_map/ppermute | solution.py:739
  592.4 11.3 %collective-permute-start.42 = (bf16[64,3200]{1,0:T(8,128)(2,1)S(1)}, bf16[64,3200]{1,0:T(8,128)(2,1)S(1)}, u32[]{:S(2)}, u32[]{:S(2)}) collective-permute-start(bf16[64,3200]{1,0:T(8,128)(2,1)S(1)} %get-tuple-element.310), channel_id=1, source_target_pairs={{0,2},{2,0},{4,6},{6,4},{8,10},{10,8},{12,14},{14,12},{16,18},{18,... | collective-permute-start | bytes 1228808 | tf_op jit(solution)/shard_map/ppermute | solution.py:34
  (120 other events, 823.3 us)
Sparse Core Ops, SparseCore 0:
  11.6 36.5 all-gather.4
  50.2 73.9 all-gather.6
  126.3 38.3 all-gather.8
  166.1 74.6 all-gather.10
  340.7 76.6 reduce-scatter.4
  419.5 38.6 reduce-scatter.6
  460.5 53.2 reduce-scatter.8
  519.4 71.7 reduce-scatter.10

commit v5 on v4

--- a/solution.py
+++ b/solution.py
@@ -611,9 +611,13 @@
         far_back, far_sum = ff_back(*far_in, weights, unit, far[0])
         far_sum, far_back = lax.optimization_barrier((far_total(far_sum), far_back))
         g_gate_up = weight_grad(blocks, near_back, far_back)
-        product, g_gate_up = lax.optimization_barrier((near[1], g_gate_up))
+        upper, lower = jnp.split(far_sum, 2, axis=0)
+        upper, g_gate_up = lax.optimization_barrier((flip_x(upper), g_gate_up))
+        product, upper = lax.optimization_barrier((near[1], upper))
         g_down = weight_grad([own, sibling, *far_in], product, far[1], 0)
-        grad_normed = four_total(near_sum, far_sum)
+        lower, g_down = lax.optimization_barrier((flip_x(lower), g_down))
+        whole_far = jnp.concatenate([upper, lower], axis=0)
+        grad_normed = near_sum[0] + swap(near_sum[1]).astype(F32) + whole_far.astype(F32)
         grad_normed, g_down = lax.optimization_barrier((grad_normed, g_down))
         grad_hidden, grad_gain = norm_back(grad_normed, hidden, gain, grad_out)
         return grad_hidden, grad_gain, ring_sum(g_gate_up), g_down, settle, ring_sum(other)

time: 619 us -> 617 us (level)
    ppermute x17 -> x18, waiting for transfers between devices: 107 us -> 94.7 us  [flip_x(): return lax.ppermute(values, 'dp', [(i, i ^ 1) for i in range(n)])]
    reduce_scatter x4, waiting for transfers between devices: 17.6 us -> 25.8 us  [ring_sum(): lax.psum_scatter(grad, 'dp', scatter_dimension=0, axis_index_groups=ring_...]
    ppermute x17 -> x18, starting transfers between devices: 19.2 us -> 21.6 us  [flip_x(): return lax.ppermute(values, 'dp', [(i, i ^ 1) for i in range(n)])]
  transfers between devices with their start and end apart: 54 -> 55, of which waited for: 30 -> 31; matrix products, arithmetic and copies ran while one was open for 24% -> 24% of each run, Pallas kernels for 33% -> 33%
where the time goes in v5:
time: 617 us; the launch traced here: 611 us
  Pallas kernels  230 us (37%)
  waiting for transfers between devices  157 us (25%)
  other arithmetic  72.4 us (12%)
  local copies, waits for them, and re-layouts  59.7 us (10%)
  matrix products  43.4 us (7%)
  starting transfers between devices  32.2 us (5%)
  between operations  15.9 us (3%)
    pallas_call x6, Pallas kernels, ff_call(): pl.pallas_call(kernel, grid=(2,), out_shape=[*outs, *ends], in_specs=[who...  114 us
    ppermute x18, waiting for transfers between devices, flip_x(): return lax.ppermute(values, 'dp', [(i, i ^ 1) for i in range(n)])  94.7 us
    pallas_call x4, Pallas kernels, weight_grad(): pl.pallas_call(weight_grad_kernel, grid=(depth // tile,), out_shape=out,...  53.6 us
    unnamed x237, local copies, waits for them, and re-layouts  37.2 us
    ppermute x25, waiting for transfers between devices, swap(): return lax.ppermute(values, 'tensor', [(0, 1), (1, 0)])  27.7 us
    reduce_scatter x4, waiting for transfers between devices, ring_sum(): lax.psum_scatter(grad, 'dp', scatter_dimension=0, axis_index_groups=ring_...  25.8 us
    pallas_call x1, Pallas kernels, attend_back(): pl.pallas_call(functools.partial(attend_back_kernel, min(256, length)), g...  23.1 us
    ppermute x18, starting transfers between devices, flip_x(): return lax.ppermute(values, 'dp', [(i, i ^ 1) for i in range(n)])  21.6 us
  transfers between devices with their start and end apart: 55, of which 31 were waited for; matrix products, arithmetic and copies ran while one was open for 24% of the time, Pallas kernels for 33%

profile of v5, /device:TPU:0, one launch (start us, length us, event | category | flops | bytes accessed | tf_op | source)
XLA Modules:
  0.0 611.0 jit_solution(14042762036136766211)
XLA Ops:
  12.6 3.0 collective-permute-start.7
  15.6 10.2 %collective-permute-done.7 = bf16[64,3456]{1,0:T(8,128)(2,1)S(1)} collective-permute-done((bf16[64,3456]{1,0:T(8,128)(2,1)S(1)}, bf16[64,3456]{1,0:T(8,128)(2,1)S(1)}, u32[]{:S(2)}, u32[]{:S(2)}) %collective-permute-start.7) | collective-permute-done | bytes 442400 | tf_op jit(solution)/shard_map/ppermute | solution.py:34
  31.4 12.6 %collective-permute-done = bf16[64,1536]{1,0:T(8,128)(2,1)} collective-permute-done((bf16[64,1536]{1,0:T(8,128)(2,1)}, bf16[64,1536]{1,0:T(8,128)(2,1)}, u32[]{:S(2)}, u32[]{:S(2)}) %collective-permute-start) | collective-permute-done | bytes 196640 | tf_op jit(solution)/shard_map/ppermute | solution.py:34
  59.2 28.4 %collective-permute-done.2 = bf16[512,1664]{1,0:T(8,128)(2,1)} collective-permute-done((bf16[512,1664]{1,0:T(8,128)(2,1)}, bf16[512,1664]{1,0:T(8,128)(2,1)}, u32[]{:S(2)}, u32[]{:S(2)}) %collective-permute-start.2) | collective-permute-done | bytes 1703968 | tf_op jit(solution)/shard_map/ppermute | solution.py:34
  112.8 4.6 multiply_convert_fusion.6
  131.1 15.0 %shard_map.237 = (bf16[1024,2304]{1,0:T(8,128)(2,1)}, bf16[1024,1152]{1,0:T(8,128)(2,1)}, f32[512,1024]{1,0:T(8,128)}, bf16[512,1024]{1,0:T(8,128)(2,1)}) custom-call(bf16[512,1024]{1,0:T(8,128)(2,1)} %copy-done.55, bf16[512,1024]{1,0:T(8,128)(2,1)} %copy-done.91, bf16[1024,3456]{1,0:T(8,128)(2,1)} %all-gather.7.cloned.1.call-done.w_both.w_down, ...), custom_call_target="tpu_custom_call" | custom-call | flops 7247757312 | bytes 19398656 | tf_op jit(solution)/shard_map/pallas_call | solution.py:198
  146.1 6.9 %collective-permute-done.8.h0.l2 = bf16[512,1024]{1,0:T(8,128)(2,1)S(1)} collective-permute-done((bf16[512,1024]{1,0:T(8,128)(2,1)S(1)}, bf16[512,1024]{1,0:T(8,128)(2,1)S(1)}, u32[]{:S(2)}, u32[]{:S(2)}) %collective-permute-start.8) | collective-permute-done | bytes 1048608 | tf_op jit(solution)/shard_map/ppermute | solution.py:34
  156.6 15.3 %shard_map.238 = (bf16[1024,2304]{1,0:T(8,128)(2,1)}, bf16[1024,1152]{1,0:T(8,128)(2,1)}, f32[512,1024]{1,0:T(8,128)}, bf16[512,1024]{1,0:T(8,128)(2,1)}) custom-call(bf16[512,1024]{1,0:T(8,128)(2,1)} %copy-done.92, bf16[512,1024]{1,0:T(8,128)(2,1)} %copy-done.93, bf16[1024,3456]{1,0:T(8,128)(2,1)} %all-gather.7.cloned.1.call-done.w_both.w_down, ...), custom_call_target="tpu_custom_call" | custom-call | flops 7247757312 | bytes 19398656 | tf_op jit(solution)/shard_map/pallas_call | solution.py:198
  178.0 24.2 %collective-permute-done.12 = bf16[512,1024]{1,0:T(8,128)(2,1)S(1)} collective-permute-done((bf16[512,1024]{1,0:T(8,128)(2,1)S(1)}, bf16[512,1024]{1,0:T(8,128)(2,1)S(1)}, u32[]{:S(2)}, u32[]{:S(2)}) %collective-permute-start.12) | collective-permute-done | bytes 1048608 | tf_op jit(solution)/shard_map/ppermute | solution.py:34
  207.6 6.7 %fusion.13.q_ref.k_ref.v_ref = f32[1024,1024]{1,0:T(8,128)} fusion(bf16[1024,1536]{1,0:T(8,128)(2,1)} %all-gather.9.cloned.1.call-done, bf16[512,1024]{1,0:T(8,128)(2,1)} %get-tuple-element.296, bf16[512,1024]{1,0:T(8,128)(2,1)} %get-tuple-element.295), kind=kOutput, calls=%fused_computation.68 | convolution fusion | flops 2151677952 | bytes 8388608 | tf_op jit(solution)/shard_map/dot_general | solution.py:677
  214.3 21.0 %shard_map.239 = (bf16[512,1024]{1,0:T(8,128)(2,1)}, bf16[256,1024]{1,0:T(8,128)(2,1)}, bf16[256,1024]{1,0:T(8,128)(2,1)}, bf16[512,1024]{1,0:T(8,128)(2,1)}, f32[4,2,1024]{2,1,0:T(2,128)}) custom-call(s32[1,1024]{1,0:T(1,128)} %bitcast.156, f32[32,1024]{1,0:T(8,128)} %get-tuple-element.359.cos_ref, f32[32,1024]{1,0:T(8,128)} %get-tuple-element.358.sin_ref, ...), custom_call_target="tpu_custom_call" | custom-call | flops 1073741824 | bytes 8388608 | tf_op jit(solution)/shard_map/pallas_call | solution.py:307
  247.0 25.8 %shard_map.240 = (bf16[1024,1152]{1,0:T(8,128)(2,1)}, bf16[1024,2304]{1,0:T(8,128)(2,1)}, f32[512,1024]{1,0:T(8,128)}, bf16[512,1024]{1,0:T(8,128)(2,1)}, f32[51...) custom-call(bf16[512,1024]{1,0:T(8,128)(2,1)} %multiply_convert_fusion.3.h0.l0, ...), custom_call_target="tpu_custom_call" | custom-call | flops 14495514624 | bytes 24641536 | tf_op jit(solution)/shard_map/pallas_call | solution.py:198
  276.7 26.4 %shard_map.241 = (bf16[1024,1152]{1,0:T(8,128)(2,1)}, bf16[1024,2304]{1,0:T(8,128)(2,1)}, f32[512,1024]{1,0:T(8,128)}, bf16[512,1024]{1,0:T(8,128)(2,1)}, f32[51...) custom-call(bf16[512,1024]{1,0:T(8,128)(2,1)} %collective-permute-done.18.h0.l2, bf16[512,1024]{1,0:T(8,128)(2,1)} %copy-done.97, ...), custom_call_target="tpu_custom_call" | custom-call | flops 14495514624 | bytes 24641536 | tf_op jit(solution)/shard_map/pallas_call | solution.py:198
  306.1 3.0 add_convert_fusion.4
  309.5 15.8 %shard_map.242.rest_0_ = bf16[1024,2304]{1,0:T(8,128)(2,1)} custom-call(bf16[512,1024]{1,0:T(8,128)(2,1)} %multiply_convert_fusion.3.h0.l0, bf16[512,1024]{1,0:T(8,128)(2,1)} %collective-permute-done.16.h1.l1, bf16[512,1024]{1,0:T(8,128)(2,1)} %collective-permute-done.18.h0.l2, bf16[512,1024]{1,0:T(8,128)(2,1)} %copy-done.97, ...), custom_call_target="tpu_custom_call" | custom-call | flops 9663676416 | bytes 4718592 | tf_op jit(solution)/shard_map/pallas_call | solution.py:247
  325.3 11.6 %shard_map.243 = bf16[1024,3456]{1,0:T(8,128)(2,1)} custom-call(bf16[512,1024]{1,0:T(8,128)(2,1)} %copy-done.18, bf16[512,1024]{1,0:T(8,128)(2,1)} %collective-permute-done.17.e1.l1, bf16[512,1024]{1,0:T(8,128)(2,1)} %collective-permute-done.14.e0.l2, bf16[512,1024]{1,0:T(8,128)(2,1)} %collective-permute-done.21.e1.l3, ...), custom_call_target="tpu_custom_call" | custom-call | bytes 7077888 | tf_op jit(solution)/shard_map/pallas_call | solution.py:247
  336.9 3.8 convert_add_fusion.4
  340.8 2.9 multiply_reduce_fusion.3
  348.0 4.2 convolution_convert_fusion.do_ref
  353.9 23.1 %shard_map.244 = (bf16[512,1024]{1,0:T(8,128)(2,1)}, bf16[256,1024]{1,0:T(8,128)(2,1)}, bf16[256,1024]{1,0:T(8,128)(2,1)}) custom-call(s32[1,1024]{1,0:T(1,128)} %bitcast.157, f32[32,1024]{1,0:T(8,128)} %get-tuple-element.359.cos_ref, f32[32,1024]{1,0:T(8,128)} %get-tuple-element.358.sin_ref, bf16[512,1024]{1,0:T(8,128)(2,1)} %get-tuple-element.151.q_ref, ...), custom_call_target="tpu_custom_call" | custom-call | flops 3221225472 | bytes 4194304 | tf_op jit(solution)/shard_map/pallas_call | solution.py:373
  385.9 4.2 fusion.69
  395.8 15.6 %shard_map.245 = (bf16[1024,2304]{1,0:T(8,128)(2,1)}, f32[512,1024]{1,0:T(8,128)}, bf16[512,1024]{1,0:T(8,128)(2,1)}) custom-call(bf16[512,1024]{1,0:T(8,128)(2,1)} %get-tuple-element.279.e0.l0, bf16[512,1024]{1,0:T(8,128)(2,1)} %copy-done.56, bf16[1024,3456]{1,0:T(8,128)(2,1)} %all-gather.7.cloned.1.call-done.w_both.w_down, ...), custom_call_target="tpu_custom_call" | custom-call | flops 7247757312 | bytes 21757952 | tf_op jit(solution)/shard_map/pallas_call | solution.py:198
  411.4 7.9 %shard_map.246 = bf16[1024,1536]{1,0:T(8,128)(2,1)} custom-call(bf16[1024,1024]{1,0:T(8,128)(2,1)} %pad_maximum_fusion.2.refs_0_, bf16[1024,1024]{1,0:T(8,128)(2,1)} %pad_maximum_fusion.3.refs_1_, bf16[512,1024]{1,0:T(8,128)(2,1)} %get-tuple-element.172.refs_2_, bf16[256,1024]{1,0:T(8,128)(2,1)} %get-tuple-element.173.refs_3_, ...), custom_call_target="tpu_custom_call" | custom-call | flops 3221225472 | bytes 10485760 | tf_op jit(solution)/shard_map/pallas_call | solution.py:412
  423.1 16.0 %shard_map.247 = (bf16[1024,2304]{1,0:T(8,128)(2,1)}, f32[512,1024]{1,0:T(8,128)}, bf16[512,1024]{1,0:T(8,128)(2,1)}) custom-call(bf16[512,1024]{1,0:T(8,128)(2,1)} %copy-done.57, bf16[512,1024]{1,0:T(8,128)(2,1)} %copy-done.58, bf16[1024,3456]{1,0:T(8,128)(2,1)} %all-gather.7.cloned.1.call-done.w_both.w_down, ...), custom_call_target="tpu_custom_call" | custom-call | flops 7247757312 | bytes 21757952 | tf_op jit(solution)/shard_map/pallas_call | solution.py:198
  444.8 16.0 %shard_map.248 = bf16[1024,2304]{1,0:T(8,128)(2,1)} custom-call(bf16[512,1024]{1,0:T(8,128)(2,1)} %copy-done.55, bf16[512,1024]{1,0:T(8,128)(2,1)} %copy-done.91, bf16[512,1024]{1,0:T(8,128)(2,1)} %copy-done.92, bf16[512,1024]{1,0:T(8,128)(2,1)} %copy-done.93, bf16[1024,2304]{1,0:T(8,128)(2,1)} %get-tuple-element.185.near, ...), custom_call_target="tpu_custom_call" | custom-call | flops 9663676416 | bytes 4718592 | tf_op jit(solution)/shard_map/pallas_call | solution.py:247
  463.4 10.2 %shard_map.249.extra = bf16[1024,1152]{1,0:T(8,128)(2,1)} custom-call(bf16[512,1024]{1,0:T(8,128)(2,1)} %get-tuple-element.279.e0.l0, bf16[512,1024]{1,0:T(8,128)(2,1)} %copy-done.56, bf16[512,1024]{1,0:T(8,128)(2,1)} %copy-done.57, bf16[512,1024]{1,0:T(8,128)(2,1)} %copy-done.58, bf16[1024,1152]{1,0:T(8,128)(2,1)} %get-tuple-element.189.near, ...), custom_call_target="tpu_custom_call" | custom-call | bytes 2359296 | tf_op jit(solution)/shard_map/pallas_call | solution.py:247
  486.9 3.3 fusion.77
  498.7 10.4 %shard_map.250 = bf16[1024,3200]{1,0:T(8,128)(2,1)} custom-call(bf16[1024,1024]{1,0:T(8,128)(2,1)} %pad_maximum_fusion.1.left0, bf16[1024,1024]{1,0:T(8,128)(2,1)} %pad_maximum_fusion.4.left1, bf16[1024,512]{1,0:T(8,128)(2,1)} %multiply_convert_fusion.2.g0, bf16[1024,512]{1,0:T(8,128)(2,1)} %get-tuple-element.199.g1, ...), custom_call_target="tpu_custom_call" | custom-call | flops 4294967296 | bytes 14942208 | tf_op jit(solution)/shard_map/pallas_call | solution.py:441
  536.3 4.2 collective-permute-done.44
  560.3 3.5 collective-permute-done.40
  564.3 24.6 %reduce-scatter.11.cloned.1.call-done = bf16[128,3200]{1,0:T(8,128)(2,1)} async-done(((bf16[1024,3200]{1,0:T(8,128)(2,1)}), bf16[128,3200]{1,0:T(8,128)(2,1)}) %reduce-scatter.11.cloned.1.call-update) | async-done | bytes 819216 | tf_op jit(solution)/shard_map/reduce_scatter | solution.py:65
  598.5 2.9 collective-permute-done.43
  (493 shorter events, 211.7 us)
Async XLA Ops:
  7.2 40.9 %all-gather.5.cloned.1.call-start = ((), (), s32[]{:S(2)}) async-start(), calls=%async_computation.4 | async-start | bytes 2506752 | tf_op jit(solution)/shard_map/all_gather | solution.py:61
  11.5 118.6 %all-gather.7.cloned.1.call-start = ((), (), s32[]{:S(2)}) async-start(), calls=%async_computation.5 | async-start | bytes 7962624 | tf_op jit(solution)/shard_map/all_gather | solution.py:61
  12.6 13.2 %collective-permute-start.7 = (bf16[64,3456]{1,0:T(8,128)(2,1)S(1)}, bf16[64,3456]{1,0:T(8,128)(2,1)S(1)}, u32[]{:S(2)}, u32[]{:S(2)}) collective-permute-start(bf16[64,3456]{1,0:T(8,128)(2,1)S(1)} %pad_maximum_fusion.13), channel_id=1, source_target_pairs={{0,2},{2,0},{4,6},{6,4},{8,10},{10,8},{12,14},{14,12},{16,18},{18,... | collective-permute-start | bytes 1327112 | tf_op jit(solution)/shard_map/ppermute | solution.py:34
  27.0 180.7 %all-gather.9.cloned.1.call-start = ((), (), s32[]{:S(2)}) async-start(), calls=%async_computation.6 | async-start | bytes 3538944 | tf_op jit(solution)/shard_map/all_gather | solution.py:61
  28.1 17.6 %collective-permute-start.1 = (bf16[64,3456]{1,0:T(8,128)(2,1)S(1)}, bf16[64,3456]{1,0:T(8,128)(2,1)S(1)}, u32[]{:S(2)}, u32[]{:S(2)}) collective-permute-start(bf16[64,3456]{1,0:T(8,128)(2,1)S(1)} %pad_maximum_fusion.11), channel_id=1, source_target_pairs={{0,2},{2,0},{4,6},{6,4},{8,10},{10,8},{12,14},{14,12},{16,18},{18,... | collective-permute-start | bytes 1327112 | tf_op jit(solution)/shard_map/ppermute | solution.py:34
  30.8 13.2 %collective-permute-start = (bf16[64,1536]{1,0:T(8,128)(2,1)}, bf16[64,1536]{1,0:T(8,128)(2,1)}, u32[]{:S(2)}, u32[]{:S(2)}) collective-permute-start(bf16[64,1536]{1,0:T(8,128)(2,1)} %pad_maximum_fusion.15), channel_id=1, source_target_pairs={{0,2},{2,0},{4,6},{6,4},{8,10},{10,8},{12,14},{14,12},{16,18},{18,... | collective-permute-start | bytes 589832 | tf_op jit(solution)/shard_map/ppermute | solution.py:34
  50.9 36.7 %collective-permute-start.2 = (bf16[512,1664]{1,0:T(8,128)(2,1)}, bf16[512,1664]{1,0:T(8,128)(2,1)}, u32[]{:S(2)}, u32[]{:S(2)}) collective-permute-start(bf16[512,1664]{1,0:T(8,128)(2,1)} %slice.404), channel_id=1, source_target_pairs={{0,2},{2,0},{4,6},{6,4},{8,10},{10,8},{12,14},{14,12},{16,18},{18,... | collective-permute-start | bytes 5111816 | tf_op jit(solution)/shard_map/ppermute | solution.py:34
  57.8 187.1 %all-gather.11.cloned.1.call-start = ((), (), s32[]{:S(2)}) async-start(), calls=%async_computation.7 | async-start | bytes 7962624 | tf_op jit(solution)/shard_map/all_gather | solution.py:61
  94.2 12.5 %collective-permute-start.3 = (bf16[512,1024]{1,0:T(8,128)(2,1)}, bf16[512,1024]{1,0:T(8,128)(2,1)}, u32[]{:S(2)}, u32[]{:S(2)}) collective-permute-start(bf16[512,1024]{1,0:T(8,128)(2,1)} %fusion.2), channel_id=1, source_target_pairs={{0,1},{1,0},{2,3},{3,2},{4,5},{5,4},{6,7},{7,6},{8,9},{9,8},{10,11... | collective-permute-start | bytes 3145736 | tf_op jit(solution)/shard_map/ppermute | solution.py:29
  99.1 18.4 %collective-permute-start.4 = (bf16[512,512]{1,0:T(8,128)(2,1)}, bf16[512,512]{1,0:T(8,128)(2,1)S(1)}, u32[]{:S(2)}, u32[]{:S(2)}) collective-permute-start(bf16[512,512]{1,0:T(8,128)(2,1)} %slice.405), channel_id=1, source_target_pairs={{0,2},{2,0},{4,6},{6,4},{8,10},{10,8},{12,14},{14,12},{16,18},{18,... | collective-permute-start | bytes 1572872 | tf_op jit(solution)/shard_map/ppermute | solution.py:34
  121.2 298.1 %reduce-scatter.5.cloned.1.call-start = ((), (), s32[]{:S(2)}) async-start(), calls=%async_computation.8 | async-start | bytes 7962624 | tf_op jit(solution)/shard_map/reduce_scatter | solution.py:65
  127.6 25.3 %collective-permute-start.8 = (bf16[512,1024]{1,0:T(8,128)(2,1)S(1)}, bf16[512,1024]{1,0:T(8,128)(2,1)S(1)}, u32[]{:S(2)}, u32[]{:S(2)}) collective-permute-start(bf16[512,1024]{1,0:T(8,128)(2,1)S(1)} %multiply_convert_fusion.5.h0.l0), channel_id=1, source_target_pairs={{0,2},{2,0},{4,6},{6,4},{8,10},{10,8},{12,14},{14,12},{16,18},{18,... | collective-permute-start | bytes 3145736 | tf_op jit(solution)/shard_map/ppermute | solution.py:34
  177.0 25.3 %collective-permute-start.12 = (bf16[512,1024]{1,0:T(8,128)(2,1)S(1)}, bf16[512,1024]{1,0:T(8,128)(2,1)S(1)}, u32[]{:S(2)}, u32[]{:S(2)}) collective-permute-start(bf16[512,1024]{1,0:T(8,128)(2,1)S(1)} %add_convert_fusion.5), channel_id=1, source_target_pairs={{0,2},{2,0},{4,6},{6,4},{8,10},{10,8},{12,14},{14,12},{16,18},{18,... | collective-permute-start | bytes 3145736 | tf_op jit(solution)/shard_map/ppermute | solution.py:34
  203.4 32.0 %collective-permute-start.14 = (bf16[512,1024]{1,0:T(8,128)(2,1)S(1)}, bf16[512,1024]{1,0:T(8,128)(2,1)}, u32[]{:S(2)}, u32[]{:S(2)}) collective-permute-start(bf16[512,1024]{1,0:T(8,128)(2,1)S(1)} %slice_dynamic-update-slice_fusion.22.e0.l0), channel_id=1, source_target_pairs={{0,2},{2,0},{4,6},{6,4},{8,10},{10,8},{12,14},{14,12},{16,18},{18,... | collective-permute-start | bytes 3145736 | tf_op jit(solution)/shard_map/ppermute | solution.py:34
  244.1 28.9 %collective-permute-start.21 = (bf16[512,1024]{1,0:T(8,128)(2,1)}, bf16[512,1024]{1,0:T(8,128)(2,1)}, u32[]{:S(2)}, u32[]{:S(2)}) collective-permute-start(bf16[512,1024]{1,0:T(8,128)(2,1)} %collective-permute-done.14.e0.l2), channel_id=1, source_target_pairs={{0,1},{1,0},{2,3},{3,2},{4,5},{5,4},{6,7},{7,6},{8,9},{9,8},{10,11... | collective-permute-start | bytes 3145736 | tf_op jit(solution)/shard_map/ppermute | solution.py:29
  244.5 28.3 %collective-permute-start.18 = (bf16[512,1024]{1,0:T(8,128)(2,1)}, bf16[512,1024]{1,0:T(8,128)(2,1)}, u32[]{:S(2)}, u32[]{:S(2)}) collective-permute-start(bf16[512,1024]{1,0:T(8,128)(2,1)} %multiply_convert_fusion.3.h0.l0), channel_id=1, source_target_pairs={{0,2},{2,0},{4,6},{6,4},{8,10},{10,8},{12,14},{14,12},{16,18},{18,... | collective-permute-start | bytes 3145736 | tf_op jit(solution)/shard_map/ppermute | solution.py:34
  303.3 33.5 %collective-permute-start.19 = (bf16[512,1024]{1,0:T(8,128)(2,1)}, bf16[512,1024]{1,0:T(8,128)(2,1)S(1)}, u32[]{:S(2)}, u32[]{:S(2)}) collective-permute-start(bf16[512,1024]{1,0:T(8,128)(2,1)} %get-tuple-element.131), channel_id=1, source_target_pairs={{0,1},{1,0},{2,3},{3,2},{4,5},{5,4},{6,7},{7,6},{8,9},{9,8},{10,11... | collective-permute-start | bytes 3145736 | tf_op jit(solution)/shard_map/ppermute | solution.py:29
  309.1 27.8 %collective-permute-start.23 = (bf16[512,1024]{1,0:T(8,128)(2,1)}, bf16[512,1024]{1,0:T(8,128)(2,1)}, u32[]{:S(2)}, u32[]{:S(2)}) collective-permute-start(bf16[512,1024]{1,0:T(8,128)(2,1)} %add_convert_fusion.4), channel_id=1, source_target_pairs={{0,2},{2,0},{4,6},{6,4},{8,10},{10,8},{12,14},{14,12},{16,18},{18,... | collective-permute-start | bytes 3145736 | tf_op jit(solution)/shard_map/ppermute | solution.py:34
  340.7 146.2 %reduce-scatter.7.cloned.1.call-start = ((), (), s32[]{:S(2)}) async-start(), calls=%async_computation.9 | async-start | bytes 3538944 | tf_op jit(solution)/shard_map/reduce_scatter | solution.py:65
  352.3 25.5 %collective-permute-start.27 = (bf16[512,1024]{1,0:T(8,128)(2,1)}, bf16[512,1024]{1,0:T(8,128)(2,1)}, u32[]{:S(2)}, u32[]{:S(2)}) collective-permute-start(bf16[512,1024]{1,0:T(8,128)(2,1)} %add_convert_fusion.3), channel_id=1, source_target_pairs={{0,2},{2,0},{4,6},{6,4},{8,10},{10,8},{12,14},{14,12},{16,18},{18,... | collective-permute-start | bytes 3145736 | tf_op jit(solution)/shard_map/ppermute | solution.py:34
  391.7 27.6 %collective-permute-start.30 = (bf16[512,1024]{1,0:T(8,128)(2,1)}, bf16[512,1024]{1,0:T(8,128)(2,1)S(1)}, u32[]{:S(2)}, u32[]{:S(2)}) collective-permute-start(bf16[512,1024]{1,0:T(8,128)(2,1)} %get-tuple-element.279.e0.l0), channel_id=1, source_target_pairs={{0,2},{2,0},{4,6},{6,4},{8,10},{10,8},{12,14},{14,12},{16,18},{18,... | collective-permute-start | bytes 3145736 | tf_op jit(solution)/shard_map/ppermute | solution.py:34
  419.3 95.7 %reduce-scatter.9.cloned.1.call-start = ((), (), s32[]{:S(2)}) async-start(), calls=%async_computation.10 | async-start | bytes 5308416 | tf_op jit(solution)/shard_map/reduce_scatter | solution.py:65
  444.1 16.8 %collective-permute-start.34 = (bf16[256,1024]{1,0:T(8,128)(2,1)S(1)}, bf16[256,1024]{1,0:T(8,128)(2,1)S(1)}, u32[]{:S(2)}, u32[]{:S(2)}) collective-permute-start(bf16[256,1024]{1,0:T(8,128)(2,1)S(1)} %get-tuple-element.311), channel_id=1, source_target_pairs={{0,2},{2,0},{4,6},{6,4},{8,10},{10,8},{12,14},{14,12},{16,18},{18,... | collective-permute-start | bytes 1572872 | tf_op jit(solution)/shard_map/ppermute | solution.py:34
  460.8 128.0 %reduce-scatter.11.cloned.1.call-start = ((), (), s32[]{:S(2)}) async-start(), calls=%async_computation.11 | async-start | bytes 7372800 | tf_op jit(solution)/shard_map/reduce_scatter | solution.py:65
  462.0 14.3 %collective-permute-start.31 = (bf16[512,1024]{1,0:T(8,128)(2,1)S(1)}, bf16[512,1024]{1,0:T(8,128)(2,1)S(1)}, u32[]{:S(2)}, u32[]{:S(2)}) collective-permute-start(bf16[512,1024]{1,0:T(8,128)(2,1)S(1)} %copy-done.95), channel_id=1, source_target_pairs={{0,1},{1,0},{2,3},{3,2},{4,5},{5,4},{6,7},{7,6},{8,9},{9,8},{10,11... | collective-permute-start | bytes 3145736 | tf_op jit(solution)/shard_map/ppermute | solution.py:29
  462.0 14.3 %collective-permute-start.35 = (bf16[256,1024]{1,0:T(8,128)(2,1)S(1)}, bf16[256,1024]{1,0:T(8,128)(2,1)S(1)}, u32[]{:S(2)}, u32[]{:S(2)}) collective-permute-start(bf16[256,1024]{1,0:T(8,128)(2,1)S(1)} %get-tuple-element.312), channel_id=1, source_target_pairs={{0,2},{2,0},{4,6},{6,4},{8,10},{10,8},{12,14},{14,12},{16,18},{18,... | collective-permute-start | bytes 1572872 | tf_op jit(solution)/shard_map/ppermute | solution.py:34
  517.3 27.4 %collective-permute-start.46 = (bf16[64,3456]{1,0:T(8,128)(2,1)}, bf16[64,3456]{1,0:T(8,128)(2,1)}, u32[]{:S(2)}, u32[]{:S(2)}) collective-permute-start(bf16[64,3456]{1,0:T(8,128)(2,1)} %get-tuple-element.314), channel_id=1, source_target_pairs={{0,2},{2,0},{4,6},{6,4},{8,10},{10,8},{12,14},{14,12},{16,18},{18,... | collective-permute-start | bytes 1327112 | tf_op jit(solution)/shard_map/ppermute | solution.py:34
  519.8 14.9 %collective-permute-start.45 = (bf16[64,1536]{1,0:T(8,128)(2,1)S(1)}, bf16[64,1536]{1,0:T(8,128)(2,1)S(1)}, u32[]{:S(2)}, u32[]{:S(2)}) collective-permute-start(bf16[64,1536]{1,0:T(8,128)(2,1)S(1)} %broadcast_select_fusion.19), channel_id=1, source_target_pairs={{0,2},{2,0},{4,6},{6,4},{8,10},{10,8},{12,14},{14,12},{16,18},{18,... | collective-permute-start | bytes 589832 | tf_op jit(solution)/shard_map/ppermute | solution.py:34
  522.5 18.0 %collective-permute-start.44 = (bf16[64,2304]{1,0:T(8,128)(2,1)}, bf16[64,2304]{1,0:T(8,128)(2,1)}, u32[]{:S(2)}, u32[]{:S(2)}) collective-permute-start(bf16[64,2304]{1,0:T(8,128)(2,1)} %get-tuple-element.322), channel_id=1, source_target_pairs={{0,2},{2,0},{4,6},{6,4},{8,10},{10,8},{12,14},{14,12},{16,18},{18,... | collective-permute-start | bytes 884744 | tf_op jit(solution)/shard_map/ppermute | solution.py:34
  528.8 20.2 %collective-permute-start.37 = (bf16[512,1024]{1,0:T(8,128)(2,1)}, bf16[512,1024]{1,0:T(8,128)(2,1)}, u32[]{:S(2)}, u32[]{:S(2)}) collective-permute-start(bf16[512,1024]{1,0:T(8,128)(2,1)} %add_convert_fusion), channel_id=1, source_target_pairs={{0,1},{1,0},{2,3},{3,2},{4,5},{5,4},{6,7},{7,6},{8,9},{9,8},{10,11... | collective-permute-start | bytes 3145736 | tf_op jit(solution)/shard_map/ppermute | solution.py:29
  563.9 28.5 %collective-permute-start.41 = (f32[8,1024]{1,0:T(8,128)S(1)}, f32[8,1024]{1,0:T(8,128)S(1)}, u32[]{:S(2)}, u32[]{:S(2)}) collective-permute-start(f32[8,1024]{1,0:T(8,128)S(1)} %add.273), channel_id=1, source_target_pairs={{0,8},{2,10},{4,12},{6,14},{8,0},{10,2},{12,4},{14,6},{16,24},{18,... | collective-permute-start | bytes 98312 | tf_op jit(solution)/shard_map/ppermute | solution.py:743
  590.1 11.3 %collective-permute-start.43 = (bf16[64,3200]{1,0:T(8,128)(2,1)S(1)}, bf16[64,3200]{1,0:T(8,128)(2,1)S(1)}, u32[]{:S(2)}, u32[]{:S(2)}) collective-permute-start(bf16[64,3200]{1,0:T(8,128)(2,1)S(1)} %get-tuple-element.320), channel_id=1, source_target_pairs={{0,2},{2,0},{4,6},{6,4},{8,10},{10,8},{12,14},{14,12},{16,18},{18,... | collective-permute-start | bytes 1228808 | tf_op jit(solution)/shard_map/ppermute | solution.py:34
  (121 other events, 809.0 us)
Sparse Core Ops, SparseCore 0:
  11.6 36.5 all-gather.4
  50.2 73.9 all-gather.6
  126.3 38.3 all-gather.8
  166.1 74.6 all-gather.10
  340.8 76.5 reduce-scatter.4
  419.6 38.7 reduce-scatter.6
  461.0 54.0 reduce-scatter.8
  517.3 71.4 reduce-scatter.10
